TPU v7x, 32 devices: a whole 2x2x4 slice. The times are simulated.
32 devices in a mesh: dp: 8 (over y, x, core), seq: 4 (over z).
Axes of the slice: x: 2, y: 2, z: 4, core: 2. Of those that a mesh axis runs over, the one named last changes fastest.
Arguments:
- tokens: bfloat16 [8, 1024, 768], P('dp', 'seq'), may hold values from -6 to 6
- codon_positions: int32 [8, 1024], P('dp', 'seq'), may hold values from 0 to 4093, as said below
- start_flags: int32 [8], P('dp'), may hold values 0 or 1
- start_embed: float32 [768], replicated, may hold values from -3 to 3
- norm_gain: float32 [2, 768], replicated, may hold values from 0.25 to 1.75
- norm_shift: float32 [2, 768], replicated, may hold values from -2 to 2
- w_qkv: bfloat16 [768, 2304], replicated, may hold values from -0.21875 to 0.21875
- b_qkv: float32 [2304], replicated, may hold values from -3 to 3
- w_out: bfloat16 [768, 768], replicated, may hold values from -0.875 to 0.875
- b_out: float32 [768], replicated, may hold values from -3 to 3
- w_up: bfloat16 [768, 3072], replicated, may hold values from -0.21875 to 0.21875
- b_up: float32 [3072], replicated, may hold values from -3 to 3
- w_down: bfloat16 [3072, 768], replicated, may hold values from -0.21875 to 0.21875
- b_down: float32 [768], replicated, may hold values from -3 to 3
- cotangent: bfloat16 [8, 1024, 768], P('dp', 'seq'), may hold values from -6 to 6
Outputs:
- layer_out: bfloat16 [8, 1024, 768], P('dp', 'seq')
- grad_tokens: bfloat16 [8, 1024, 768], P('dp', 'seq')
- grad_start: float32 [768], replicated
- grad_gain: float32 [2, 768], replicated
- grad_shift: float32 [2, 768], replicated
- grad_w_qkv: float32 [768, 2304], replicated
- grad_b_qkv: float32 [2304], replicated
- grad_w_out: float32 [768, 768], replicated
- grad_b_out: float32 [768], replicated
- grad_w_up: float32 [768, 3072], replicated
- grad_b_up: float32 [3072], replicated
- grad_w_down: float32 [3072, 768], replicated
- grad_b_down: float32 [768], replicated
Inputs may be any that keep to these rules, and one draw needn't show every extreme that they name: `codon_positions`: within a gene the position rises by 1 or 2 from one codon to the next; some gene starts at 0, and some gene ends at the largest position.
All inputs are finite; a program needn't handle non-finite values. No bound on the sum of `start_flags` on one device may be relied on, other than what follows from the above.
Results may differ from a plain program's by a relative error of at most 0.013.
Values may be sent and summed in bfloat16 or wider, within the bound.
No kernel may reach another device: no remote copies, remote signals or barrier semaphores. Data moves between devices by JAX's collectives and lax.ppermute only.
A program may use at most 192 MiB of HBM per device.

v0:
```python
from functools import partial

import jax
import jax.numpy as jnp
from jax import lax
from jax.sharding import PartitionSpec as P

HEADS = 12
HEAD_DIM = 64


epsilon = 1e-05


def norm_forward(values, gain_row, shift_row):
    centered = values - jnp.mean(values, axis=-1, keepdims=True)
    inverse = lax.rsqrt(jnp.mean(centered * centered, axis=-1, keepdims=True) + epsilon)
    unit_rows = centered * inverse
    return (unit_rows * gain_row + shift_row, unit_rows, inverse)


def norm_backward(grad_rows, unit_rows, inverse, gain_row):
    scaled = grad_rows * gain_row
    row_inner = (
        scaled
        - jnp.mean(scaled, axis=-1, keepdims=True)
        - unit_rows * jnp.mean(scaled * unit_rows, axis=-1, keepdims=True)
    )
    return (
        row_inner * inverse,
        jnp.sum(grad_rows * unit_rows, axis=(0, 1)),
        jnp.sum(grad_rows, axis=(0, 1)),
    )


def rotate(values, cos_table, sin_table):
    middle_index = values.shape[-1] // 2
    former = values[..., :middle_index]
    latter = values[..., middle_index:]
    return jnp.concatenate(
        [former * cos_table - latter * sin_table, latter * cos_table + former * sin_table], axis=-1
    )


def rotary_tables(positions):
    half_dim = HEAD_DIM // 2
    frequency = 10000.0 ** (-2.0 * jnp.arange(half_dim, dtype=jnp.float32) / HEAD_DIM)
    angles = positions.astype(jnp.float32)[:, :, None, None] * frequency
    return (jnp.cos(angles), jnp.sin(angles))


def project_heads(normed_low, w_qkv, b_qkv, cos_table, sin_table, groups):
    seq_count, span_rows, model_width = normed_low.shape
    mixed_proj = (
        jnp.einsum("scd,de->sce", normed_low, w_qkv, preferred_element_type=jnp.float32) + b_qkv
    )
    mixed_proj = mixed_proj.reshape(seq_count, span_rows, HEADS, 3, HEAD_DIM)
    queries = rotate(mixed_proj[:, :, :, 0], cos_table, sin_table)
    keyset = rotate(mixed_proj[:, :, :, 1], cos_table, sin_table)
    stacked = jnp.stack([queries, keyset, mixed_proj[:, :, :, 2]], axis=3).astype(jnp.bfloat16)
    return stacked.reshape(seq_count, span_rows, groups, -1)


def attend_heads(items):
    item_count = items.shape[0]
    length = items.shape[1]
    local_heads = items.shape[3] // (3 * HEAD_DIM)
    factor = HEAD_DIM ** (-0.5)
    unpacked = items.reshape(item_count, length, local_heads, 3, HEAD_DIM)
    keyset = unpacked[:, :, :, 1]
    valueset = unpacked[:, :, :, 2]
    block_rows = min(512, length)
    blocked = jnp.moveaxis(
        unpacked[:, :, :, 0].reshape(
            item_count, length // block_rows, block_rows, local_heads, HEAD_DIM
        ),
        1,
        0,
    )

    def one_block(query_block):
        scores = (
            jnp.einsum("nqhe,nkhe->nhqk", query_block, keyset, preferred_element_type=jnp.float32)
            * factor
        )
        highest_score = jnp.max(scores, axis=-1, keepdims=True)
        shifted = jnp.exp(scores - highest_score)
        totals = jnp.sum(shifted, axis=-1, keepdims=True)
        weights = (shifted / totals).astype(jnp.bfloat16)
        attended = jnp.einsum(
            "nhqk,nkhe->nqhe", weights, valueset, preferred_element_type=jnp.float32
        )
        return (attended.astype(jnp.bfloat16), (highest_score + jnp.log(totals))[..., 0])

    attended, logsum = lax.map(one_block, blocked)
    attended = jnp.moveaxis(attended, 0, 1).reshape(item_count, length, 1, local_heads * HEAD_DIM)
    return (attended, jnp.moveaxis(logsum, 0, 1), items)


def attend_backward(heads_qkv, grad_heads, logsum):
    item_count = heads_qkv.shape[0]
    length = heads_qkv.shape[1]
    local_heads = heads_qkv.shape[3] // (3 * HEAD_DIM)
    factor = HEAD_DIM ** (-0.5)
    unpacked = heads_qkv.reshape(item_count, length, local_heads, 3, HEAD_DIM)
    keyset = unpacked[:, :, :, 1]
    valueset = unpacked[:, :, :, 2]
    block_rows = min(512, length)

    def blocks_of(array):
        return jnp.moveaxis(
            array.reshape(item_count, length // block_rows, block_rows, local_heads, HEAD_DIM), 1, 0
        )

    def one_block(running, pieces):
        grad_keys, grad_values = running
        query_block, grad_block, logsum_block = pieces
        scores = (
            jnp.einsum("nqhe,nkhe->nhqk", query_block, keyset, preferred_element_type=jnp.float32)
            * factor
        )
        weights = jnp.exp(scores - logsum_block[..., None])
        grad_values = grad_values + jnp.einsum(
            "nhqk,nqhe->nkhe",
            weights.astype(jnp.bfloat16),
            grad_block,
            preferred_element_type=jnp.float32,
        )
        grad_weights = jnp.einsum(
            "nqhe,nkhe->nhqk", grad_block, valueset, preferred_element_type=jnp.float32
        )
        row_inner = jnp.sum(weights * grad_weights, axis=-1, keepdims=True)
        grad_scores = (weights * (grad_weights - row_inner)).astype(jnp.bfloat16)
        grad_query = (
            jnp.einsum("nhqk,nkhe->nqhe", grad_scores, keyset, preferred_element_type=jnp.float32)
            * factor
        )
        grad_keys = (
            grad_keys
            + jnp.einsum(
                "nhqk,nqhe->nkhe", grad_scores, query_block, preferred_element_type=jnp.float32
            )
            * factor
        )
        return ((grad_keys, grad_values), grad_query)

    zero_grad = jnp.zeros((item_count, length, local_heads, HEAD_DIM), jnp.float32)
    grad_attended = grad_heads.reshape(item_count, length, local_heads, HEAD_DIM)
    (grad_keys, grad_values), grad_queries = lax.scan(
        one_block,
        (zero_grad, zero_grad),
        (blocks_of(unpacked[:, :, :, 0]), blocks_of(grad_attended), jnp.moveaxis(logsum, 1, 0)),
    )
    grad_queries = jnp.moveaxis(grad_queries, 0, 1).reshape(
        item_count, length, local_heads, HEAD_DIM
    )
    stacked = jnp.stack([grad_queries, grad_keys, grad_values], axis=3).astype(jnp.bfloat16)
    return stacked.reshape(item_count, length, 1, -1)


def per_device(
    tokens,
    codon_positions,
    start_flags,
    start_embed,
    norm_gain,
    norm_shift,
    w_qkv,
    b_qkv,
    w_out,
    b_out,
    w_up,
    b_up,
    w_down,
    b_down,
    cotangent,
):
    seq_count, span_rows, model_width = tokens.shape
    groups = lax.axis_size("seq")
    cos_table, sin_table = rotary_tables(codon_positions)
    flag_values = start_flags.astype(jnp.float32)[:, None, None]
    residual = tokens.astype(jnp.float32) + flag_values * start_embed
    first_out, first_unit, first_inverse = norm_forward(residual, norm_gain[0], norm_shift[0])
    first_low = first_out.astype(jnp.bfloat16)
    packed = project_heads(first_low, w_qkv, b_qkv, cos_table, sin_table, groups)
    attended_heads, logsum, heads_qkv = attend_heads(
        lax.all_to_all(packed, "seq", split_axis=2, concat_axis=1, tiled=True)
    )
    attended = lax.all_to_all(
        attended_heads, "seq", split_axis=1, concat_axis=2, tiled=True
    ).reshape(seq_count, span_rows, model_width)
    middle = (
        residual
        + jnp.einsum("scd,de->sce", attended, w_out, preferred_element_type=jnp.float32)
        + b_out
    )
    second_out, second_unit, second_inverse = norm_forward(middle, norm_gain[1], norm_shift[1])
    second_low = second_out.astype(jnp.bfloat16)
    hidden = jnp.einsum("scd,df->scf", second_low, w_up, preferred_element_type=jnp.float32) + b_up
    gelu_value, gelu_pullback = jax.vjp(partial(jax.nn.gelu, approximate=False), hidden)
    active = gelu_value.astype(jnp.bfloat16)
    layer_out = (
        middle
        + jnp.einsum("scf,fd->scd", active, w_down, preferred_element_type=jnp.float32)
        + b_down
    ).astype(jnp.bfloat16)
    grad_down = jnp.einsum("scf,scd->fd", active, cotangent, preferred_element_type=jnp.float32)
    grad_bdown = jnp.sum(cotangent.astype(jnp.float32), axis=(0, 1))
    grad_active = jnp.einsum("scd,fd->scf", cotangent, w_down, preferred_element_type=jnp.float32)
    grad_hidden = gelu_pullback(grad_active)[0].astype(jnp.bfloat16)
    grad_up = jnp.einsum("scd,scf->df", second_low, grad_hidden, preferred_element_type=jnp.float32)
    grad_bup = jnp.sum(grad_hidden.astype(jnp.float32), axis=(0, 1))
    grad_second = jnp.einsum("scf,df->scd", grad_hidden, w_up, preferred_element_type=jnp.float32)
    grad_from_second, gain_second, shift_second = norm_backward(
        grad_second, second_unit, second_inverse, norm_gain[1]
    )
    grad_middle = cotangent.astype(jnp.float32) + grad_from_second
    grad_branch = grad_middle.astype(jnp.bfloat16)
    grad_wout = jnp.einsum("scd,sce->de", attended, grad_branch, preferred_element_type=jnp.float32)
    grad_bout = jnp.sum(grad_branch.astype(jnp.float32), axis=(0, 1))
    grad_attended = jnp.einsum(
        "sce,de->scd", grad_branch, w_out, preferred_element_type=jnp.float32
    ).astype(jnp.bfloat16)
    grad_heads = lax.all_to_all(
        grad_attended.reshape(seq_count, span_rows, groups, -1),
        "seq",
        split_axis=2,
        concat_axis=1,
        tiled=True,
    )
    grad_packed = attend_backward(heads_qkv, grad_heads, logsum)
    grad_split = (
        lax.all_to_all(grad_packed, "seq", split_axis=1, concat_axis=2, tiled=True)
        .reshape(seq_count, span_rows, HEADS, 3, HEAD_DIM)
        .astype(jnp.float32)
    )
    grad_query = rotate(grad_split[:, :, :, 0], cos_table, -sin_table)
    grad_keys = rotate(grad_split[:, :, :, 1], cos_table, -sin_table)
    grad_mixed = (
        jnp.stack([grad_query, grad_keys, grad_split[:, :, :, 2]], axis=3)
        .reshape(seq_count, span_rows, 3 * model_width)
        .astype(jnp.bfloat16)
    )
    grad_qkv = jnp.einsum("scd,sce->de", first_low, grad_mixed, preferred_element_type=jnp.float32)
    grad_bqkv = jnp.sum(grad_mixed.astype(jnp.float32), axis=(0, 1))
    grad_first = jnp.einsum("sce,de->scd", grad_mixed, w_qkv, preferred_element_type=jnp.float32)
    grad_from_first, gain_first, shift_first = norm_backward(
        grad_first, first_unit, first_inverse, norm_gain[0]
    )
    grad_residual = grad_middle + grad_from_first
    grad_start = jnp.sum(grad_residual * flag_values, axis=(0, 1))
    grad_gain = jnp.stack([gain_first, gain_second])
    grad_shift = jnp.stack([shift_first, shift_second])
    (
        grad_start,
        grad_gain,
        grad_shift,
        grad_qkv,
        grad_bqkv,
        grad_wout,
        grad_bout,
        grad_up,
        grad_bup,
        grad_down,
        grad_bdown,
    ) = lax.psum(
        (
            grad_start,
            grad_gain,
            grad_shift,
            grad_qkv,
            grad_bqkv,
            grad_wout,
            grad_bout,
            grad_up,
            grad_bup,
            grad_down,
            grad_bdown,
        ),
        ("dp", "seq"),
    )
    return (
        layer_out,
        grad_residual.astype(jnp.bfloat16),
        grad_start,
        grad_gain,
        grad_shift,
        grad_qkv,
        grad_bqkv,
        grad_wout,
        grad_bout,
        grad_up,
        grad_bup,
        grad_down,
        grad_bdown,
    )


def solution(mesh):
    placed = (
        P("dp", "seq", None),
        P("dp", "seq"),
        P("dp"),
        P(),
        P(),
        P(),
        P(),
        P(),
        P(),
        P(),
        P(),
        P(),
        P(),
        P(),
        P("dp", "seq", None),
    )
    return jax.shard_map(
        per_device,
        mesh=mesh,
        in_specs=placed,
        out_specs=(
            P("dp", "seq", None),
            P("dp", "seq", None),
            P(),
            P(),
            P(),
            P(),
            P(),
            P(),
            P(),
            P(),
            P(),
            P(),
            P(),
        ),
        check_vma=False,
    )
```

profile of v0, /device:TPU:0, one launch (start us, length us, event | category | flops | bytes accessed | tf_op | source)
XLA Modules:
  0.0 741.5 jit_solution(8277213866488118646)
XLA Ops:
  12.7 3.6 convolution_add_fusion
  16.3 3.0 copy.96
  20.5 1.5 slice_bitcast_fusion.4
  24.7 6.6 all-to-all-start
  31.3 28.6 %all-to-all-done = bf16[1,256,4,576]{1,3,0,2:T(8,128)(2,1)} async-done(((bf16[1,256,4,576]{1,3,0,2:T(8,128)(2,1)}), bf16[1,256,4,576]{1,3,0,2:T(8,128)(2,1)}, u32[]{:S(2)}, u32[]{:S(2)}) %all-to-all-start) | async-done | bytes 1179680 | tf_op jit(solution)/shard_map/all_to_all | solution.py:187
  59.9 3.2 copy.100
  63.1 3.4 reshape.638
  66.5 2.3 slice_bitcast_fusion.5
  68.8 2.0 transpose_reshape_squeeze.4
  70.8 1.8 copy.101
  72.6 13.5 %while.27 = (s32[]{:T(128)}, bf16[2,1,512,3,64]{2,4,3,1,0:T(8,128)(2,1)}, f32[2,1,3,512]{3,2,1,0:T(4,128)}, bf16[2,1,512,3,64]{2,4,3,1,0:T(8,128)(2,1)}, bf16[1,...) while((s32[]{:T(128)}, bf16[2,1,512,3,64]{2,4,3,1,0:T(8,128)(2,1)}, ...), condition=%wide.region_5.6_spmd, body=%wide.region_2.5_spmd.sunk | while | flops 416905728 | bytes 24930540 | solution.py:95
  72.6 2.2 multiply_reduce_fusion.9
  76.2 1.8 fusion.126
  79.4 2.2 multiply_reduce_fusion.9
  82.9 1.8 fusion.126
  86.1 2.1 copy.102
  88.3 2.0 reshape_transpose.3
  90.3 3.5 copy.103
  94.4 5.7 reduce.29
  100.1 2.4 reshape.654
  102.5 15.9 %all_to_all.54 = bf16[4,2,24576]{2,1,0:T(2,128)(2,1)} all-to-all(bf16[4,2,24576]{2,1,0:T(2,128)(2,1)} %reshape.654), channel_id=1, replica_groups=mesh['dp'=8,'seq'=4] {'seq'}, dimensions={0} | all-to-all | bytes 786432 | tf_op jit(solution)/shard_map/all_to_all | solution.py:189
  118.4 3.6 reshape.655
  122.0 3.4 copy.104
  125.4 2.0 all_to_all.44
  128.5 2.1 fusion.90
  131.0 11.6 %multiply_convert_fusion.1 = (bf16[256,3072]{1,0:T(8,128)(2,1)}, f32[256,3072]{1,0:T(8,128)S(1)}, f32[256,3072]{1,0:T(8,128)S(1)}) fusion(f32[3072]{0:T(1024)S(1)} %copy-done.48, bf16[768,3072]{1,0:T(8,128)(2,1)} %param.29, f32[1,256,768]{2,1,0:T(8,128)S(1)} %get-tuple-element.279, f32[768]{0:T(1024)S(1)} %get-tuple-element.200, ...), kind=kOutput, calls=%fused_computation.56 | convolution fusion | flops 1260847104 | bytes 13389824 | tf_op jit(solution)/shard_map/scd,df->scf/dot_general | solution.py:199
  142.5 2.8 convert_reduce_fusion
  145.3 2.2 fusion.56
  151.4 1.9 copy.106
  153.3 4.3 all-to-all-start.2
  157.6 10.4 %all-to-all-done.2 = bf16[1,256,4,192]{1,3,0,2:T(8,128)(2,1)} async-done(((bf16[1,256,4,192]{1,3,0,2:T(8,128)(2,1)}), bf16[1,256,4,192]{1,3,0,2:T(8,128)(2,1)}, u32[]{:S(2)}, u32[]{:S(2)}) %all-to-all-start.2) | async-done | bytes 393248 | tf_op jit(solution)/shard_map/all_to_all | solution.py:224
  168.0 2.0 copy.108
  170.0 2.0 transpose_reshape_reshape.3
  172.0 1.8 copy.110
  173.8 22.1 %while.28 = (s32[]{:T(128)}, f32[1,1024,3,64]{1,3,2,0:T(8,128)}, f32[1,1024,3,64]{1,3,2,0:T(8,128)}, bf16[2,1,512,3,64]{2,4,3,1,0:T(8,128)(2,1)}, bf16[2,1,512,3...) while((s32[]{:T(128)}, f32[1,1024,3,64]{1,3,2,0:T(8,128)}, ...), condition=%wide.region_12.13_spmd.clone, body=%wide.region_10.12_spmd.clone.sunk | while | flops 1026587136 | bytes 74758568 | solution.py:149
  174.5 2.2 fusion.135
  178.2 2.1 multiply_reduce_fusion.10
  180.4 1.6 multiply_convert_fusion.3
  185.6 2.2 fusion.135
  189.3 2.1 multiply_reduce_fusion.10
  191.5 1.6 multiply_convert_fusion.3
  195.9 2.1 copy.111
  198.1 2.0 stack.50
  204.7 6.4 copy.113
  211.1 11.0 %reduce.30 = bf16[1024,576]{1,0:T(8,128)(2,1)} reduce(bf16[1024,1,1,576]{3,2,1,0:T(2,128)(2,1)} %bitcast.272, bf16[]{:T(256)} %broadcast.309), dimensions={1,2}, to_apply=%bitcast.202.reduce_sub_computation | reduce | bytes 2359298
  222.1 4.1 reshape.656
  226.3 4.3 all-to-all-start.3
  230.6 3.3 fusion.68
  233.9 5.2 fusion.71
  239.1 5.3 fusion.83
  244.5 12.2 %all-to-all-done.3 = bf16[4,2,73728]{2,1,0:T(2,128)(2,1)} async-done(((bf16[4,2,73728]{2,1,0:T(2,128)(2,1)}), bf16[4,2,73728]{2,1,0:T(2,128)(2,1)}, u32[]{:S(2)}, u32[]{:S(2)}) %all-to-all-start.3) | async-done | bytes 1179680 | tf_op jit(solution)/shard_map/all_to_all | solution.py:233
  256.6 4.9 reshape.657
  261.5 6.0 copy.114
  267.5 3.5 reshape.645
  271.1 2.1 copy.115
  276.5 4.3 fusion.80
  283.4 6.0 fusion.55
  291.4 2.8 fusion.57
  295.6 1.7 multiply_reduce_fusion.2
  297.3 41.3 %all-reduce = (f32[768]{0:T(1024)}, f32[2,768]{1,0:T(2,128)}, f32[2,768]{1,0:T(2,128)}, f32[2304]{0:T(1024)}, f32[768]{0:T(1024)}, /*index=5*/f32[3072]{0:T(1024)}, f32[768]{0:T(1024)}) all-reduce(f32[768]{0:T(1024)} %get-tuple-element.247, f32[2,768]{1,0:T(2,128)} %pad_maximum_fusion.2, ...), channel_id=1, replica_groups=mesh['dp'=8,'seq'=4] {'dp','seq'}, use_global_device_ids=true, to_apply=%region_16.17 | all-reduce | flops 10752 | bytes 86016 | tf_op jit(solution)/shard_map/psum | solution.py:266
  338.6 374.8 %all-reduce.4.cloned.1.call-done = (f32[768,2304]{1,0:T(8,128)}, f32[768,768]{1,0:T(8,128)}, f32[768,3072]{1,0:T(8,128)}, f32[3072,768]{1,0:T(8,128)}) async-done(((f32[768,2304]{1,0:T(8,128)}, f32[768,768]{1,0:T(8,128)}, f32[768,3072]{1,0:T(8,128)}, f32[3072,768]{1,0:T(8,128)}), (f32[768,2304]{1,0:T(8,128)}, f32[768,768]{1,0:T(8,128)}, f32[768,3072]{1,0:T(8,128)}, ...) | async-done | bytes 28311568 | tf_op jit(solution)/shard_map/psum | solution.py:266
  713.3 6.6 copy.155
  721.3 9.3 %copy.157 = f32[768,3072]{1,0:T(8,128)} copy(f32[768,3072]{1,0:T(8,128)} %get-tuple-element.452) | data formatting | bytes 18874368
  730.7 3.7 copy.158
  (213 shorter events, 44.8 us)
Async XLA Ops:
  7.2 5.5 copy-start
  10.0 2.1 copy-start.39
  19.3 2.7 copy-start.47
  24.7 35.2 %all-to-all-start = ((bf16[1,256,4,576]{1,3,0,2:T(8,128)(2,1)}), bf16[1,256,4,576]{1,3,0,2:T(8,128)(2,1)}, u32[]{:S(2)}, u32[]{:S(2)}) async-start(bf16[1,256,4,576]{1,3,0,2:T(8,128)(2,1)} %bitcast.283), calls=%async_computation | async-start | bytes 2359296 | tf_op jit(solution)/shard_map/all_to_all | solution.py:187
  74.8 1.3 copy-start.7
  74.8 1.3 copy-start.25
  76.2 1.8 copy-start.36
  81.6 1.3 copy-start.7
  81.6 1.3 copy-start.25
  82.9 1.8 copy-start.36
  100.1 28.4 %copy-start.49 = (f32[768]{0:T(1024)S(1)}, f32[768]{0:T(1024)}, u32[]{:S(2)}) copy-start(f32[768]{0:T(1024)} %param.28) | copy-start | bytes 9220
  127.4 3.5 copy-start.48
  128.5 2.4 copy-start.21
  128.5 14.0 %slice-start.5 = ((s8[4718592]{0:T(1024)(128)(4,1)}), s8[4194304]{0:T(1024)(128)(4,1)S(1)}, s32[]{:S(2)}) async-start(s8[4718592]{0:T(1024)(128)(4,1)} %bitcast.294), calls=%async_computation.10 | async-start | bytes 8388608
  128.5 16.8 %slice-start.3 = ((s8[4718592]{0:T(1024)(128)(4,1)}), s8[4194304]{0:T(1024)(128)(4,1)S(1)}, s32[]{:S(2)}) async-start(s8[4718592]{0:T(1024)(128)(4,1)} %bitcast.292), calls=%async_computation.8 | async-start | bytes 8388608
  130.6 17.6 %copy-start.14 = (f32[1,256,768]{2,1,0:T(8,128)}, f32[1,256,768]{2,1,0:T(8,128)S(1)}, u32[]{:S(2)}) copy-start(f32[1,256,768]{2,1,0:T(8,128)S(1)} %get-tuple-element.279) | copy-start | bytes 2359300
  130.9 17.3 %copy-start.43 = (f32[256]{0:T(256)}, f32[256]{0:T(256)S(1)}, u32[]{:S(2)}) copy-start(f32[256]{0:T(256)S(1)} %add_rsqrt_fusion) | copy-start | bytes 3076
  130.9 11.6 %copy-start.19 = (bf16[1,256,768]{2,1,0:T(8,128)(2,1)S(1)}, bf16[1,256,768]{2,1,0:T(8,128)(2,1)}, u32[]{:S(2)}) copy-start(bf16[1,256,768]{2,1,0:T(8,128)(2,1)} %param.33) | copy-start | bytes 1179652
  130.9 11.6 %slice-start.6 = ((s8[4718592]{0:T(1024)(128)(4,1)}), s8[524288]{0:T(1024)(128)(4,1)S(1)}, s32[]{:S(2)}) async-start(s8[4718592]{0:T(1024)(128)(4,1)} %bitcast.294), calls=%async_computation.11 | async-start | bytes 1048576
  130.9 14.4 %slice-start.4 = ((s8[4718592]{0:T(1024)(128)(4,1)}), s8[524288]{0:T(1024)(128)(4,1)S(1)}, s32[]{:S(2)}) async-start(s8[4718592]{0:T(1024)(128)(4,1)} %bitcast.292), calls=%async_computation.9 | async-start | bytes 1048576
  145.3 2.2 copy-start.22
  147.5 2.6 copy-start.24
  149.2 0.9 copy-start.10
  153.3 14.7 %all-to-all-start.2 = ((bf16[1,256,4,192]{1,3,0,2:T(8,128)(2,1)}), bf16[1,256,4,192]{1,3,0,2:T(8,128)(2,1)}, u32[]{:S(2)}, u32[]{:S(2)}) async-start(bf16[1,256,4,192]{1,3,0,2:T(8,128)(2,1)} %bitcast.289), calls=%async_computation.2 | async-start | bytes 786432 | tf_op jit(solution)/shard_map/all_to_all | solution.py:224
  174.5 2.2 copy-start.5
  174.5 2.2 copy-start.9
  176.8 1.4 copy-start.8
  178.2 2.2 copy-start.6
  180.4 1.6 copy-start.1
  180.4 1.6 copy-start.27
  182.0 1.1 copy-start.2
  182.0 1.2 copy-start.4
  184.0 0.9 copy-start.3
  185.6 2.2 copy-start.5
  185.6 2.2 copy-start.9
  187.8 1.4 copy-start.8
  189.3 2.2 copy-start.6
  191.4 1.6 copy-start.1
  191.5 1.6 copy-start.27
  193.1 1.1 copy-start.2
  193.1 1.2 copy-start.4
  195.1 0.9 copy-start.3
  226.3 30.3 %all-to-all-start.3 = ((bf16[4,2,73728]{2,1,0:T(2,128)(2,1)}), bf16[4,2,73728]{2,1,0:T(2,128)(2,1)}, u32[]{:S(2)}, u32[]{:S(2)}) async-start(bf16[4,2,73728]{2,1,0:T(2,128)(2,1)} %reshape.656), calls=%async_computation.3 | async-start | bytes 2359296 | tf_op jit(solution)/shard_map/all_to_all | solution.py:233
  230.6 482.8 %all-reduce.4.cloned.1.call-start = ((), (), s32[]{:S(2)}) async-start(), calls=%async_computation.4 | async-start | bytes 56623104 | tf_op jit(solution)/shard_map/psum | solution.py:266
  230.6 3.3 copy-start.17
  230.6 3.3 copy-start.20
  233.9 5.2 copy-start.15
  233.9 5.2 copy-start.23
  233.9 5.2 copy-start.44
  274.2 2.3 copy-start.12
  274.2 2.3 copy-start.32
  274.2 2.2 copy-start.35
  274.3 2.2 copy-start.40
  274.3 2.2 copy-start.42
  275.5 1.0 copy-start.16
  283.4 6.0 copy-start.38
  291.4 3.0 copy-start.45
  291.4 3.6 copy-start.46
  291.4 4.2 copy-start.11
  291.4 4.2 copy-start.13
  713.3 6.6 copy-start.18
  719.9 10.7 %slice-start = ((s8[9437184]{0:T(1024)(128)(4,1)}), s8[4194304]{0:T(1024)(128)(4,1)S(1)}, s32[]{:S(2)}) async-start(s8[9437184]{0:T(1024)(128)(4,1)} %bitcast.274), calls=%async_computation.5 | async-start | bytes 8388608
  721.3 9.3 %slice-start.1 = ((s8[9437184]{0:T(1024)(128)(4,1)}), s8[4194304]{0:T(1024)(128)(4,1)S(1)}, s32[]{:S(2)}) async-start(s8[9437184]{0:T(1024)(128)(4,1)} %bitcast.274), calls=%async_computation.6 | async-start | bytes 8388608
  721.3 9.3 %slice-start.2 = ((s8[9437184]{0:T(1024)(128)(4,1)}), s8[1048576]{0:T(1024)(128)(4,1)S(1)}, s32[]{:S(2)}) async-start(s8[9437184]{0:T(1024)(128)(4,1)} %bitcast.274), calls=%async_computation.7 | async-start | bytes 2097152
  (12 other events, 8.4 us)
Sparse Core Ops, SparseCore 0:
  280.9 432.3 all-reduce.3
where the time goes:
time: 747 us; the launch traced here: 742 us
  waiting for transfers between devices  426 us (57%)
  local copies, waits for them, and re-layouts  116 us (16%)
  matrix products  73.5 us (10%)
  blocking collectives  57.1 us (8%)
  other arithmetic  37.8 us (5%)
  between operations  15.7 us (2%)
  starting transfers between devices  15.2 us (2%)
    psum x1, waiting for transfers between devices, per_device(): lax.psum((grad_start, grad_gain, grad_shift, grad_qkv, grad_bqkv, grad_wo...  375 us
    unnamed x95, local copies, waits for them, and re-layouts  42.1 us
    psum x1, blocking collectives, per_device(): lax.psum((grad_start, grad_gain, grad_shift, grad_qkv, grad_bqkv, grad_wo...  41.3 us
    all_to_all x1, waiting for transfers between devices, per_device(): lax.all_to_all(packed, 'seq', split_axis=2, concat_axis=1, tiled=True)  28.6 us
    unnamed x7, other arithmetic  16.7 us
    all_to_all x1, blocking collectives, per_device(): lax.all_to_all(attended_heads, 'seq', split_axis=1, concat_axis=2, tiled=...  15.9 us
  transfers between devices with their start and end apart: 4, of which 4 were waited for; matrix products, arithmetic and copies ran while one was open for 4% of the time, Pallas kernels for 0%

commit v1 on v0

v1 whole, which is shorter than its diff:
```python
import math

import jax
import jax.numpy as jnp
from jax import lax
from jax.experimental import pallas as pl
from jax.experimental.pallas import tpu as pltpu
from jax.sharding import PartitionSpec as P

HEADS = 12
HEAD_DIM = 64
EPS = 1e-05
BF = jnp.bfloat16
F32 = jnp.float32
VMEM_LIMIT = 56 * 1024 * 1024
HEADS_PER_STEP = 4


def dot(a, b, dims):
    return lax.dot_general(a, b, (dims, ((), ())), preferred_element_type=F32)


NN = ((1,), (0,))
NT = ((1,), (1,))
TN = ((0,), (0,))


def params(**kw):
    return pltpu.CompilerParams(vmem_limit_bytes=VMEM_LIMIT, **kw)


def unit_norm(values):
    centered = values - jnp.mean(values, axis=-1, keepdims=True)
    inverse = lax.rsqrt(jnp.mean(centered * centered, axis=-1, keepdims=True) + EPS)
    return centered * inverse, inverse


def norm_back(grad, unit, inverse, gain):
    e = grad * gain
    inner = e - jnp.mean(e, axis=-1, keepdims=True) - unit * jnp.mean(e * unit, axis=-1, keepdims=True)
    return inner * inverse


def forward_kernel(
    x_ref, shift_in_ref, gain_ref, shift_ref, w_ref, b_ref, cos_ref, sin_ref,
    q_out, k_out, v_out, p_out, o_out, first_t_out, first_ref,
):
    group = pl.program_id(0)
    rows = q_out.shape[1]

    @pl.when(group == 0)
    def _():
        residual = x_ref[...].astype(F32) + shift_in_ref[...]
        unit, _ = unit_norm(residual)
        first = unit * gain_ref[0:1, :] + shift_ref[0:1, :]
        first_ref[...] = first.astype(BF)
        first_t_out[...] = first.T.astype(BF)

    half = HEAD_DIM // 2
    cos, sin = cos_ref[...], sin_ref[...]
    first = first_ref[...]
    query = dot(w_ref[0], first[:rows], NT) + b_ref[0]
    keys = dot(w_ref[1], first, NT) + b_ref[1]
    values = (dot(w_ref[2], first, NT) + b_ref[2]).astype(BF)
    v_out[...] = values

    def rotated(part, head, width):
        lo = part[head * HEAD_DIM : head * HEAD_DIM + half]
        hi = part[head * HEAD_DIM + half : (head + 1) * HEAD_DIM]
        c, s = cos[:, :width], sin[:, :width]
        return jnp.concatenate([lo * c - hi * s, hi * c + lo * s], axis=0)

    for head in range(HEADS_PER_STEP):
        at = slice(head * HEAD_DIM, (head + 1) * HEAD_DIM)
        q_t = (rotated(query, head, rows) * HEAD_DIM**-0.5).astype(BF)
        k_t = rotated(keys, head, first.shape[0])
        q_out[at, :] = q_t
        k_out[at, :] = k_t.astype(BF)
        scores = dot(k_t.T.astype(BF), q_t, NN)
        top = jnp.max(scores, axis=0, keepdims=True)
        weights = jnp.exp(scores - top)
        total = jnp.sum(weights, axis=0, keepdims=True)
        weights = (weights * (1.0 / total)).astype(BF)
        p_out[head] = weights
        o_out[at, :] = dot(values[at], weights, NN)


def attention_forward(x_all, start_row, gain, shift, w_t, b_cols, cos, sin):
    length, width = x_all.shape
    rows = length // lax.axis_size("seq")
    step = HEADS_PER_STEP * HEAD_DIM
    whole = lambda shape: pl.BlockSpec(shape, lambda g: (0,) * len(shape))
    return pl.pallas_call(
        forward_kernel,
        grid=(HEADS // HEADS_PER_STEP,),
        in_specs=[
            whole((length, width)),
            whole((1, width)),
            whole((2, width)),
            whole((2, width)),
            pl.BlockSpec((3, step, width), lambda g: (0, g, 0)),
            pl.BlockSpec((3, step, 1), lambda g: (0, g, 0)),
            whole(cos.shape),
            whole(sin.shape),
        ],
        out_specs=[
            pl.BlockSpec((step, rows), lambda g: (g, 0)),
            pl.BlockSpec((step, length), lambda g: (g, 0)),
            pl.BlockSpec((step, length), lambda g: (g, 0)),
            pl.BlockSpec((HEADS_PER_STEP, length, rows), lambda g: (g, 0, 0)),
            pl.BlockSpec((step, rows), lambda g: (g, 0)),
            whole((width, length)),
        ],
        out_shape=[
            jax.ShapeDtypeStruct((width, rows), BF),
            jax.ShapeDtypeStruct((width, length), BF),
            jax.ShapeDtypeStruct((width, length), BF),
            jax.ShapeDtypeStruct((HEADS, length, rows), BF),
            jax.ShapeDtypeStruct((width, rows), F32),
            jax.ShapeDtypeStruct((width, length), BF),
        ],
        scratch_shapes=[pltpu.VMEM((length, width), BF)],
        compiler_params=params(),
        name="attention_forward",
        cost_estimate=pl.CostEstimate(flops=6 * 10**9, bytes_accessed=20 * 10**6, transcendentals=3 * 10**6),
    )(x_all, start_row, gain, shift, w_t, b_cols, cos, sin)


def feed_kernel(
    o_ref, x_ref, start_ref, gain_ref, shift_ref, w_out_ref, b_out_ref, w_up_ref, b_up_ref,
    w_down_ref, b_down_ref, cot_ref,
    layer_ref, gmid_ref, do_ref, gdown_ref, gup_ref, small_ref, gbup_ref,
    middle_ref, unit_ref, inv_ref, second_ref, second_t_ref, acc_ref, gsec_ref,
):
    j = pl.program_id(0)
    last = pl.num_programs(0) - 1

    @pl.when(j == 0)
    def _():
        attended = o_ref[...].T.astype(BF)
        residual = x_ref[...].astype(F32) + start_ref[...]
        middle = residual + dot(attended, w_out_ref[...], NN) + b_out_ref[...]
        middle_ref[...] = middle
        unit, inverse = unit_norm(middle)
        unit_ref[...] = unit
        inv_ref[...] = inverse
        second = unit * gain_ref[1:2, :] + shift_ref[1:2, :]
        second_ref[...] = second.astype(BF)
        second_t_ref[...] = second.T.astype(BF)
        acc_ref[...] = jnp.zeros_like(acc_ref)
        gsec_ref[...] = jnp.zeros_like(gsec_ref)

    @pl.when(j < last)
    def _():
        cot = cot_ref[...]
        hidden = dot(second_ref[...], w_up_ref[...], NN) + b_up_ref[...]
        cdf = 0.5 + 0.5 * lax.erf(hidden * (0.5**0.5))
        active = (hidden * cdf).astype(BF)
        slope = cdf + hidden * (jnp.exp(-0.5 * hidden * hidden) * (1.0 / math.sqrt(2.0 * math.pi)))
        acc_ref[...] += dot(active, w_down_ref[...], NN)
        ghid = dot(cot, w_down_ref[...], NT) * slope
        ghid_low = ghid.astype(BF)
        gsec_ref[...] += dot(ghid_low, w_up_ref[...], NT)
        gdown_ref[...] = dot(active, cot, TN).astype(BF)
        gup_ref[0] = dot(second_t_ref[...], ghid_low, NN).astype(BF)
        gbup_ref[...] = jnp.sum(ghid_low.astype(F32), axis=0, keepdims=True)

    @pl.when(j == last)
    def _():
        cot = cot_ref[...].astype(F32)
        layer_ref[...] = (middle_ref[...] + acc_ref[...] + b_down_ref[...]).astype(BF)
        gsec, unit = gsec_ref[...], unit_ref[...]
        gmid = cot + norm_back(gsec, unit, inv_ref[...], gain_ref[1:2, :])
        gmid_ref[...] = gmid
        branch = gmid.astype(BF)
        gup_ref[0] = dot(o_ref[...].astype(BF), branch, NN).astype(BF)
        do_ref[...] = dot(w_out_ref[...], branch, NT).astype(BF)
        total = lambda v: jnp.sum(v, axis=0, keepdims=True)
        small_ref[0:1, :] = total(gsec * unit)
        small_ref[1:2, :] = total(gsec)
        small_ref[2:3, :] = total(branch.astype(F32))
        small_ref[3:4, :] = total(cot)


def feed_forward(o_t, x_own, start_row, gain, shift, w_out, b_out, w_up, b_up, w_down, b_down, cot):
    rows, width = x_own.shape
    hidden = w_up.shape[1]
    steps = hidden // width
    whole = lambda shape: pl.BlockSpec(shape, lambda j: (0,) * len(shape))
    held = lambda j: jnp.minimum(j, steps - 1)
    return pl.pallas_call(
        feed_kernel,
        grid=(steps + 1,),
        in_specs=[
            whole((width, rows)),
            whole((rows, width)),
            whole((1, width)),
            whole((2, width)),
            whole((2, width)),
            whole((width, width)),
            whole((1, width)),
            pl.BlockSpec((width, width), lambda j: (0, held(j))),
            pl.BlockSpec((1, width), lambda j: (0, held(j))),
            pl.BlockSpec((width, width), lambda j: (held(j), 0)),
            whole((1, width)),
            whole((rows, width)),
        ],
        out_specs=[
            whole((rows, width)),
            whole((rows, width)),
            whole((width, rows)),
            pl.BlockSpec((width, width), lambda j: (held(j), 0)),
            pl.BlockSpec((1, width, width), lambda j: (j, 0, 0)),
            whole((4, width)),
            pl.BlockSpec((1, width), lambda j: (0, held(j))),
        ],
        out_shape=[
            jax.ShapeDtypeStruct((rows, width), BF),
            jax.ShapeDtypeStruct((rows, width), F32),
            jax.ShapeDtypeStruct((width, rows), BF),
            jax.ShapeDtypeStruct((hidden, width), BF),
            jax.ShapeDtypeStruct((steps + 1, width, width), BF),
            jax.ShapeDtypeStruct((4, width), F32),
            jax.ShapeDtypeStruct((1, hidden), F32),
        ],
        scratch_shapes=[
            pltpu.VMEM((rows, width), F32),
            pltpu.VMEM((rows, width), F32),
            pltpu.VMEM((rows, 1), F32),
            pltpu.VMEM((rows, width), BF),
            pltpu.VMEM((width, rows), BF),
            pltpu.VMEM((rows, width), F32),
            pltpu.VMEM((rows, width), F32),
        ],
        compiler_params=params(),
        name="feed_forward",
        cost_estimate=pl.CostEstimate(flops=8 * 10**9, bytes_accessed=24 * 10**6, transcendentals=10**6),
    )(o_t, x_own, start_row, gain, shift, w_out, b_out, w_up, b_up, w_down, b_down, cot)


def backward_kernel(
    q_ref, k_ref, v_ref, p_ref, o_ref, do_ref, first_t_ref, w_ref, cos_ref, sin_ref,
    gqkv_ref, gb_ref, gx_own, gx_1, gx_2, gx_3,
    acc_ref, gq_ref, gk_ref, gv_ref,
):
    group = pl.program_id(0)
    rows = q_ref.shape[1]
    half = HEAD_DIM // 2
    cos, sin = cos_ref[...], sin_ref[...]

    def unrotated(part, width):
        lo, hi = part[:half], part[half:]
        c, s = cos[:, :width], sin[:, :width]
        return jnp.concatenate([lo * c + hi * s, hi * c - lo * s], axis=0)

    for head in range(HEADS_PER_STEP):
        at = slice(head * HEAD_DIM, (head + 1) * HEAD_DIM)
        do_t = do_ref[at, :]
        weights = p_ref[head]
        gweights = dot(v_ref[at, :].astype(F32).T.astype(BF), do_t, NN)
        inner = jnp.sum(do_t.astype(F32) * o_ref[at, :], axis=0, keepdims=True)
        gscores = (weights.astype(F32) * (gweights - inner)).astype(BF)
        gq = dot(k_ref[at, :], gscores, NN) * HEAD_DIM**-0.5
        gk = dot(q_ref[at, :], gscores, NT)
        gv_ref[at, :] = dot(do_t, weights, NT).astype(BF)
        gq_ref[at, :] = unrotated(gq, rows).astype(BF)
        gk_ref[at, :] = unrotated(gk, gk.shape[1]).astype(BF)

    gq, gk, gv = gq_ref[...], gk_ref[...], gv_ref[...]
    first_t = first_t_ref[...]
    gqkv_ref[0] = dot(first_t[:, :rows], gq, NT).astype(BF)
    gqkv_ref[1] = dot(first_t, gk, NT).astype(BF)
    gqkv_ref[2] = dot(first_t, gv, NT).astype(BF)
    ones = jnp.ones((8, gk.shape[1]), BF)
    gb_ref[0] = dot(ones[:, :rows], gq, NT)
    gb_ref[1] = dot(ones, gk, NT)
    gb_ref[2] = dot(ones, gv, NT)
    back = dot(w_ref[1], gk, NN) + dot(w_ref[2], gv, NN)
    own = dot(w_ref[0], gq, NN)

    @pl.when(group == 0)
    def _():
        acc_ref[...] = back

    @pl.when(group > 0)
    def _():
        acc_ref[...] += back

    acc_ref[:, :rows] += own

    @pl.when(group == pl.num_programs(0) - 1)
    def _():
        gx_own[...] = acc_ref[:, :rows]
        gx_1[...] = acc_ref[:, rows : 2 * rows].astype(BF)
        gx_2[...] = acc_ref[:, 2 * rows : 3 * rows].astype(BF)
        gx_3[...] = acc_ref[:, 3 * rows :].astype(BF)


def attention_backward(q_t, k_t, v_t, p_t, o_t, do_t, first_t, w_cols, cos, sin):
    width, rows = q_t.shape
    length = k_t.shape[1]
    step = HEADS_PER_STEP * HEAD_DIM
    whole = lambda shape: pl.BlockSpec(shape, lambda g: (0,) * len(shape))
    return pl.pallas_call(
        backward_kernel,
        grid=(HEADS // HEADS_PER_STEP,),
        in_specs=[
            pl.BlockSpec((step, rows), lambda g: (g, 0)),
            pl.BlockSpec((step, length), lambda g: (g, 0)),
            pl.BlockSpec((step, length), lambda g: (g, 0)),
            pl.BlockSpec((HEADS_PER_STEP, length, rows), lambda g: (g, 0, 0)),
            pl.BlockSpec((step, rows), lambda g: (g, 0)),
            pl.BlockSpec((step, rows), lambda g: (g, 0)),
            whole((width, length)),
            pl.BlockSpec((3, width, step), lambda g: (0, 0, g)),
            whole(cos.shape),
            whole(sin.shape),
        ],
        out_specs=[
            pl.BlockSpec((3, width, step), lambda g: (0, 0, g)),
            pl.BlockSpec((3, 8, step), lambda g: (0, 0, g)),
            whole((width, rows)),
            whole((width, rows)),
            whole((width, rows)),
            whole((width, rows)),
        ],
        out_shape=[
            jax.ShapeDtypeStruct((3, width, width), BF),
            jax.ShapeDtypeStruct((3, 8, width), F32),
            jax.ShapeDtypeStruct((width, rows), F32),
            jax.ShapeDtypeStruct((width, rows), BF),
            jax.ShapeDtypeStruct((width, rows), BF),
            jax.ShapeDtypeStruct((width, rows), BF),
        ],
        scratch_shapes=[
            pltpu.VMEM((width, length), F32),
            pltpu.VMEM((step, rows), BF),
            pltpu.VMEM((step, length), BF),
            pltpu.VMEM((step, length), BF),
        ],
        compiler_params=params(),
        name="attention_backward",
        cost_estimate=pl.CostEstimate(flops=12 * 10**9, bytes_accessed=30 * 10**6, transcendentals=0),
    )(q_t, k_t, v_t, p_t, o_t, do_t, first_t, w_cols, cos, sin)


def entry_kernel(g0_ref, g1_ref, g2_ref, g3_ref, x_ref, start_ref, gain_ref, gmid_ref, flag_ref, gtok_ref, small_ref):
    grad_t = g0_ref[...] + g1_ref[...].astype(F32) + g2_ref[...].astype(F32) + g3_ref[...].astype(F32)
    grad = grad_t.T
    residual = x_ref[...].astype(F32) + start_ref[...]
    unit, inverse = unit_norm(residual)
    gres = gmid_ref[...] + norm_back(grad, unit, inverse, gain_ref[0:1, :])
    gtok_ref[...] = gres.astype(BF)
    small_ref[0:1, :] = jnp.sum(grad * unit, axis=0, keepdims=True)
    small_ref[1:2, :] = jnp.sum(grad, axis=0, keepdims=True)
    small_ref[2:3, :] = jnp.sum(gres, axis=0, keepdims=True) * flag_ref[...]


def entry_backward(pieces, x_own, start_row, gain, gmid, flag_row):
    rows, width = x_own.shape
    return pl.pallas_call(
        entry_kernel,
        out_shape=[jax.ShapeDtypeStruct((rows, width), BF), jax.ShapeDtypeStruct((3, width), F32)],
        compiler_params=params(),
        name="entry_backward",
        cost_estimate=pl.CostEstimate(flops=10**7, bytes_accessed=4 * 10**6, transcendentals=0),
    )(*pieces, x_own, start_row, gain, gmid, flag_row)


BITS = {"c": ("dp", 1), "x": ("dp", 2), "y": ("dp", 4), "z": ("seq", 1), "w": ("seq", 2)}


def my_bit(name):
    axis, mask = BITS[name]
    return (lax.axis_index(axis) // mask) % 2


def other_bits():
    dp = lax.axis_size("dp")
    return [1 << k for k in range(3, dp.bit_length() - 1)]


def xor_pairs(size, mask):
    return [(i, i ^ mask) for i in range(size)]


def swap(value, names):
    dp, seq = lax.axis_size("dp"), lax.axis_size("seq")
    pairs = []
    for d in range(dp):
        axis, mask = BITS[names[d % 2]]
        for s in range(seq):
            to = (d ^ mask) * seq + s if axis == "dp" else d * seq + (s ^ mask)
            pairs.append((d * seq + s, to))
    return lax.ppermute(value, ("dp", "seq"), pairs)


def pick(array, index):
    return lax.dynamic_index_in_dim(array, index, 1, keepdims=False)


def scatter_sum(grads, orders):
    core = my_bit("c")
    parts = [grads.reshape(grads.shape[:1] + (2,) * 5 + grads.shape[2:])]
    for names in zip(*orders):
        bit = jnp.where(core == 0, my_bit(names[0]), my_bit(names[1]))
        send = sum(pick(p, 1 - bit).astype(F32) for p in parts).astype(BF)
        parts = [pick(p, bit) for p in parts] + [swap(send, names)]
    shard = sum(p.astype(F32) for p in parts)
    for mask in other_bits():
        shard = shard + lax.ppermute(shard.astype(BF), "dp", xor_pairs(lax.axis_size("dp"), mask)).astype(F32)
    return shard.astype(BF)


def gather_blocks(shard, orders):
    held = shard[:, None]
    for names in list(zip(*orders))[:0:-1]:
        held = jnp.concatenate([held, swap(held, names)], axis=1)
    return held, swap(held, ("c", "c"))


def place_of(orders):
    core = my_bit("c")
    low = []
    for order in orders:
        at = jnp.int32(0)
        for name in order[1:]:
            at = at * 2 + my_bit(name)
        low.append(at)
    own, other = jnp.where(core == 0, low[0], low[1]), jnp.where(core == 0, low[1], low[0])
    return jnp.stack([core, own, other]).astype(jnp.int32)


def all_sum(value):
    for axis in ("dp", "seq"):
        size = lax.axis_size(axis)
        for k in range(size.bit_length() - 1):
            value = value + lax.ppermute(value, axis, xor_pairs(size, 1 << k))
    return value


def spread_kernel(kind, at_ref, held_ref, other_ref, *outs):
    core = at_ref[0]
    held, other = held_ref[:, 0].astype(F32), other_ref[:, 0].astype(F32)
    for side in range(2):
        block = jnp.where(core == side, held, other)
        if kind == "heads":
            (out,) = outs
            two = 2 * HEAD_DIM
            for pair in range(HEADS // 2):
                q, k, v = (block[i, :, pair * two : (pair + 1) * two] for i in range(3))
                low = lambda a: a[:, :HEAD_DIM]
                high = lambda a: a[:, HEAD_DIM:]
                row = jnp.concatenate([low(q), low(k), low(v), high(q), high(k), high(v)], axis=1)
                out[side, 0, :, pair * 3 * two : (pair + 1) * 3 * two] = row
        else:
            width = block.shape[-1]
            main = outs[0]
            wide = main.shape[-1] // width
            for i in range(wide):
                main[side, 0, :, i * width : (i + 1) * width] = block[i]
            if len(outs) > 1:
                outs[1][side, 0] = block[wide]


def spread(kind, place, held, other, widths):
    n, half, rows, width = held.shape
    block = lambda who: pl.BlockSpec((n, 1, rows, width), lambda b, at: (0, b ^ at[who], 0, 0))
    outs = pl.pallas_call(
        lambda *refs: spread_kernel(kind, *refs),
        grid_spec=pltpu.PrefetchScalarGridSpec(
            num_scalar_prefetch=1,
            grid=(half,),
            in_specs=[block(1), block(2)],
            out_specs=[pl.BlockSpec((2, 1, rows, w), lambda b, at: (0, b, 0, 0)) for w in widths],
        ),
        out_shape=[jax.ShapeDtypeStruct((2, half, rows, w), F32) for w in widths],
        compiler_params=params(),
        name="spread_" + kind,
        cost_estimate=pl.CostEstimate(flops=0, bytes_accessed=12 * n * half * rows * width, transcendentals=0),
    )(place, held, other)
    return [o.reshape(2 * half * rows, w) for o, w in zip(outs, widths)]


ORDERS_DOWN = (("c", "x", "y", "z", "w"), ("c", "y", "x", "z", "w"))
ORDERS_UP = (("c", "x", "y", "z", "w"), ("c", "z", "x", "y", "w"))
ORDERS_HEADS = (("c", "y", "x", "z", "w"), ("c", "z", "y", "x", "w"))


def total_of(kind, grads, orders, widths):
    n, blocks = grads.shape[0], 32
    grads = grads.reshape(n, blocks, grads.shape[1] // blocks, grads.shape[2])
    held, other = gather_blocks(scatter_sum(grads, orders), orders)
    return spread(kind, place_of(orders), held, other, widths)


def per_device(
    tokens, codon_positions, start_flags, start_embed, norm_gain, norm_shift, w_qkv, b_qkv,
    w_out, b_out, w_up, b_up, w_down, b_down, cotangent,
):
    width = tokens.shape[-1]
    groups = lax.axis_size("seq")
    x_own, cot, positions = tokens[0], cotangent[0], codon_positions[0]
    flag = start_flags.astype(F32)
    start_row = flag[:, None] * start_embed[None, :]

    def everyone(value):
        return [value] + [lax.ppermute(value, "seq", xor_pairs(groups, k)) for k in range(1, groups)]

    positions = jnp.concatenate(everyone(positions))
    x_all = jnp.concatenate(everyone(x_own))
    half = HEAD_DIM // 2
    frequency = 10000.0 ** (-2.0 * jnp.arange(half, dtype=F32) / HEAD_DIM)
    angles = frequency[:, None] * positions.astype(F32)[None, :]
    cos, sin = jnp.cos(angles), jnp.sin(angles)
    by_head = w_qkv.reshape(width, HEADS, 3, HEAD_DIM)
    w_cols = by_head.transpose(2, 0, 1, 3).reshape(3, width, width)
    w_t = by_head.transpose(2, 1, 3, 0).reshape(3, width, width)
    b_cols = b_qkv.reshape(HEADS, 3, HEAD_DIM).transpose(1, 0, 2).reshape(3, width, 1)

    q_t, k_t, v_t, p_t, o_t, first_t = attention_forward(x_all, start_row, norm_gain, norm_shift, w_t, b_cols, cos, sin)
    layer_out, gmid, do_t, gdown, gup, small_feed, gbup = feed_forward(
        o_t, x_own, start_row, norm_gain, norm_shift, w_out, b_out[None], w_up, b_up[None], w_down, b_down[None], cot
    )
    (grad_down,) = total_of("down", gdown[None], ORDERS_DOWN, (width,))
    grad_up, grad_wout = total_of("up", gup, ORDERS_UP, (w_up.shape[1], width))
    gqkv, gbqkv, *pieces = attention_backward(q_t, k_t, v_t, p_t, o_t, do_t, first_t, w_cols, cos, sin)
    (grad_qkv,) = total_of("heads", gqkv, ORDERS_HEADS, (3 * width,))
    pieces = pieces[:1] + [lax.ppermute(piece, "seq", xor_pairs(groups, k + 1)) for k, piece in enumerate(pieces[1:])]
    grad_tokens, small_entry = entry_backward(pieces, x_own, start_row, norm_gain, gmid, flag[:, None])
    smalls = all_sum(jnp.concatenate([small_feed, gbup.reshape(-1, width), gbqkv[:, 0], small_entry]))
    gain_1, shift_1, grad_bout, grad_bdown = smalls[:4]
    grad_bup = smalls[4:-6].reshape(-1)
    grad_bqkv = smalls[-6:-3].reshape(3, HEADS, HEAD_DIM).transpose(1, 0, 2).reshape(-1)
    gain_0, shift_0, grad_start = smalls[-3:]
    return (
        layer_out[None],
        grad_tokens[None],
        grad_start,
        jnp.stack([gain_0, gain_1]),
        jnp.stack([shift_0, shift_1]),
        grad_qkv,
        grad_bqkv,
        grad_wout,
        grad_bout,
        grad_up,
        grad_bup,
        grad_down,
        grad_bdown,
    )


def solution(mesh):
    rows = P("dp", "seq", None)
    return jax.shard_map(
        per_device,
        mesh=mesh,
        in_specs=(rows, P("dp", "seq"), P("dp")) + (P(),) * 11 + (rows,),
        out_specs=(rows, rows) + (P(),) * 11,
        check_vma=False,
    )
```

time: 747 us -> 407 us (0.54)
  waiting for transfers between devices: 426 us -> 118 us
  Pallas kernels: 0 us -> 96.7 us
  matrix products: 73.5 us -> 0 us
  starting transfers between devices: 15.2 us -> 88.1 us
  local copies, waits for them, and re-layouts: 116 us -> 49.4 us
  blocking collectives: 57.1 us -> 0 us
  between operations: 15.7 us -> 1.57 us
  other arithmetic: 37.8 us -> 50.7 us
    psum x1 -> x0, waiting for transfers between devices: 375 us -> none  [per_device(): lax.psum((grad_start, grad_gain, grad_shift, grad_qkv, grad_bqkv, grad_wo...]
    ppermute x0 -> x44, waiting for transfers between devices: none -> 118 us  [the longest x30 70 us: swap(): return lax.ppermute(value, ('dp', 'seq'), pairs)]
    pallas_call x0 -> x7, Pallas kernels: none -> 96.7 us  [the longest x3 37.6 us: spread(): pl.pallas_call(lambda *refs: spread_kernel(kind, *refs), grid_spec=pltpu....]
    ppermute x0 -> x44, starting transfers between devices: none -> 88.1 us  [the longest x30 51.2 us: swap(): return lax.ppermute(value, ('dp', 'seq'), pairs)]
    dot_general x26 -> x0, matrix products: 73.5 us -> none  [the longest x1 11.6 us: per_device(): jnp.einsum('scd,df->scf', second_low, w_up, preferred_element_type=jnp.fl...]
    all_to_all x3 -> x0, waiting for transfers between devices: 51.2 us -> none  [the longest x1 28.6 us: per_device(): lax.all_to_all(packed, 'seq', split_axis=2, concat_axis=1, tiled=True)]
    psum x1 -> x0, blocking collectives: 41.3 us -> none  [per_device(): lax.psum((grad_start, grad_gain, grad_shift, grad_qkv, grad_bqkv, grad_wo...]
    unnamed x95 -> x39, local copies, waits for them, and re-layouts: 42.1 us -> 17 us
  transfers between devices with their start and end apart: 4 -> 44, of which waited for: 4 -> 20; matrix products, arithmetic and copies ran while one was open for 4% -> 23% of each run, Pallas kernels for 0% -> 12%
where the time goes in v1:
time: 407 us; the launch traced here: 405 us
  waiting for transfers between devices  118 us (29%)
  Pallas kernels  96.7 us (24%)
  starting transfers between devices  88.1 us (22%)
  other arithmetic  50.7 us (12%)
  local copies, waits for them, and re-layouts  49.4 us (12%)
    ppermute x30, waiting for transfers between devices, swap(): return lax.ppermute(value, ('dp', 'seq'), pairs)  70 us
    ppermute x30, starting transfers between devices, swap(): return lax.ppermute(value, ('dp', 'seq'), pairs)  51.2 us
    pallas_call x3, Pallas kernels, spread(): pl.pallas_call(lambda *refs: spread_kernel(kind, *refs), grid_spec=pltpu....  37.6 us
    convert_element_type x12, other arithmetic, scatter_sum(): send = sum((pick(p, 1 - bit).astype(F32) for p in parts)).astype(BF)  25.2 us
    ppermute x3, waiting for transfers between devices, per_device(): lax.ppermute(piece, 'seq', xor_pairs(groups, k + 1))  23.5 us
    pallas_call x1, Pallas kernels, attention_backward(): pl.pallas_call(backward_kernel, grid=(HEADS // HEADS_PER_STEP,), in_specs...  22 us
    ppermute x6, starting transfers between devices, everyone(): lax.ppermute(value, 'seq', xor_pairs(groups, k))  17.6 us
    pallas_call x1, Pallas kernels, attention_forward(): pl.pallas_call(forward_kernel, grid=(HEADS // HEADS_PER_STEP,), in_specs=...  17.5 us
  transfers between devices with their start and end apart: 44, of which 20 were waited for; matrix products, arithmetic and copies ran while one was open for 23% of the time, Pallas kernels for 12%

profile of v1, /device:TPU:0, one launch (start us, length us, event | category | flops | bytes accessed | tf_op | source)
XLA Modules:
  0.0 404.5 jit_solution(9271357539980662798)
XLA Ops:
  0.6 5.1 %collective-permute-start.2 = (bf16[256,768]{1,0:T(8,128)(2,1)}, bf16[256,768]{1,0:T(8,128)(2,1)}, u32[]{:S(2)}, u32[]{:S(2)}) collective-permute-start(bf16[256,768]{1,0:T(8,128)(2,1)} %bitcast.281), channel_id=1, source_target_pairs={{0,3},{1,2},{2,1},{3,0},{4,7},{5,6},{6,5},{7,4},{8,11},{9,10},{10,... | collective-permute-start | bytes 1179656 | tf_op jit(solution)/shard_map/ppermute | solution.py:508
  6.4 3.7 collective-permute-start.5
  12.6 4.5 %copy.30 = bf16[768,2304]{0,1:T(8,128)(2,1)S(1)} copy(bf16[768,2304]{1,0:T(8,128)(2,1)} %param.21) | data formatting | bytes 7077888 | tf_op args[6]
  17.1 14.9 %collective-permute-done.5 = s32[256]{0:T(256)S(1)} collective-permute-done((s32[256]{0:T(256)}, s32[256]{0:T(256)S(1)}, u32[]{:S(2)}, u32[]{:S(2)}) %collective-permute-start.5) | collective-permute-done | bytes 1056 | tf_op jit(solution)/shard_map/ppermute | solution.py:508
  32.1 8.1 %collective-permute-start.3 = (s32[256]{0:T(256)}, s32[256]{0:T(256)}, u32[]{:S(2)}, u32[]{:S(2)}) collective-permute-start(s32[256]{0:T(256)} %bitcast.6), channel_id=1, source_target_pairs={{0,1},{1,0},{2,3},{3,2},{4,5},{5,4},{6,7},{7,6},{8,9},{9,8},{10,11... | collective-permute-start | bytes 3080 | tf_op jit(solution)/shard_map/ppermute | solution.py:508
  40.2 2.0 copy.31
  44.2 2.9 reshape.707.b_ref
  49.7 1.9 multiply_sine_fusion
  51.6 2.6 pad_maximum_fusion.x_ref
  54.2 17.5 %attention_forward.1 = (bf16[768,256]{1,0:T(8,128)(2,1)}, bf16[768,1024]{1,0:T(8,128)(2,1)}, bf16[768,1024]{1,0:T(8,128)(2,1)}, bf16[12,1024,256]{2,1,0:T(8,128)...) custom-call(bf16[1024,768]{1,0:T(8,128)(2,1)} %pad_maximum_fusion.x_ref, f32[1,768]{1,0:T(1,128)} %mul.71.shift_in_ref.start_ref, ...), custom_call_target="tpu_custom_call" | custom-call | flops 6000000000 | bytes 20000000 | tf_op jit(solution)/shard_map/attention_forward/pallas_call | solution.py:93
  71.7 16.0 %feed_forward.1 = (bf16[256,768]{1,0:T(8,128)(2,1)}, f32[256,768]{1,0:T(8,128)}, bf16[768,256]{1,0:T(8,128)(2,1)}, bf16[3072,768]{1,0:T(8,128)(2,1)}, bf16[5,768...) custom-call(f32[768,256]{1,0:T(8,128)} %get-tuple-element.36.o_ref, bf16[256,768]{1,0:T(8,128)(2,1)} %bitcast.285, ...), custom_call_target="tpu_custom_call" | custom-call | flops 8000000000 | bytes 24000000 | tf_op jit(solution)/shard_map/feed_forward/pallas_call | solution.py:191
  87.8 3.9 copy_bitcast_fusion
  93.7 2.0 copy.34
  95.7 6.0 %copy.35.w_ref = bf16[3,768,768]{2,1,0:T(8,128)(2,1)} copy(bf16[3,768,768]{1,2,0:T(8,128)(2,1)} %bitcast.259) | data formatting | bytes 7077888 | tf_op jit(solution)/shard_map/reshape | solution.py:517
  101.8 2.2 fusion
  105.5 22.0 %attention_backward.1 = (bf16[3,768,768]{2,1,0:T(8,128)(2,1)}, f32[3,8,768]{2,1,0:T(8,128)}, f32[768,256]{1,0:T(8,128)}, bf16[768,256]{1,0:T(8,128)(2,1)}, bf16[...) custom-call(bf16[768,256]{1,0:T(8,128)(2,1)} %get-tuple-element.38.q_ref, bf16[768,1024]{1,0:T(8,128)(2,1)} %get-tuple-element.39.k_ref, ...), custom_call_target="tpu_custom_call" | custom-call | flops 12000000000 | bytes 30000000 | tf_op jit(solution)/shard_map/attention_backward/pallas_call | solution.py:304
  127.5 2.8 copy_bitcast_fusion.1
  130.3 3.0 fusion.3
  134.9 3.1 fusion.1
  138.5 11.6 %collective-permute-done.26 = bf16[5,2,2,24,768]{4,3,0,2,1:T(8,128)(2,1)} collective-permute-done((bf16[5,2,2,24,768]{4,3,0,2,1:T(8,128)(2,1)}, bf16[5,2,2,24,768]{4,3,0,2,1:T(8,128)(2,1)}, u32[]{:S(2)}, u32[]{:S(2)}) %collective-permute-start.26) | collective-permute-done | bytes 737312 | tf_op jit(solution)/shard_map/ppermute | solution.py:395
  150.1 2.2 fusion.6
  152.7 7.4 %collective-permute-done.27 = bf16[5,2,24,768]{3,2,0,1:T(8,128)(2,1)} collective-permute-done((bf16[5,2,24,768]{3,2,0,1:T(8,128)(2,1)}, bf16[5,2,24,768]{3,2,0,1:T(8,128)(2,1)}, u32[]{:S(2)}, u32[]{:S(2)}) %collective-permute-start.27) | collective-permute-done | bytes 368672 | tf_op jit(solution)/shard_map/ppermute | solution.py:395
  163.0 2.3 fusion.2
  166.8 2.4 fusion.4
  169.8 4.1 %collective-permute-done.28 = bf16[5,24,768]{2,1,0:T(8,128)(2,1)S(1)} collective-permute-done((bf16[5,24,768]{2,1,0:T(8,128)(2,1)S(1)}, bf16[5,24,768]{2,1,0:T(8,128)(2,1)S(1)}, u32[]{:S(2)}, u32[]{:S(2)}) %collective-permute-start.28) | collective-permute-done | bytes 184352 | tf_op jit(solution)/shard_map/ppermute | solution.py:395
  173.9 2.1 constant_dynamic-update-slice_fusion.9
  176.0 11.4 %collective-permute-done.29 = bf16[5,1,24,768]{3,2,1,0:T(8,128)(2,1)S(1)} collective-permute-done((bf16[5,1,24,768]{3,2,1,0:T(8,128)(2,1)S(1)}, bf16[5,1,24,768]{3,2,1,0:T(8,128)(2,1)S(1)}, u32[]{:S(2)}, u32[]{:S(2)}) %collective-permute-start.29) | collective-permute-done | bytes 184352 | tf_op jit(solution)/shard_map/ppermute | solution.py:395
  188.2 2.1 fusion.7
  190.3 2.0 collective-permute-start.37
  192.3 2.1 fusion.5
  194.4 3.3 collective-permute-done.30
  197.7 2.1 pad_maximum_fusion.4
  199.7 2.6 collective-permute-start.31
  204.4 7.3 %collective-permute-done.38 = bf16[1,96,768]{2,1,0:T(8,128)(2,1)S(1)} collective-permute-done((bf16[1,96,768]{2,1,0:T(8,128)(2,1)S(1)}, bf16[1,96,768]{2,1,0:T(8,128)(2,1)S(1)}, u32[]{:S(2)}, u32[]{:S(2)}) %collective-permute-start.38) | collective-permute-done | bytes 147488 | tf_op jit(solution)/shard_map/ppermute | solution.py:395
  211.7 2.0 constant_dynamic-update-slice_fusion.14
  213.8 2.0 fusion.8
  215.7 2.5 collective-permute-start.17
  218.2 4.2 %collective-permute-done.39 = bf16[1,1,96,768]{3,2,1,0:T(8,128)(2,1)} collective-permute-done((bf16[1,1,96,768]{3,2,1,0:T(8,128)(2,1)}, bf16[1,1,96,768]{3,2,1,0:T(8,128)(2,1)}, u32[]{:S(2)}, u32[]{:S(2)}) %collective-permute-start.39) | collective-permute-done | bytes 147488 | tf_op jit(solution)/shard_map/ppermute | solution.py:395
  222.4 1.7 pad_maximum_fusion.8
  226.8 2.7 collective-permute-start.18
  229.5 7.1 %collective-permute-done.40 = bf16[1,2,96,768]{3,2,1,0:T(8,128)(2,1)} collective-permute-done((bf16[1,2,96,768]{3,2,1,0:T(8,128)(2,1)}, bf16[1,2,96,768]{3,2,1,0:T(8,128)(2,1)}, u32[]{:S(2)}, u32[]{:S(2)}) %collective-permute-start.40) | collective-permute-done | bytes 294944 | tf_op jit(solution)/shard_map/ppermute | solution.py:395
  237.9 1.8 constant_dynamic-update-slice_fusion.4
  239.9 6.4 %collective-permute-done.19 = bf16[3,1,24,768]{3,2,1,0:T(8,128)(2,1)S(1)} collective-permute-done((bf16[3,1,24,768]{3,2,1,0:T(8,128)(2,1)S(1)}, bf16[3,1,24,768]{3,2,1,0:T(8,128)(2,1)S(1)}, u32[]{:S(2)}, u32[]{:S(2)}) %collective-permute-start.19) | collective-permute-done | bytes 110624 | tf_op jit(solution)/shard_map/ppermute | solution.py:395
  249.0 5.7 %collective-permute-done.20 = bf16[3,2,24,768]{3,2,1,0:T(8,128)(2,1)S(1)} collective-permute-done((bf16[3,2,24,768]{3,2,1,0:T(8,128)(2,1)S(1)}, bf16[3,2,24,768]{3,2,1,0:T(8,128)(2,1)S(1)}, u32[]{:S(2)}, u32[]{:S(2)}) %collective-permute-start.20) | collective-permute-done | bytes 221216 | tf_op jit(solution)/shard_map/ppermute | solution.py:395
  255.6 1.8 constant_dynamic-update-slice_fusion.7
  257.3 2.0 constant_dynamic-update-slice_fusion.6
  260.6 12.4 %collective-permute-start.33 = (bf16[5,16,24,768]{3,2,1,0:T(8,128)(2,1)}, bf16[5,16,24,768]{3,2,1,0:T(8,128)(2,1)S(1)}, u32[]{:S(2)}, u32[]{:S(2)}) collective-permute-start(bf16[5,16,24,768]{3,2,1,0:T(8,128)(2,1)} %constant_dynamic-update-slice_fusion.5.refs_1_), channel_id=1, source_target_pairs={{0,4},{1,5},{2,6},{3,7},{4,0},{5,1},{6,2},{7,3},{8,12},{9,13},{10,... | collective-permute-start | bytes 8847368 | tf_op jit(solution)/shard_map/ppermute | solution.py:395
  273.2 1.8 collective-permute-start.22
  276.5 1.7 constant_dynamic-update-slice_fusion.12
  280.2 12.4 %collective-permute-start.43 = (bf16[1,16,96,768]{3,2,1,0:T(8,128)(2,1)}, bf16[1,16,96,768]{3,2,1,0:T(8,128)(2,1)}, u32[]{:S(2)}, u32[]{:S(2)}) collective-permute-start(bf16[1,16,96,768]{3,2,1,0:T(8,128)(2,1)} %constant_dynamic-update-slice_fusion.10.refs_1_), channel_id=1, source_target_pairs={{0,4},{1,5},{2,6},{3,7},{4,0},{5,1},{6,2},{7,3},{8,12},{9,13},{10,... | collective-permute-start | bytes 7077896 | tf_op jit(solution)/shard_map/ppermute | solution.py:395
  296.0 5.4 %collective-permute-start.23 = (bf16[3,16,24,768]{3,2,1,0:T(8,128)(2,1)}, bf16[3,16,24,768]{3,2,1,0:T(8,128)(2,1)}, u32[]{:S(2)}, u32[]{:S(2)}) collective-permute-start(bf16[3,16,24,768]{3,2,1,0:T(8,128)(2,1)} %constant_dynamic-update-slice_fusion.refs_1_), channel_id=1, source_target_pairs={{0,4},{1,5},{2,6},{3,7},{4,0},{5,1},{6,2},{7,3},{8,12},{9,13},{10,... | collective-permute-start | bytes 5308424 | tf_op jit(solution)/shard_map/ppermute | solution.py:395
  301.5 2.8 collective-permute-start.7
  304.6 1.7 collective-permute-start.8
  308.5 23.1 %collective-permute-done.7.g2_ref = bf16[768,256]{1,0:T(8,128)(2,1)} collective-permute-done((bf16[768,256]{1,0:T(8,128)(2,1)}, bf16[768,256]{1,0:T(8,128)(2,1)}, u32[]{:S(2)}, u32[]{:S(2)}) %collective-permute-start.7) | collective-permute-done | bytes 393248 | tf_op jit(solution)/shard_map/ppermute | solution.py:529
  331.5 3.5 entry_backward.1
  337.8 3.2 collective-permute-start.10
  341.0 2.1 collective-permute-done.10
  343.8 3.5 collective-permute-done.11
  347.3 8.2 %collective-permute-start.12 = (f32[14,768]{1,0:T(8,128)S(1)}, f32[14,768]{1,0:T(8,128)S(1)}, u32[]{:S(2)}, u32[]{:S(2)}) collective-permute-start(f32[14,768]{1,0:T(8,128)S(1)} %add.952), channel_id=1, source_target_pairs={{0,1},{1,0},{2,3},{3,2},{4,5},{5,4},{6,7},{7,6},{8,9},{9,8},{10,11... | collective-permute-start | bytes 129032 | tf_op jit(solution)/shard_map/ppermute | solution.py:438
  357.6 2.8 collective-permute-start.13
  365.3 11.9 %spread_heads.1 = f32[2,16,24,2304]{3,2,1,0:T(8,128)} custom-call(s32[3]{0:T(128)} %pad_add_fusion.refs_0_, bf16[3,16,24,768]{3,2,1,0:T(8,128)(2,1)} %constant_dynamic-update-slice_fusion.refs_1_, bf16[3,16,24,768]{3,2,1,0:T(8,128)(2,1)} %collective-permute-done.23.refs_2_), custom_call_target="tpu_custom_call" | custom-call | bytes 10616832 | tf_op jit(solution)/shard_map/spread_heads/pallas_call | solution.py:469
  377.2 12.4 %spread_down.1 = f32[2,16,96,768]{3,2,1,0:T(8,128)} custom-call(s32[3]{0:T(128)} %pad_add_fusion.2.refs_0_, bf16[1,16,96,768]{3,2,1,0:T(8,128)(2,1)} %constant_dynamic-update-slice_fusion.10.refs_1_, bf16[1,16,96,768]{3,2,1,0:T(8,128)(2,1)} %collective-permute-done.43.refs_2_), custom_call_target="tpu_custom_call" | custom-call | bytes 14155776 | tf_op jit(solution)/shard_map/spread_down/pallas_call | solution.py:469
  389.6 1.6 copy-done.3
  391.2 13.3 %spread_up.1 = (f32[2,16,24,3072]{3,2,1,0:T(8,128)}, f32[2,16,24,768]{3,2,1,0:T(8,128)}) custom-call(s32[3]{0:T(128)} %pad_add_fusion.1.refs_0_, bf16[5,16,24,768]{3,2,1,0:T(8,128)(2,1)} %constant_dynamic-update-slice_fusion.5.refs_1_, bf16[5,16,24,768]{3,2,1,0:T(8,128)(2,1)} %copy-done.3), custom_call_target="tpu_custom_call" | custom-call | bytes 17694720 | tf_op jit(solution)/shard_map/spread_up/pallas_call | solution.py:469
  (135 shorter events, 49.8 us)
Async XLA Ops:
  0.6 51.0 %collective-permute-start.2 = (bf16[256,768]{1,0:T(8,128)(2,1)}, bf16[256,768]{1,0:T(8,128)(2,1)}, u32[]{:S(2)}, u32[]{:S(2)}) collective-permute-start(bf16[256,768]{1,0:T(8,128)(2,1)} %bitcast.281), channel_id=1, source_target_pairs={{0,3},{1,2},{2,1},{3,0},{4,7},{5,6},{6,5},{7,4},{8,11},{9,10},{10,... | collective-permute-start | bytes 1179656 | tf_op jit(solution)/shard_map/ppermute | solution.py:508
  5.8 45.9 %collective-permute-start.1 = (bf16[256,768]{1,0:T(8,128)(2,1)}, bf16[256,768]{1,0:T(8,128)(2,1)}, u32[]{:S(2)}, u32[]{:S(2)}) collective-permute-start(bf16[256,768]{1,0:T(8,128)(2,1)} %bitcast.282), channel_id=1, source_target_pairs={{0,2},{1,3},{2,0},{3,1},{4,6},{5,7},{6,4},{7,5},{8,10},{9,11},{10,... | collective-permute-start | bytes 1179656 | tf_op jit(solution)/shard_map/ppermute | solution.py:508
  5.8 45.9 %collective-permute-start = (bf16[256,768]{1,0:T(8,128)(2,1)}, bf16[256,768]{1,0:T(8,128)(2,1)}, u32[]{:S(2)}, u32[]{:S(2)}) collective-permute-start(bf16[256,768]{1,0:T(8,128)(2,1)} %bitcast.283), channel_id=1, source_target_pairs={{0,1},{1,0},{2,3},{3,2},{4,5},{5,4},{6,7},{7,6},{8,9},{9,8},{10,11... | collective-permute-start | bytes 1179656 | tf_op jit(solution)/shard_map/ppermute | solution.py:508
  6.4 25.7 %collective-permute-start.5 = (s32[256]{0:T(256)}, s32[256]{0:T(256)S(1)}, u32[]{:S(2)}, u32[]{:S(2)}) collective-permute-start(s32[256]{0:T(256)} %bitcast.6), channel_id=1, source_target_pairs={{0,3},{1,2},{2,1},{3,0},{4,7},{5,6},{6,5},{7,4},{8,11},{9,10},{10,... | collective-permute-start | bytes 3080 | tf_op jit(solution)/shard_map/ppermute | solution.py:508
  10.1 38.8 %collective-permute-start.4 = (s32[256]{0:T(256)}, s32[256]{0:T(256)}, u32[]{:S(2)}, u32[]{:S(2)}) collective-permute-start(s32[256]{0:T(256)} %bitcast.6), channel_id=1, source_target_pairs={{0,2},{1,3},{2,0},{3,1},{4,6},{5,7},{6,4},{7,5},{8,10},{9,11},{10,... | collective-permute-start | bytes 3080 | tf_op jit(solution)/shard_map/ppermute | solution.py:508
  32.1 8.1 %copy-start.12 = (s32[256]{0:T(256)}, s32[256]{0:T(256)S(1)}, u32[]{:S(2)}) copy-start(s32[256]{0:T(256)S(1)} %collective-permute-done.5) | copy-start | bytes 3076
  32.1 16.9 %collective-permute-start.3 = (s32[256]{0:T(256)}, s32[256]{0:T(256)}, u32[]{:S(2)}, u32[]{:S(2)}) collective-permute-start(s32[256]{0:T(256)} %bitcast.6), channel_id=1, source_target_pairs={{0,1},{1,0},{2,3},{3,2},{4,5},{5,4},{6,7},{7,6},{8,9},{9,8},{10,11... | collective-permute-start | bytes 3080 | tf_op jit(solution)/shard_map/ppermute | solution.py:508
  40.2 2.0 copy-start.10
  40.2 7.0 %copy-start.11 = (f32[768]{0:T(1024)S(1)}, f32[768]{0:T(1024)}, u32[]{:S(2)}) copy-start(f32[768]{0:T(1024)} %param.24) | copy-start | bytes 9220
  87.8 3.9 copy-start
  91.7 10.1 %collective-permute-start.24 = (bf16[5,2,2,2,2,24,768]{6,5,0,4,3,2,1:T(8,128)(2,1)}, bf16[5,2,2,2,2,24,768]{6,5,0,4,3,2,1:T(8,128)(2,1)}, u32[]{:S(2)}, u32[]{:S(2)}) collective-permute-start(bf16[5,2,2,2,2,24,768]{6,5,0,4,3,2,1:T(8,128)(2,1)} %copy_bitcast_fusion), channel_id=1, source_target_pairs={{0,4},{1,5},{2,6},{3,7},{4,0},{5,1},{6,2},{7,3},{8,12},{9,13},{10,... | collective-permute-start | bytes 8847368 | tf_op jit(solution)/shard_map/ppermute | solution.py:395
  93.2 41.6 %collective-permute-start.34 = (bf16[1,2,2,2,2,96,768]{6,5,4,3,2,1,0:T(8,128)(2,1)}, bf16[1,2,2,2,2,96,768]{6,5,4,3,2,1,0:T(8,128)(2,1)}, u32[]{:S(2)}, u32[]{:S(2)}) collective-permute-start(bf16[1,2,2,2,2,96,768]{6,5,4,3,2,1,0:T(8,128)(2,1)} %dynamic-slice_bitcast_fusion), channel_id=1, source_target_pairs={{0,4},{1,5},{2,6},{3,7},{4,0},{5,1},{6,2},{7,3},{8,12},{9,13},{10,... | collective-permute-start | bytes 7077896 | tf_op jit(solution)/shard_map/ppermute | solution.py:395
  103.9 26.4 %collective-permute-start.25 = (bf16[5,2,2,2,24,768]{5,4,0,3,2,1:T(8,128)(2,1)S(1)}, bf16[5,2,2,2,24,768]{5,4,0,3,2,1:T(8,128)(2,1)S(1)}, u32[]{:S(2)}, u32[]{:S(2)}) collective-permute-start(bf16[5,2,2,2,24,768]{5,4,0,3,2,1:T(8,128)(2,1)S(1)} %fusion), channel_id=1, source_target_pairs={{0,8},{1,9},{2,10},{3,11},{4,5},{5,4},{6,7},{7,6},{8,0},{9,1},{10,... | collective-permute-start | bytes 4423688 | tf_op jit(solution)/shard_map/ppermute | solution.py:395
  130.3 32.7 %collective-permute-start.14 = (bf16[3,2,2,2,2,24,768]{6,5,0,4,3,2,1:T(8,128)(2,1)}, bf16[3,2,2,2,2,24,768]{6,5,0,4,3,2,1:T(8,128)(2,1)}, u32[]{:S(2)}, u32[]{:S(2)}) collective-permute-start(bf16[3,2,2,2,2,24,768]{6,5,0,4,3,2,1:T(8,128)(2,1)} %copy_bitcast_fusion.1), channel_id=1, source_target_pairs={{0,4},{1,5},{2,6},{3,7},{4,0},{5,1},{6,2},{7,3},{8,12},{9,13},{10,... | collective-permute-start | bytes 5308424 | tf_op jit(solution)/shard_map/ppermute | solution.py:395
  130.3 4.5 %copy-start.6 = (bf16[5,2,2,2,24,768]{5,4,0,3,2,1:T(8,128)(2,1)}, bf16[5,2,2,2,24,768]{5,4,0,3,2,1:T(8,128)(2,1)S(1)}, u32[]{:S(2)}) copy-start(bf16[5,2,2,2,24,768]{5,4,0,3,2,1:T(8,128)(2,1)S(1)} %collective-permute-done.25) | copy-start | bytes 4423684
  133.3 16.7 %collective-permute-start.26 = (bf16[5,2,2,24,768]{4,3,0,2,1:T(8,128)(2,1)}, bf16[5,2,2,24,768]{4,3,0,2,1:T(8,128)(2,1)}, u32[]{:S(2)}, u32[]{:S(2)}) collective-permute-start(bf16[5,2,2,24,768]{4,3,0,2,1:T(8,128)(2,1)} %fusion.3), channel_id=1, source_target_pairs={{0,16},{1,17},{2,18},{3,19},{4,12},{5,13},{6,14},{7,15},{8,24},{9,... | collective-permute-start | bytes 2211848 | tf_op jit(solution)/shard_map/ppermute | solution.py:395
  134.9 28.2 %copy-start.1 = (bf16[3,768,768]{2,1,0:T(8,128)(2,1)S(1)}, bf16[3,768,768]{2,1,0:T(8,128)(2,1)}, u32[]{:S(2)}) copy-start(bf16[3,768,768]{2,1,0:T(8,128)(2,1)} %get-tuple-element.54) | copy-start | bytes 10616836
  137.9 28.9 %collective-permute-start.35 = (bf16[1,2,2,2,96,768]{5,4,3,2,1,0:T(8,128)(2,1)}, bf16[1,2,2,2,96,768]{5,4,3,2,1,0:T(8,128)(2,1)}, u32[]{:S(2)}, u32[]{:S(2)}) collective-permute-start(bf16[1,2,2,2,96,768]{5,4,3,2,1,0:T(8,128)(2,1)} %fusion.1), channel_id=1, source_target_pairs={{0,8},{1,9},{2,10},{3,11},{4,20},{5,21},{6,22},{7,23},{8,0},{9,1},... | collective-permute-start | bytes 3538952 | tf_op jit(solution)/shard_map/ppermute | solution.py:395
  152.3 7.8 %collective-permute-start.27 = (bf16[5,2,24,768]{3,2,0,1:T(8,128)(2,1)}, bf16[5,2,24,768]{3,2,0,1:T(8,128)(2,1)}, u32[]{:S(2)}, u32[]{:S(2)}) collective-permute-start(bf16[5,2,24,768]{3,2,0,1:T(8,128)(2,1)} %fusion.6), channel_id=1, source_target_pairs={{0,1},{1,0},{2,3},{3,2},{4,20},{5,21},{6,22},{7,23},{8,9},{9,8},{1... | collective-permute-start | bytes 1105928 | tf_op jit(solution)/shard_map/ppermute | solution.py:395
  161.5 12.3 %collective-permute-start.28 = (bf16[5,24,768]{2,1,0:T(8,128)(2,1)S(1)}, bf16[5,24,768]{2,1,0:T(8,128)(2,1)S(1)}, u32[]{:S(2)}, u32[]{:S(2)}) collective-permute-start(bf16[5,24,768]{2,1,0:T(8,128)(2,1)S(1)} %fusion.9), channel_id=1, source_target_pairs={{0,2},{1,3},{2,0},{3,1},{4,6},{5,7},{6,4},{7,5},{8,10},{9,11},{10,... | collective-permute-start | bytes 552968 | tf_op jit(solution)/shard_map/ppermute | solution.py:395
  165.3 27.0 %collective-permute-start.15 = (bf16[3,2,2,2,24,768]{5,4,0,3,2,1:T(8,128)(2,1)}, bf16[3,2,2,2,24,768]{5,4,0,3,2,1:T(8,128)(2,1)}, u32[]{:S(2)}, u32[]{:S(2)}) collective-permute-start(bf16[3,2,2,2,24,768]{5,4,0,3,2,1:T(8,128)(2,1)} %fusion.2), channel_id=1, source_target_pairs={{0,16},{1,17},{2,18},{3,19},{4,5},{5,4},{6,7},{7,6},{8,24},{9,25},... | collective-permute-start | bytes 2654216 | tf_op jit(solution)/shard_map/ppermute | solution.py:395
  169.3 18.9 %collective-permute-start.36 = (bf16[1,2,2,96,768]{4,3,2,1,0:T(8,128)(2,1)}, bf16[1,2,2,96,768]{4,3,2,1,0:T(8,128)(2,1)}, u32[]{:S(2)}, u32[]{:S(2)}) collective-permute-start(bf16[1,2,2,96,768]{4,3,2,1,0:T(8,128)(2,1)} %fusion.4), channel_id=1, source_target_pairs={{0,16},{1,17},{2,18},{3,19},{4,12},{5,13},{6,14},{7,15},{8,24},{9,... | collective-permute-start | bytes 1769480 | tf_op jit(solution)/shard_map/ppermute | solution.py:395
  176.0 11.5 %copy-start.2 = (bf16[5,1,24,768]{3,2,1,0:T(8,128)(2,1)}, bf16[5,1,24,768]{3,2,1,0:T(8,128)(2,1)S(1)}, u32[]{:S(2)}) copy-start(bf16[5,1,24,768]{3,2,1,0:T(8,128)(2,1)S(1)} %get-tuple-element.65) | copy-start | bytes 552964
  176.0 11.5 %collective-permute-start.29 = (bf16[5,1,24,768]{3,2,1,0:T(8,128)(2,1)S(1)}, bf16[5,1,24,768]{3,2,1,0:T(8,128)(2,1)S(1)}, u32[]{:S(2)}, u32[]{:S(2)}) collective-permute-start(bf16[5,1,24,768]{3,2,1,0:T(8,128)(2,1)S(1)} %get-tuple-element.65), channel_id=1, source_target_pairs={{0,2},{1,3},{2,0},{3,1},{4,6},{5,7},{6,4},{7,5},{8,10},{9,11},{10,... | collective-permute-start | bytes 552968 | tf_op jit(solution)/shard_map/ppermute | solution.py:395
  187.4 0.8 copy-start.4
  188.2 9.5 %collective-permute-start.30 = (bf16[5,2,24,768]{3,2,1,0:T(8,128)(2,1)}, bf16[5,2,24,768]{3,2,1,0:T(8,128)(2,1)}, u32[]{:S(2)}, u32[]{:S(2)}) collective-permute-start(bf16[5,2,24,768]{3,2,1,0:T(8,128)(2,1)} %pad_maximum_fusion.7), channel_id=1, source_target_pairs={{0,1},{1,0},{2,3},{3,2},{4,20},{5,21},{6,22},{7,23},{8,9},{9,8},{1... | collective-permute-start | bytes 1105928 | tf_op jit(solution)/shard_map/ppermute | solution.py:395
  190.3 12.0 %collective-permute-start.37 = (bf16[1,2,96,768]{3,2,1,0:T(8,128)(2,1)}, bf16[1,2,96,768]{3,2,1,0:T(8,128)(2,1)}, u32[]{:S(2)}, u32[]{:S(2)}) collective-permute-start(bf16[1,2,96,768]{3,2,1,0:T(8,128)(2,1)} %fusion.7), channel_id=1, source_target_pairs={{0,1},{1,0},{2,3},{3,2},{4,5},{5,4},{6,7},{7,6},{8,9},{9,8},{10,11... | collective-permute-start | bytes 884744 | tf_op jit(solution)/shard_map/ppermute | solution.py:395
  194.4 19.4 %collective-permute-start.16 = (bf16[3,2,2,24,768]{4,3,0,2,1:T(8,128)(2,1)}, bf16[3,2,2,24,768]{4,3,0,2,1:T(8,128)(2,1)}, u32[]{:S(2)}, u32[]{:S(2)}) collective-permute-start(bf16[3,2,2,24,768]{4,3,0,2,1:T(8,128)(2,1)} %fusion.5), channel_id=1, source_target_pairs={{0,8},{1,9},{2,10},{3,11},{4,20},{5,21},{6,22},{7,23},{8,0},{9,1},... | collective-permute-start | bytes 1327112 | tf_op jit(solution)/shard_map/ppermute | solution.py:395
  199.7 24.4 %collective-permute-start.31 = (bf16[5,4,24,768]{3,2,1,0:T(8,128)(2,1)}, bf16[5,4,24,768]{3,2,1,0:T(8,128)(2,1)}, u32[]{:S(2)}, u32[]{:S(2)}) collective-permute-start(bf16[5,4,24,768]{3,2,1,0:T(8,128)(2,1)} %pad_maximum_fusion.4), channel_id=1, source_target_pairs={{0,16},{1,17},{2,18},{3,19},{4,12},{5,13},{6,14},{7,15},{8,24},{9,... | collective-permute-start | bytes 2211848 | tf_op jit(solution)/shard_map/ppermute | solution.py:395
  203.7 8.1 %collective-permute-start.38 = (bf16[1,96,768]{2,1,0:T(8,128)(2,1)S(1)}, bf16[1,96,768]{2,1,0:T(8,128)(2,1)S(1)}, u32[]{:S(2)}, u32[]{:S(2)}) collective-permute-start(bf16[1,96,768]{2,1,0:T(8,128)(2,1)S(1)} %fusion.12), channel_id=1, source_target_pairs={{0,2},{1,3},{2,0},{3,1},{4,6},{5,7},{6,4},{7,5},{8,10},{9,11},{10,... | collective-permute-start | bytes 442376 | tf_op jit(solution)/shard_map/ppermute | solution.py:395
  213.8 8.6 %collective-permute-start.39 = (bf16[1,1,96,768]{3,2,1,0:T(8,128)(2,1)}, bf16[1,1,96,768]{3,2,1,0:T(8,128)(2,1)}, u32[]{:S(2)}, u32[]{:S(2)}) collective-permute-start(bf16[1,1,96,768]{3,2,1,0:T(8,128)(2,1)} %get-tuple-element.63), channel_id=1, source_target_pairs={{0,2},{1,3},{2,0},{3,1},{4,6},{5,7},{6,4},{7,5},{8,10},{9,11},{10,... | collective-permute-start | bytes 442376 | tf_op jit(solution)/shard_map/ppermute | solution.py:395
  215.7 9.9 %collective-permute-start.17 = (bf16[3,2,24,768]{3,2,0,1:T(8,128)(2,1)}, bf16[3,2,24,768]{3,2,0,1:T(8,128)(2,1)}, u32[]{:S(2)}, u32[]{:S(2)}) collective-permute-start(bf16[3,2,24,768]{3,2,0,1:T(8,128)(2,1)} %fusion.8), channel_id=1, source_target_pairs={{0,1},{1,0},{2,3},{3,2},{4,12},{5,13},{6,14},{7,15},{8,9},{9,8},{1... | collective-permute-start | bytes 663560 | tf_op jit(solution)/shard_map/ppermute | solution.py:395
  224.1 12.6 %collective-permute-start.40 = (bf16[1,2,96,768]{3,2,1,0:T(8,128)(2,1)}, bf16[1,2,96,768]{3,2,1,0:T(8,128)(2,1)}, u32[]{:S(2)}, u32[]{:S(2)}) collective-permute-start(bf16[1,2,96,768]{3,2,1,0:T(8,128)(2,1)} %pad_maximum_fusion.8), channel_id=1, source_target_pairs={{0,1},{1,0},{2,3},{3,2},{4,5},{5,4},{6,7},{7,6},{8,9},{9,8},{10,11... | collective-permute-start | bytes 884744 | tf_op jit(solution)/shard_map/ppermute | solution.py:395
  225.6 33.8 %collective-permute-start.32 = (bf16[5,8,24,768]{3,2,1,0:T(8,128)(2,1)S(1)}, bf16[5,8,24,768]{3,2,1,0:T(8,128)(2,1)S(1)}, u32[]{:S(2)}, u32[]{:S(2)}) collective-permute-start(bf16[5,8,24,768]{3,2,1,0:T(8,128)(2,1)S(1)} %pad_maximum_fusion.1), channel_id=1, source_target_pairs={{0,8},{1,9},{2,10},{3,11},{4,5},{5,4},{6,7},{7,6},{8,0},{9,1},{10,... | collective-permute-start | bytes 4423688 | tf_op jit(solution)/shard_map/ppermute | solution.py:395
  226.8 11.1 %collective-permute-start.18 = (bf16[3,24,768]{2,1,0:T(8,128)(2,1)S(1)}, bf16[3,24,768]{2,1,0:T(8,128)(2,1)S(1)}, u32[]{:S(2)}, u32[]{:S(2)}) collective-permute-start(bf16[3,24,768]{2,1,0:T(8,128)(2,1)S(1)} %fusion.15), channel_id=1, source_target_pairs={{0,2},{1,3},{2,0},{3,1},{4,6},{5,7},{6,4},{7,5},{8,10},{9,11},{10,... | collective-permute-start | bytes 331784 | tf_op jit(solution)/shard_map/ppermute | solution.py:395
  237.8 17.1 %copy-start.5 = (bf16[5,1,24,768]{3,2,1,0:T(8,128)(2,1)S(1)}, bf16[5,1,24,768]{3,2,1,0:T(8,128)(2,1)}, u32[]{:S(2)}) copy-start(bf16[5,1,24,768]{3,2,1,0:T(8,128)(2,1)} %copy-done.4) | copy-start | bytes 552964
  237.8 9.9 %collective-permute-start.41 = (bf16[1,4,96,768]{3,2,1,0:T(8,128)(2,1)S(1)}, bf16[1,4,96,768]{3,2,1,0:T(8,128)(2,1)S(1)}, u32[]{:S(2)}, u32[]{:S(2)}) collective-permute-start(bf16[1,4,96,768]{3,2,1,0:T(8,128)(2,1)S(1)} %pad_maximum_fusion.5), channel_id=1, source_target_pairs={{0,16},{1,17},{2,18},{3,19},{4,12},{5,13},{6,14},{7,15},{8,24},{9,... | collective-permute-start | bytes 1769480 | tf_op jit(solution)/shard_map/ppermute | solution.py:395
  239.7 6.6 %collective-permute-start.19 = (bf16[3,1,24,768]{3,2,1,0:T(8,128)(2,1)S(1)}, bf16[3,1,24,768]{3,2,1,0:T(8,128)(2,1)S(1)}, u32[]{:S(2)}, u32[]{:S(2)}) collective-permute-start(bf16[3,1,24,768]{3,2,1,0:T(8,128)(2,1)S(1)} %get-tuple-element.67), channel_id=1, source_target_pairs={{0,2},{1,3},{2,0},{3,1},{4,6},{5,7},{6,4},{7,5},{8,10},{9,11},{10,... | collective-permute-start | bytes 331784 | tf_op jit(solution)/shard_map/ppermute | solution.py:395
  246.3 8.4 %collective-permute-start.20 = (bf16[3,2,24,768]{3,2,1,0:T(8,128)(2,1)S(1)}, bf16[3,2,24,768]{3,2,1,0:T(8,128)(2,1)S(1)}, u32[]{:S(2)}, u32[]{:S(2)}) collective-permute-start(bf16[3,2,24,768]{3,2,1,0:T(8,128)(2,1)S(1)} %pad_maximum_fusion.9), channel_id=1, source_target_pairs={{0,1},{1,0},{2,3},{3,2},{4,12},{5,13},{6,14},{7,15},{8,9},{9,8},{1... | collective-permute-start | bytes 663560 | tf_op jit(solution)/shard_map/ppermute | solution.py:395
  248.9 30.1 %collective-permute-start.42 = (bf16[1,8,96,768]{3,2,1,0:T(8,128)(2,1)S(1)}, bf16[1,8,96,768]{3,2,1,0:T(8,128)(2,1)S(1)}, u32[]{:S(2)}, u32[]{:S(2)}) collective-permute-start(bf16[1,8,96,768]{3,2,1,0:T(8,128)(2,1)S(1)} %pad_maximum_fusion.2), channel_id=1, source_target_pairs={{0,8},{1,9},{2,10},{3,11},{4,20},{5,21},{6,22},{7,23},{8,0},{9,1},... | collective-permute-start | bytes 3538952 | tf_op jit(solution)/shard_map/ppermute | solution.py:395
  254.8 18.3 %collective-permute-start.21 = (bf16[3,4,24,768]{3,2,1,0:T(8,128)(2,1)S(1)}, bf16[3,4,24,768]{3,2,1,0:T(8,128)(2,1)S(1)}, u32[]{:S(2)}, u32[]{:S(2)}) collective-permute-start(bf16[3,4,24,768]{3,2,1,0:T(8,128)(2,1)S(1)} %pad_maximum_fusion.6), channel_id=1, source_target_pairs={{0,8},{1,9},{2,10},{3,11},{4,20},{5,21},{6,22},{7,23},{8,0},{9,1},... | collective-permute-start | bytes 1327112 | tf_op jit(solution)/shard_map/ppermute | solution.py:395
  260.6 129.0 %collective-permute-start.33 = (bf16[5,16,24,768]{3,2,1,0:T(8,128)(2,1)}, bf16[5,16,24,768]{3,2,1,0:T(8,128)(2,1)S(1)}, u32[]{:S(2)}, u32[]{:S(2)}) collective-permute-start(bf16[5,16,24,768]{3,2,1,0:T(8,128)(2,1)} %constant_dynamic-update-slice_fusion.5.refs_1_), channel_id=1, source_target_pairs={{0,4},{1,5},{2,6},{3,7},{4,0},{5,1},{6,2},{7,3},{8,12},{9,13},{10,... | collective-permute-start | bytes 8847368 | tf_op jit(solution)/shard_map/ppermute | solution.py:395
  273.1 19.4 %copy-start.13 = (bf16[768,256]{1,0:T(8,128)(2,1)S(1)}, bf16[768,256]{1,0:T(8,128)(2,1)}, u32[]{:S(2)}) copy-start(bf16[768,256]{1,0:T(8,128)(2,1)} %get-tuple-element.45) | copy-start | bytes 1179652
  273.2 21.9 %collective-permute-start.22 = (bf16[3,8,24,768]{3,2,1,0:T(8,128)(2,1)S(1)}, bf16[3,8,24,768]{3,2,1,0:T(8,128)(2,1)S(1)}, u32[]{:S(2)}, u32[]{:S(2)}) collective-permute-start(bf16[3,8,24,768]{3,2,1,0:T(8,128)(2,1)S(1)} %pad_maximum_fusion.3), channel_id=1, source_target_pairs={{0,16},{1,17},{2,18},{3,19},{4,5},{5,4},{6,7},{7,6},{8,24},{9,25},... | collective-permute-start | bytes 2654216 | tf_op jit(solution)/shard_map/ppermute | solution.py:395
  279.1 28.7 %copy-start.9 = (f32[1,3072]{1,0:T(1,128)S(1)}, f32[1,3072]{1,0:T(1,128)}, u32[]{:S(2)}) copy-start(f32[1,3072]{1,0:T(1,128)} %get-tuple-element.51) | copy-start | bytes 36868
  280.2 97.0 %collective-permute-start.43 = (bf16[1,16,96,768]{3,2,1,0:T(8,128)(2,1)}, bf16[1,16,96,768]{3,2,1,0:T(8,128)(2,1)}, u32[]{:S(2)}, u32[]{:S(2)}) collective-permute-start(bf16[1,16,96,768]{3,2,1,0:T(8,128)(2,1)} %constant_dynamic-update-slice_fusion.10.refs_1_), channel_id=1, source_target_pairs={{0,4},{1,5},{2,6},{3,7},{4,0},{5,1},{6,2},{7,3},{8,12},{9,13},{10,... | collective-permute-start | bytes 7077896 | tf_op jit(solution)/shard_map/ppermute | solution.py:395
  292.6 12.1 %collective-permute-start.6 = (bf16[768,256]{1,0:T(8,128)(2,1)S(1)}, bf16[768,256]{1,0:T(8,128)(2,1)S(1)}, u32[]{:S(2)}, u32[]{:S(2)}) collective-permute-start(bf16[768,256]{1,0:T(8,128)(2,1)S(1)} %copy-done.13), channel_id=1, source_target_pairs={{0,1},{1,0},{2,3},{3,2},{4,5},{5,4},{6,7},{7,6},{8,9},{9,8},{10,11... | collective-permute-start | bytes 1179656 | tf_op jit(solution)/shard_map/ppermute | solution.py:529
  295.0 40.0 %copy-start.8 = (f32[4,768]{1,0:T(4,128)S(1)}, f32[4,768]{1,0:T(4,128)}, u32[]{:S(2)}) copy-start(f32[4,768]{1,0:T(4,128)} %get-tuple-element.50) | copy-start | bytes 36868
  296.0 69.3 %collective-permute-start.23 = (bf16[3,16,24,768]{3,2,1,0:T(8,128)(2,1)}, bf16[3,16,24,768]{3,2,1,0:T(8,128)(2,1)}, u32[]{:S(2)}, u32[]{:S(2)}) collective-permute-start(bf16[3,16,24,768]{3,2,1,0:T(8,128)(2,1)} %constant_dynamic-update-slice_fusion.refs_1_), channel_id=1, source_target_pairs={{0,4},{1,5},{2,6},{3,7},{4,0},{5,1},{6,2},{7,3},{8,12},{9,13},{10,... | collective-permute-start | bytes 5308424 | tf_op jit(solution)/shard_map/ppermute | solution.py:395
  301.5 30.1 %collective-permute-start.7 = (bf16[768,256]{1,0:T(8,128)(2,1)}, bf16[768,256]{1,0:T(8,128)(2,1)}, u32[]{:S(2)}, u32[]{:S(2)}) collective-permute-start(bf16[768,256]{1,0:T(8,128)(2,1)} %get-tuple-element.46), channel_id=1, source_target_pairs={{0,2},{1,3},{2,0},{3,1},{4,6},{5,7},{6,4},{7,5},{8,10},{9,11},{10,... | collective-permute-start | bytes 1179656 | tf_op jit(solution)/shard_map/ppermute | solution.py:529
  304.6 26.9 %copy-start.7 = (bf16[768,256]{1,0:T(8,128)(2,1)}, bf16[768,256]{1,0:T(8,128)(2,1)S(1)}, u32[]{:S(2)}) copy-start(bf16[768,256]{1,0:T(8,128)(2,1)S(1)} %collective-permute-done.6.g1_ref) | copy-start | bytes 1179652
  304.6 26.9 %collective-permute-start.8 = (bf16[768,256]{1,0:T(8,128)(2,1)}, bf16[768,256]{1,0:T(8,128)(2,1)}, u32[]{:S(2)}, u32[]{:S(2)}) collective-permute-start(bf16[768,256]{1,0:T(8,128)(2,1)} %get-tuple-element.47), channel_id=1, source_target_pairs={{0,3},{1,2},{2,1},{3,0},{4,7},{5,6},{6,5},{7,4},{8,11},{9,10},{10,... | collective-permute-start | bytes 1179656 | tf_op jit(solution)/shard_map/ppermute | solution.py:529
  335.8 1.3 collective-permute-start.9
  337.8 5.3 %collective-permute-start.10 = (f32[14,768]{1,0:T(8,128)S(1)}, f32[14,768]{1,0:T(8,128)S(1)}, u32[]{:S(2)}, u32[]{:S(2)}) collective-permute-start(f32[14,768]{1,0:T(8,128)S(1)} %fusion.21), channel_id=1, source_target_pairs={{0,8},{4,12},{8,0},{12,4},{16,24},{20,28},{24,16},{28,20},{1,9},{5... | collective-permute-start | bytes 129032 | tf_op jit(solution)/shard_map/ppermute | solution.py:438
  343.1 4.2 %collective-permute-start.11 = (f32[14,768]{1,0:T(8,128)S(1)}, f32[14,768]{1,0:T(8,128)S(1)}, u32[]{:S(2)}, u32[]{:S(2)}) collective-permute-start(f32[14,768]{1,0:T(8,128)S(1)} %add.951), channel_id=1, source_target_pairs={{0,16},{4,20},{8,24},{12,28},{16,0},{20,4},{24,8},{28,12},{1,17},{... | collective-permute-start | bytes 129032 | tf_op jit(solution)/shard_map/ppermute | solution.py:438
  347.3 10.3 %collective-permute-start.12 = (f32[14,768]{1,0:T(8,128)S(1)}, f32[14,768]{1,0:T(8,128)S(1)}, u32[]{:S(2)}, u32[]{:S(2)}) collective-permute-start(f32[14,768]{1,0:T(8,128)S(1)} %add.952), channel_id=1, source_target_pairs={{0,1},{1,0},{2,3},{3,2},{4,5},{5,4},{6,7},{7,6},{8,9},{9,8},{10,11... | collective-permute-start | bytes 129032 | tf_op jit(solution)/shard_map/ppermute | solution.py:438
  357.6 5.0 %collective-permute-start.13 = (f32[14,768]{1,0:T(8,128)S(1)}, f32[14,768]{1,0:T(8,128)S(1)}, u32[]{:S(2)}, u32[]{:S(2)}) collective-permute-start(f32[14,768]{1,0:T(8,128)S(1)} %add.953), channel_id=1, source_target_pairs={{0,2},{1,3},{2,0},{3,1},{4,6},{5,7},{6,4},{7,5},{8,10},{9,11},{10,... | collective-permute-start | bytes 129032 | tf_op jit(solution)/shard_map/ppermute | solution.py:438
  389.6 1.6 copy-start.3

commit v2 on v1

v2 whole, which is shorter than its diff:
```python
import math

import jax
import jax.numpy as jnp
from jax import lax
from jax.experimental import pallas as pl
from jax.experimental.pallas import tpu as pltpu
from jax.sharding import PartitionSpec as P

HEADS = 12
HEAD_DIM = 64
EPS = 1e-05
BF = jnp.bfloat16
F32 = jnp.float32
VMEM_LIMIT = 56 * 1024 * 1024
HEADS_PER_STEP = 4
LIGHT = pl.CostEstimate(flops=1, bytes_accessed=1, transcendentals=0)


def dot(a, b, dims):
    return lax.dot_general(a, b, (dims, ((), ())), preferred_element_type=F32)


NN = ((1,), (0,))
NT = ((1,), (1,))
TN = ((0,), (0,))


def params(**kw):
    return pltpu.CompilerParams(vmem_limit_bytes=VMEM_LIMIT, **kw)


def unit_norm(values):
    centered = values - jnp.mean(values, axis=-1, keepdims=True)
    inverse = lax.rsqrt(jnp.mean(centered * centered, axis=-1, keepdims=True) + EPS)
    return centered * inverse, inverse


def norm_back(grad, unit, inverse, gain):
    e = grad * gain
    inner = e - jnp.mean(e, axis=-1, keepdims=True) - unit * jnp.mean(e * unit, axis=-1, keepdims=True)
    return inner * inverse


def start_flag(x_ref, rows):
    return x_ref[0, rows : rows + 1, 2 * rows : 2 * rows + 1].astype(F32)


def table(ref):
    return jnp.concatenate([ref[i] for i in range(ref.shape[0])], axis=1)


def forward_kernel(
    x_ref, shift_in_ref, gain_ref, shift_ref, w_ref, b_ref, cos_ref, sin_ref,
    q_out, k_out, v_out, p_out, o_out, first_t_out, first_ref,
):
    group = pl.program_id(0)
    rows = q_out.shape[1]

    @pl.when(group == 0)
    def _():
        x = jnp.concatenate([x_ref[i, :rows] for i in range(x_ref.shape[0])], axis=0)
        residual = x.astype(F32) + start_flag(x_ref, rows) * shift_in_ref[...]
        unit, _ = unit_norm(residual)
        first = unit * gain_ref[0:1, :] + shift_ref[0:1, :]
        first_ref[...] = first.astype(BF)
        first_t_out[...] = first.astype(BF).T

    half = HEAD_DIM // 2
    cos, sin = table(cos_ref), table(sin_ref)
    first = first_ref[...]
    query = dot(w_ref[0], first[:rows], NT) + b_ref[0]
    keys = dot(w_ref[1], first, NT) + b_ref[1]
    values = (dot(w_ref[2], first, NT) + b_ref[2]).astype(BF)
    v_out[...] = values

    def rotated(part, head, width):
        lo = part[head * HEAD_DIM : head * HEAD_DIM + half]
        hi = part[head * HEAD_DIM + half : (head + 1) * HEAD_DIM]
        c, s = cos[:, :width], sin[:, :width]
        return jnp.concatenate([lo * c - hi * s, hi * c + lo * s], axis=0)

    for head in range(HEADS_PER_STEP):
        at = slice(head * HEAD_DIM, (head + 1) * HEAD_DIM)
        q_t = (rotated(query, head, rows) * HEAD_DIM**-0.5).astype(BF)
        k_t = rotated(keys, head, first.shape[0])
        q_out[at, :] = q_t
        k_out[at, :] = k_t.astype(BF)
        scores = dot(k_t.T.astype(BF), q_t, NN)
        top = jnp.max(scores, axis=0, keepdims=True)
        weights = jnp.exp(scores - top)
        total = jnp.sum(weights, axis=0, keepdims=True)
        weights = (weights * (1.0 / total)).astype(BF)
        p_out[head] = weights
        o_out[at, :] = dot(values[at], weights, NN)


def attention_forward(x_all, start_row, gain, shift, w_t, b_cols, cos, sin):
    rows, width = cos.shape[2], x_all.shape[2]
    length = cos.shape[0] * rows
    step = HEADS_PER_STEP * HEAD_DIM
    whole = lambda shape: pl.BlockSpec(shape, lambda g: (0,) * len(shape))
    return pl.pallas_call(
        forward_kernel,
        grid=(HEADS // HEADS_PER_STEP,),
        in_specs=[
            whole(x_all.shape),
            whole((1, width)),
            whole((2, width)),
            whole((2, width)),
            pl.BlockSpec((3, step, width), lambda g: (0, g, 0)),
            pl.BlockSpec((3, step, 1), lambda g: (0, g, 0)),
            whole(cos.shape),
            whole(sin.shape),
        ],
        out_specs=[
            pl.BlockSpec((step, rows), lambda g: (g, 0)),
            pl.BlockSpec((step, length), lambda g: (g, 0)),
            pl.BlockSpec((step, length), lambda g: (g, 0)),
            pl.BlockSpec((HEADS_PER_STEP, length, rows), lambda g: (g, 0, 0)),
            pl.BlockSpec((step, rows), lambda g: (g, 0)),
            whole((width, length)),
        ],
        out_shape=[
            jax.ShapeDtypeStruct((width, rows), BF),
            jax.ShapeDtypeStruct((width, length), BF),
            jax.ShapeDtypeStruct((width, length), BF),
            jax.ShapeDtypeStruct((HEADS, length, rows), BF),
            jax.ShapeDtypeStruct((width, rows), F32),
            jax.ShapeDtypeStruct((width, length), BF),
        ],
        scratch_shapes=[pltpu.VMEM((length, width), BF)],
        compiler_params=params(),
        name="attention_forward",
        cost_estimate=LIGHT,
    )(x_all, start_row, gain, shift, w_t, b_cols, cos, sin)


def whole(shape):
    return pl.BlockSpec(shape, lambda *_: (0,) * len(shape))


def feed_chunk(second, second_t, cot, w_up, b_up, w_down):
    hidden = dot(second, w_up, NN) + b_up
    cdf = 0.5 + 0.5 * lax.erf(hidden * (0.5**0.5))
    active = (hidden * cdf).astype(BF)
    slope = cdf + hidden * (jnp.exp(-0.5 * hidden * hidden) * (1.0 / math.sqrt(2.0 * math.pi)))
    out = dot(active, w_down, NN)
    ghid = (dot(cot, w_down, NT) * slope).astype(BF)
    gsec = dot(ghid, w_up, NT)
    gdown = dot(active, cot, TN).astype(BF)
    gup = dot(second_t, ghid, NN).astype(BF)
    return out, gsec, gdown, gup, jnp.sum(ghid.astype(F32), axis=0, keepdims=True)


def store_blocks(out_ref, value, at_ref, base):
    rows = out_ref.shape[2]
    for block in range(8):
        place = block ^ (at_ref[base + 1] * 4 + at_ref[base + 2] * 2 + at_ref[base + 3])
        out_ref[0, place] = value[block * rows : (block + 1) * rows]


def feed_first_kernel(
    at_ref, o_ref, x_ref, start_ref, gain_ref, shift_ref, w_out_ref, b_out_ref, w_up_ref, b_up_ref, w_down_ref, cot_ref,
    middle_ref, second_ref, second_t_ref, acc_ref, gsec_ref, gdown_ref, gup_ref, gbup_ref,
):
    @pl.when(pl.program_id(0) == 0)
    def _():
        attended = o_ref[...].T.astype(BF)
        rows = o_ref.shape[1]
        residual = x_ref[0, :rows].astype(F32) + start_flag(x_ref, rows) * start_ref[...]
        middle = residual + dot(attended, w_out_ref[...], NN) + b_out_ref[...]
        middle_ref[...] = middle
        unit, _ = unit_norm(middle)
        second = unit * gain_ref[1:2, :] + shift_ref[1:2, :]
        second_ref[...] = second.astype(BF)
        second_t_ref[...] = second.T.astype(BF)
        acc_ref[...] = jnp.zeros_like(acc_ref)
        gsec_ref[...] = jnp.zeros_like(gsec_ref)

    out, gsec, gdown, gup, gbup_ref[0] = feed_chunk(
        second_ref[...], second_t_ref[...], cot_ref[...], w_up_ref[...], b_up_ref[...], w_down_ref[...]
    )
    store_blocks(gdown_ref, gdown, at_ref, 5)
    store_blocks(gup_ref, gup, at_ref, 5)
    acc_ref[...] += out
    gsec_ref[...] += gsec


def feed_second_kernel(
    at_ref, middle_ref, second_ref, second_t_ref, acc_in_ref, gsec_in_ref, gain_ref, w_out_ref, w_up_ref, b_up_ref,
    w_down_ref, b_down_ref, cot_ref,
    layer_ref, gmid_ref, branch_ref, do_ref, gdown_ref, gup_ref, gbup_ref, small_ref,
    acc_ref, gsec_ref,
):
    s = pl.program_id(0)

    @pl.when(s == 0)
    def _():
        acc_ref[...] = acc_in_ref[...]
        gsec_ref[...] = gsec_in_ref[...]

    out, gsec, gdown, gup, gbup_ref[0] = feed_chunk(
        second_ref[...], second_t_ref[...], cot_ref[...], w_up_ref[...], b_up_ref[...], w_down_ref[...]
    )
    store_blocks(gdown_ref, gdown, at_ref, 1)
    store_blocks(gup_ref, gup, at_ref, 1)
    acc_ref[...] += out
    gsec_ref[...] += gsec

    @pl.when(s == pl.num_programs(0) - 1)
    def _():
        cot = cot_ref[...].astype(F32)
        middle = middle_ref[...]
        unit, inverse = unit_norm(middle)
        layer_ref[...] = (middle + acc_ref[...] + b_down_ref[...]).astype(BF)
        gsec = gsec_ref[...]
        gmid = cot + norm_back(gsec, unit, inverse, gain_ref[1:2, :])
        gmid_ref[...] = gmid
        branch = gmid.astype(BF)
        branch_ref[...] = branch
        do_ref[...] = dot(w_out_ref[...], branch, NT).astype(BF)
        total = lambda v: jnp.sum(v, axis=0, keepdims=True)
        small_ref[0:1, :] = total(gsec * unit)
        small_ref[1:2, :] = total(gsec)
        small_ref[2:3, :] = total(branch.astype(F32))
        small_ref[3:4, :] = total(cot)


def feed_forward(at, o_t, x_all, start_row, gain, shift, w_out, b_out, w_up, b_up, w_down, b_down, cot):
    rows, width = cot.shape
    steps = w_up.shape[1] // width // 2
    shape = lambda *dims, kind=F32: jax.ShapeDtypeStruct(dims, kind)

    def chunk_specs(theirs):
        chunk = lambda s, at: (steps * jnp.where(theirs, 1 - at[0], at[0]) + s)
        return [
            pl.BlockSpec((width, width), lambda s, at: (0, chunk(s, at))),
            pl.BlockSpec((1, width), lambda s, at: (0, chunk(s, at))),
            pl.BlockSpec((width, width), lambda s, at: (chunk(s, at), 0)),
        ]

    def grad_specs(base):
        block = pl.BlockSpec((1, 8, width // 8, width), lambda s, at: (s ^ at[base], 0, 0, 0))
        return [
            block,
            block,
            pl.BlockSpec((1, 1, width), lambda s, at: (s, 0, 0)),
        ]

    grad_shapes = [shape(steps, 8, width // 8, width, kind=BF)] * 2 + [shape(steps, 1, width)]
    full, turned = whole((rows, width)), whole((width, rows))
    cost = LIGHT
    middle, second, second_t, acc, gsec, *theirs = pl.pallas_call(
        feed_first_kernel,
        grid_spec=pltpu.PrefetchScalarGridSpec(
            num_scalar_prefetch=1,
            grid=(steps,),
            in_specs=[
                turned, whole((1,) + x_all.shape[1:]), whole((1, width)), whole((2, width)), whole((2, width)), whole((width, width)),
                whole((1, width)), *chunk_specs(True), full,
            ],
            out_specs=[full, full, turned, full, full, *grad_specs(5)],
        ),
        out_shape=[
            shape(rows, width), shape(rows, width, kind=BF), shape(width, rows, kind=BF), shape(rows, width),
            shape(rows, width), *grad_shapes,
        ],
        compiler_params=params(),
        name="feed_first",
        cost_estimate=cost,
    )(at, o_t, x_all, start_row, gain, shift, w_out, b_out, w_up, b_up, w_down, cot)
    layer, gmid, branch, do_t, *mine, small = pl.pallas_call(
        feed_second_kernel,
        grid_spec=pltpu.PrefetchScalarGridSpec(
            num_scalar_prefetch=1,
            grid=(steps,),
            in_specs=[
                full, full, turned, full, full, whole((2, width)), whole((width, width)), *chunk_specs(False),
                whole((1, width)), full,
            ],
            out_specs=[full, full, full, turned, *grad_specs(1), whole((4, width))],
            scratch_shapes=[pltpu.VMEM((rows, width), F32), pltpu.VMEM((rows, width), F32)],
        ),
        out_shape=[
            shape(rows, width, kind=BF), shape(rows, width), shape(rows, width, kind=BF), shape(width, rows, kind=BF),
            *grad_shapes, shape(4, width),
        ],
        compiler_params=params(),
        name="feed_second",
        cost_estimate=cost,
    )(at, middle, second, second_t, acc, gsec, gain, w_out, w_up, b_up, w_down, b_down, cot)
    return layer, gmid, branch, do_t, theirs, mine, small


def backward_kernel(
    q_ref, k_ref, v_ref, p_ref, o_ref, do_ref, cos_ref, sin_ref, gq_ref, gk_ref, gv_ref, gb_ref,
):
    rows = q_ref.shape[1]
    half = HEAD_DIM // 2
    cos, sin = table(cos_ref), table(sin_ref)

    def unrotated(part, width):
        lo, hi = part[:half], part[half:]
        c, s = cos[:, :width], sin[:, :width]
        return jnp.concatenate([lo * c + hi * s, hi * c - lo * s], axis=0)

    gqs, gks, gvs = [], [], []
    for head in range(HEADS_PER_STEP):
        at = slice(head * HEAD_DIM, (head + 1) * HEAD_DIM)
        do_t = do_ref[at, :]
        weights = p_ref[head]
        gweights = dot(v_ref[at, :].T, do_t, NN)
        inner = jnp.sum(do_t.astype(F32) * o_ref[at, :], axis=0, keepdims=True)
        gscores = (weights.astype(F32) * (gweights - inner)).astype(BF)
        gq = dot(k_ref[at, :], gscores, NN) * HEAD_DIM**-0.5
        gk = dot(gscores, q_ref[at, :].T, NN)
        gvs.append(dot(weights, do_t.T, NN).astype(BF))
        gqs.append(unrotated(gq, rows).astype(BF))
        gks.append(unrotated(gk.T, gk.shape[0]).astype(BF))
    gq_ref[...] = jnp.concatenate(gqs, axis=0).T
    gk_ref[...] = jnp.concatenate(gks, axis=0).T
    gv_ref[...] = jnp.concatenate(gvs, axis=1)
    ones = jnp.ones((8, gk_ref.shape[0]), BF)
    gb_ref[0] = dot(ones[:, :rows], gq_ref[...], NN)
    gb_ref[1] = dot(ones, gk_ref[...], NN)
    gb_ref[2] = dot(ones, gv_ref[...], NN)


def attention_backward(q_t, k_t, v_t, p_t, o_t, do_t, cos, sin):
    width, rows = q_t.shape
    length = k_t.shape[1]
    step = HEADS_PER_STEP * HEAD_DIM
    narrow, wide = pl.BlockSpec((step, rows), lambda g: (g, 0)), pl.BlockSpec((step, length), lambda g: (g, 0))
    return pl.pallas_call(
        backward_kernel,
        grid=(HEADS // HEADS_PER_STEP,),
        in_specs=[
            narrow, wide, wide, pl.BlockSpec((HEADS_PER_STEP, length, rows), lambda g: (g, 0, 0)), narrow, narrow,
            whole(cos.shape), whole(sin.shape),
        ],
        out_specs=[pl.BlockSpec((n, step), lambda g: (0, g)) for n in (rows, length, length)]
        + [pl.BlockSpec((3, 8, step), lambda g: (0, 0, g))],
        out_shape=[
            jax.ShapeDtypeStruct((rows, width), BF),
            jax.ShapeDtypeStruct((length, width), BF),
            jax.ShapeDtypeStruct((length, width), BF),
            jax.ShapeDtypeStruct((3, 8, width), F32),
        ],
        compiler_params=params(),
        name="attention_backward",
        cost_estimate=LIGHT,
    )(q_t, k_t, v_t, p_t, o_t, do_t, cos, sin)


def head_grads(store, side, base, at_ref, gq_ref, gk_ref, gv_ref, first_t_ref, o_ref, branch_ref):
    rows = gq_ref.shape[0]
    part = first_t_ref.shape[0] // 2
    size = part // 4
    group = at_ref[base] * 2 + at_ref[base + 1]
    mat = at_ref[base + 2] * 2 + at_ref[base + 3]
    at = [pl.ds(pl.multiple_of(side * part + (place ^ group) * size, 32), size) for place in range(4)]
    first_t = jnp.concatenate([first_t_ref[where, :] for where in at], axis=0)
    attended = jnp.concatenate([o_ref[where, :] for where in at], axis=0).astype(BF)
    grads = (
        dot(first_t[:, :rows], gq_ref[...], NN),
        dot(first_t, gk_ref[...], NN),
        dot(first_t, gv_ref[...], NN),
        dot(attended, branch_ref[...], NN),
    )
    for i, grad in enumerate(grads):
        for place in range(4):
            store(place, i ^ mat, grad[place * size : (place + 1) * size].astype(BF))


def heads_first_kernel(at_ref, gq_ref, gk_ref, gv_ref, first_t_ref, o_ref, branch_ref, *outs):
    def store(place, mat, value):
        outs[place][mat] = value

    head_grads(store, 1 - at_ref[0], 5, at_ref, gq_ref, gk_ref, gv_ref, first_t_ref, o_ref, branch_ref)


def heads_second_kernel(
    at_ref, gq_ref, gk_ref, gv_ref, first_t_ref, o_ref, branch_ref, w_ref,
    mine_ref, gx_own, gx_near, gx_core, acc_ref,
):
    group = pl.program_id(0)
    rows = gq_ref.shape[0]
    back = dot(gk_ref[...], w_ref[1], NN) + dot(gv_ref[...], w_ref[2], NN)
    own = dot(gq_ref[...], w_ref[0], NN)

    @pl.when(group == 0)
    def _():
        acc_ref[...] = back

    @pl.when(group > 0)
    def _():
        acc_ref[...] += back

    acc_ref[:rows] += own

    def store(place, mat, value):
        mine_ref[place, mat] = value

    head_grads(store, at_ref[0], 1, at_ref, gq_ref, gk_ref, gv_ref, first_t_ref, o_ref, branch_ref)

    @pl.when(group == pl.num_programs(0) - 1)
    def _():
        gx_own[...] = acc_ref[:rows]
        gx_near[...] = acc_ref[rows : 2 * rows]
        gx_core[...] = acc_ref[2 * rows :].astype(BF)


def heads_specs(rows, width, length):
    step = HEADS_PER_STEP * HEAD_DIM
    column = lambda n: pl.BlockSpec((n, step), lambda g, at: (0, g))
    ins = [column(rows), column(length), column(length), whole((width, length)), whole((width, rows)), column(rows)]
    grad = pl.BlockSpec((4, 4, width // 8, step), lambda g, at: (0, 0, 0, g))
    return ins, grad, jax.ShapeDtypeStruct((4, 4, width // 8, width), BF)


def heads_first(at, gq, gk, gv, first_t, o_t, branch):
    rows, width = gq.shape
    ins, _, _ = heads_specs(rows, width, gk.shape[0])
    piece = pl.BlockSpec((4, width // 8, HEADS_PER_STEP * HEAD_DIM), lambda g, at: (0, 0, g))
    return pl.pallas_call(
        heads_first_kernel,
        grid_spec=pltpu.PrefetchScalarGridSpec(
            num_scalar_prefetch=1, grid=(HEADS // HEADS_PER_STEP,), in_specs=ins, out_specs=[piece] * 4
        ),
        out_shape=[jax.ShapeDtypeStruct((4, width // 8, width), BF)] * 4,
        compiler_params=params(),
        name="heads_first",
        cost_estimate=LIGHT,
    )(at, gq, gk, gv, first_t, o_t, branch)


def heads_second(at, gq, gk, gv, first_t, o_t, branch, w_t):
    rows, width = gq.shape
    ins, grad, shape = heads_specs(rows, width, gk.shape[0])
    step = HEADS_PER_STEP * HEAD_DIM
    piece = lambda kind, n: jax.ShapeDtypeStruct((n * rows, width), kind)
    return pl.pallas_call(
        heads_second_kernel,
        grid_spec=pltpu.PrefetchScalarGridSpec(
            num_scalar_prefetch=1,
            grid=(HEADS // HEADS_PER_STEP,),
            in_specs=ins + [pl.BlockSpec((3, step, width), lambda g, at: (0, g, 0))],
            out_specs=[grad, whole((rows, width)), whole((rows, width)), whole((2 * rows, width))],
            scratch_shapes=[pltpu.VMEM((gk.shape[0], width), F32)],
        ),
        out_shape=[shape, piece(F32, 1), piece(F32, 1), piece(BF, 2)],
        compiler_params=params(),
        name="heads_second",
        cost_estimate=LIGHT,
    )(at, gq, gk, gv, first_t, o_t, branch, w_t)


def entry_kernel(own_ref, core_ref, near_ref, x_ref, start_ref, gain_ref, gmid_ref, gtok_ref, small_ref):
    rows = own_ref.shape[0]
    grad = own_ref[...] + core_ref[:rows].astype(F32) + near_ref[...].astype(F32)
    flag = start_flag(x_ref, rows)
    unit, inverse = unit_norm(x_ref[0, :rows].astype(F32) + flag * start_ref[...])
    gres = gmid_ref[...] + norm_back(grad, unit, inverse, gain_ref[0:1, :])
    gtok_ref[...] = gres.astype(BF)
    small_ref[0:1, :] = jnp.sum(grad * unit, axis=0, keepdims=True)
    small_ref[1:2, :] = jnp.sum(grad, axis=0, keepdims=True)
    small_ref[2:3, :] = jnp.sum(gres, axis=0, keepdims=True) * flag


def entry_backward(pieces, x_all, start_row, gain, gmid):
    rows, width = gmid.shape
    ins = [*pieces, x_all, start_row, gain, gmid]
    specs = [whole(a.shape) for a in ins]
    specs[len(pieces)] = whole((1,) + x_all.shape[1:])
    return pl.pallas_call(
        entry_kernel,
        grid=(1,),
        in_specs=specs,
        out_specs=[whole((rows, width)), whole((3, width))],
        out_shape=[jax.ShapeDtypeStruct((rows, width), BF), jax.ShapeDtypeStruct((3, width), F32)],
        compiler_params=params(),
        name="entry_backward",
        cost_estimate=LIGHT,
    )(*ins)


BITS = {"c": ("dp", 1), "x": ("dp", 2), "y": ("dp", 4), "z": ("seq", 1), "w": ("seq", 2)}
ORDER = ("xywz", "yxwz")
LEVELS = {"a": "xy", "b": "yx", "w": "ww", "z": "zz"}


def my_bit(name):
    axis, mask = BITS[name]
    return (lax.axis_index(axis) // mask) % 2


def xor_pairs(size, mask):
    return [(i, i ^ mask) for i in range(size)]


def swap(value, names):
    dp, seq = lax.axis_size("dp"), lax.axis_size("seq")
    pairs = []
    for d in range(dp):
        axis, mask = BITS[names[d % 2]]
        for s in range(seq):
            to = (d ^ mask) * seq + s if axis == "dp" else d * seq + (s ^ mask)
            pairs.append((d * seq + s, to))
    return lax.ppermute(value, ("dp", "seq"), pairs)


def swap_seq(value, mask):
    return lax.ppermute(value, "seq", xor_pairs(lax.axis_size("seq"), mask))


def numbers():
    core = my_bit("c")
    first, second = ([my_bit(name) for name in order] for order in ORDER)
    pick = lambda a, b: jnp.where(core == 0, a, b)
    bits = [pick(a, b) for a, b in zip(first, second)] + [pick(b, a) for a, b in zip(first, second)]
    return jnp.stack([core] + bits).astype(jnp.int32)


class Chain:
    def __init__(self, last):
        self.last = last

    def then(self, step, *args):
        args, _ = lax.optimization_barrier((args, self.last))
        self.last = step(*args)
        return self.last


def add_up(parts):
    return sum(p.astype(F32) for p in parts).astype(BF)


class Part:
    def __init__(self, value, bits):
        self.value, self.bits = value, bits

    def take(self, value, sides):
        if isinstance(value, tuple):
            size = 2 if self.bits[1] in sides else 1
            first = 2 * sides[self.bits[0]] + sides.get(self.bits[1], 0)
            picked = value[first : first + 1] if size == 2 else value[first : first + 2]
            rest = {bit: side for bit, side in sides.items() if bit not in self.bits[:2]}
            inner = [Part(v, self.bits[2:]).take(v, rest) for v in picked]
            return inner[0] if size == 2 else jnp.stack(inner)
        index = tuple(sides[bit] if bit in sides else slice(None) for bit in self.bits)
        return value.reshape((2,) * len(self.bits) + value.shape[-2:])[index]


class Chunk:
    def __init__(self, theirs, received, mine):
        rows, width = mine.shape[-2:]
        blocks = lambda a: a if isinstance(a, tuple) else a.reshape((16, rows, width))
        self.parts = [Part(blocks(mine), "abwz"), Part(blocks(received), "abwz")]
        self.done = {}

    def step(self, chain, choices):
        parts, done = list(self.parts), dict(self.done)

        def sums(*values):
            out = []
            for choice in choices:
                sides = {**done, **choice}
                taken = [
                    part.take(v, {bit: side for bit, side in sides.items() if bit in part.bits})
                    for part, v in zip(parts, values)
                ]
                out.append(add_up(taken))
            return tuple(out)

        return chain.then(sums, *(part.value for part in parts))

    def halve(self, chain, bit):
        (send,) = self.step(chain, [{bit: 1}])
        self.done[bit] = 0
        left = "".join(b for b in "abwz" if b not in self.done)
        self.parts.append(Part(swap(send, LEVELS[bit]), left))

    def quarter(self, chain):
        seq = lax.axis_size("seq")
        sends = self.step(chain, [{"w": k // 2, "z": k % 2} for k in range(1, seq)])
        self.done.update(w=0, z=0)
        left = "".join(b for b in "abwz" if b not in self.done)
        self.parts += [Part(swap_seq(send, k + 1), left) for k, send in enumerate(sends)]

    def finish(self, chain):
        (held,) = self.step(chain, [{}])
        held = held[None]
        dp = lax.axis_size("dp")
        for k in range(3, dp.bit_length() - 1):
            other = lax.ppermute(held, "dp", xor_pairs(dp, 1 << k))
            held = chain.then(lambda a, b: add_up([a, b]), held, other)
        return held


class Gather:
    def __init__(self, chain, shards):
        self.held = shards[0][None] if len(shards) == 1 else chain.then(lambda *a: jnp.stack(a), *shards)
        self.received = [swap_seq(self.held, k) for k in range(1, lax.axis_size("seq"))]
        self.levels = ["a", "b"]

    def double(self, chain):
        self.held = chain.then(lambda *parts: jnp.concatenate(parts, axis=1), self.held, *self.received)
        self.received = [swap(self.held, LEVELS[self.levels.pop()])]
        if not self.levels:
            self.others = [swap(self.held, "cc")]

    def cross(self, chain):
        received, _ = lax.optimization_barrier((self.received[0], chain.last))
        chain.last = received
        self.others.append(swap(received, "cc"))

    def spread(self, chain, kind, i):
        ins = [self.held, self.received[0], *self.others]
        at = numbers()
        return chain.then(lambda *ins: spread(kind, i, at, list(ins)), *ins)


def sum_small(chain, value, axis, masks):
    size = lax.axis_size(axis)
    parts = [lax.ppermute(value, axis, xor_pairs(size, mask)) for mask in masks]
    return chain.then(lambda *parts: sum(parts), value, *parts)


def spread_kernel(kind, at_ref, *refs):
    ins, outs = refs[:4], refs[4:]
    core = at_ref[0]
    for half in range(2):
        side = core if half == 0 else 1 - core
        b3, b2, b1, b0 = (at_ref[1 + 4 * half + i] for i in range(4))
        for top in range(2):
            src = ins[2 * half + top]
            hi = b3 if top == 0 else 1 - b3
            if kind == "heads":
                for i in range(4):
                    outs[2][side, hi, i ^ (b1 * 2 + b0)] = src[0, i].astype(F32)
                continue
            for i in range(2):
                if kind == "down":
                    outs[0][side, hi, 0, i ^ b0] = src[0, i].astype(F32)
                else:
                    width = src.shape[-1]
                    col = pl.multiple_of((side * 2 + hi) * width, width)
                    outs[0][0, i ^ b0, :, pl.ds(col, width)] = src[0, i].astype(F32)
    if kind == "heads":
        w_qkv, w_out, natural = outs
        for side in range(2):
            for hi in range(2):
                w_out[side, hi, 0] = natural[side, hi, 3]
                q, k, v = (natural[side, hi, i] for i in range(3))
                cuts = [slice(h * HEAD_DIM, (h + 1) * HEAD_DIM) for h in range(q.shape[1] // HEAD_DIM)]
                w_qkv[side, hi, 0] = jnp.concatenate([m[:, cut] for cut in cuts for m in (q, k, v)], axis=1)


def spread(kind, which, at, ins):
    n, _, rows, width = ins[0].shape
    scratch, grid = [], (4,)
    if kind == "heads":
        ins = [a.reshape(n, 2, 4, rows, width) for a in ins]
        grid = (2, 2)
        part = width // 2
        spec = lambda base: pl.BlockSpec(
            (None, 1, 4, rows, part), lambda p, c, at: (which, p ^ at[base + 1], 0, 0, c)
        )
        outs = [(2, 2, 2, rows, 3 * width), (2, 2, 2, rows, width)]
        blocks = [pl.BlockSpec((2, 2, 1, rows, o[4] // 2), lambda p, c, at: (0, 0, p, 0, c)) for o in outs]
        scratch = [pltpu.VMEM((2, 2, 4, rows, part), F32)]
    else:
        ins = [a.reshape(n, 4, 2, rows, width) for a in ins]
        low = lambda base, p, at: p ^ (at[base + 1] * 2 + at[base + 2])
        spec = lambda base: pl.BlockSpec((None, 1, 2, rows, width), lambda p, at: (which, low(base, p, at), 0, 0, 0))
        if kind == "down":
            outs = [(2, 2, 4, 2, rows, width)]
            blocks = [pl.BlockSpec((2, 2, 1, 2, rows, width), lambda p, at: (0, 0, p, 0, 0, 0))]
        else:
            outs = [(4, 2, rows, 4 * width)]
            blocks = [pl.BlockSpec((1, 2, rows, 4 * width), lambda p, at: (p, 0, 0, 0))]
    made = pl.pallas_call(
        lambda *refs: spread_kernel(kind, *refs),
        grid_spec=pltpu.PrefetchScalarGridSpec(
            num_scalar_prefetch=1,
            grid=grid,
            in_specs=[spec(1), spec(1), spec(5), spec(5)],
            out_specs=blocks,
            scratch_shapes=scratch,
        ),
        out_shape=[jax.ShapeDtypeStruct(o, F32) for o in outs],
        compiler_params=params(),
        name="spread_" + kind,
        cost_estimate=LIGHT,
    )(at, *ins)
    return [m.reshape(-1, m.shape[-1]) for m in made]


class Homes:
    def __init__(self):
        self.dp, self.seq = lax.axis_size("dp"), lax.axis_size("seq")
        self.native = (lax.axis_index("seq") // 2) % 2 == my_bit("c")

    def pairs(self, native_step, foreign_step):
        out = []
        for d in range(self.dp):
            for z in range(self.seq):
                step = native_step if z // 2 % 2 == d % 2 else foreign_step
                if step is not None:
                    swap_core, mask = step
                    out.append((d * self.seq + z, (d ^ swap_core) * self.seq + (z ^ mask)))
        return out

    def move(self, value, native_step, foreign_step):
        return lax.ppermute(value, ("dp", "seq"), self.pairs(native_step, foreign_step))

    def settle(self, value):
        return jnp.where(self.native, value, self.move(value, None, (1, 2)))

    def gather(self, tokens, positions, flag, meanwhile):
        rows, width = tokens.shape
        digits = jnp.concatenate([positions // 64, positions % 64, flag]).astype(BF)
        extra = jnp.pad(digits, (0, width - digits.shape[0]))
        value = jnp.concatenate([tokens, jnp.broadcast_to(extra, (8, width))])
        far = self.move(value, None, (1, 3))
        near = self.move(value, (0, 1), (1, 2))
        (near, far), meanwhile = lax.optimization_barrier(((near, far), meanwhile))
        two = jnp.stack([jnp.where(self.native, value, near), jnp.where(self.native, near, far)])
        four = jnp.concatenate([two, swap(two, "cc")])
        return four, meanwhile


def per_device(
    tokens, codon_positions, start_flags, start_embed, norm_gain, norm_shift, w_qkv, b_qkv,
    w_out, b_out, w_up, b_up, w_down, b_down, cotangent,
):
    width = tokens.shape[-1]
    core = my_bit("c").astype(jnp.int32)
    at = numbers()
    homes = Homes()
    by_head = w_qkv.reshape(width, HEADS, 3, HEAD_DIM)
    w_t = by_head.transpose(2, 1, 3, 0).reshape(3, width, width)
    b_cols = b_qkv.reshape(HEADS, 3, HEAD_DIM).transpose(1, 0, 2).reshape(3, width, 1)
    rows = tokens.shape[1]
    x_all, (w_t, b_cols) = homes.gather(tokens[0], codon_positions[0], start_flags, (w_t, b_cols))
    cot_moved = homes.move(cotangent[0], None, (1, 2))
    half = HEAD_DIM // 2
    frequency = 10000.0 ** (-2.0 * jnp.arange(half, dtype=F32) / HEAD_DIM)
    digits = x_all[:, rows, : 2 * rows].astype(F32)
    angles = frequency[None, :, None] * (digits[:, :rows] * 64 + digits[:, rows:])[:, None, :]
    cos, sin = jnp.cos(angles), jnp.sin(angles)
    start_row = start_embed[None]
    q_t, k_t, v_t, p_t, o_t, first_t = attention_forward(x_all, start_row, norm_gain, norm_shift, w_t, b_cols, cos, sin)
    cot_moved, _ = lax.optimization_barrier((cot_moved, o_t))
    cot = jnp.where(homes.native, cotangent[0], cot_moved)
    layer_out, gmid, branch, do_t, theirs, mine, small_feed = feed_forward(
        at, o_t, x_all, start_row, norm_gain, norm_shift, w_out, b_out[None], w_up, b_up[None], w_down,
        b_down[None], cot,
    )
    chain = Chain(do_t)
    down = Chunk(theirs[0], swap(theirs[0], "cc"), mine[0])
    up = Chunk(theirs[1], swap(theirs[1], "cc"), mine[1])
    down.halve(chain, "a")
    up.halve(chain, "z")
    gq, gk, gv, gbqkv = chain.then(attention_backward, q_t, k_t, v_t, p_t, o_t, do_t, cos, sin)
    down.halve(chain, "b")
    head_inputs = (gq, gk, gv, first_t, o_t, branch)
    head_theirs = chain.then(lambda *args: heads_first(at, *args), *head_inputs)
    head_received = tuple(swap(piece, "cc") for piece in head_theirs)
    down.quarter(chain)
    head_mine, gx_own, gx_near, gx_core = chain.then(lambda *args: heads_second(at, *args), *head_inputs, w_t)
    heads = Chunk(None, head_received, head_mine)
    gx_core = swap(gx_core, "cc")
    heads.halve(chain, "a")
    gx_near = chain.then(lambda a, b: (a + b[rows:].astype(F32)).astype(BF), gx_near, gx_core)
    gx_near = swap(gx_near, "zz")
    up.halve(chain, "a")
    down_sum = down.finish(chain)
    layer_moved = homes.move(layer_out, None, (1, 2))
    heads.halve(chain, "b")
    up.halve(chain, "b")
    grad_tokens, small_entry = chain.then(
        lambda *args: entry_backward(args[:3], *args[3:]), gx_own, gx_core, gx_near, x_all, start_row, norm_gain, gmid
    )
    tokens_moved = homes.move(grad_tokens, None, (1, 2))
    hidden_bias = [jnp.concatenate([a[2][:, 0], b[2][:, 0]]) for a, b in ((mine, theirs), (theirs, mine))]
    smalls = jnp.concatenate(
        [small_feed, jnp.where(core == 0, hidden_bias[0], hidden_bias[1]), gbqkv[:, 0], small_entry]
    )
    smalls = sum_small(chain, smalls, "dp", [1])
    heads.quarter(chain)
    up.halve(chain, "w")
    smalls = sum_small(chain, smalls, "dp", [2, 4, 6])
    for k in range(3, lax.axis_size("dp").bit_length() - 1):
        smalls = sum_small(chain, smalls, "dp", [1 << k])
    up_sum = up.finish(chain)
    feed = Gather(chain, [down_sum, up_sum])
    heads = Gather(chain, [heads.finish(chain)])
    smalls = sum_small(chain, smalls, "seq", [1, 2, 3])
    feed.double(chain)
    heads.double(chain)
    feed.double(chain)
    heads.double(chain)

    def settled(smalls, layer, tokens):
        gain_1, shift_1, grad_bout, grad_bdown = smalls[:4]
        grad_bqkv = smalls[-6:-3].reshape(3, HEADS, HEAD_DIM).transpose(1, 0, 2).reshape(-1)
        gain_0, shift_0, grad_start = smalls[-3:]
        return (
            jnp.where(homes.native, layer_out, layer)[None],
            jnp.where(homes.native, grad_tokens, tokens)[None],
            grad_start,
            jnp.stack([gain_0, gain_1]),
            jnp.stack([shift_0, shift_1]),
            grad_bqkv,
            grad_bout,
            smalls[4:-6].reshape(-1),
            grad_bdown,
        )

    small_outs = chain.then(settled, smalls, layer_moved, tokens_moved)
    feed.cross(chain)
    (grad_down,) = feed.spread(chain, "down", 0)
    (grad_up,) = feed.spread(chain, "up", 1)
    heads.cross(chain)
    grad_qkv, grad_wout = heads.spread(chain, "heads", 0)
    layer, tokens_grad, grad_start, grad_gain, grad_shift, grad_bqkv, grad_bout, grad_bup, grad_bdown = small_outs
    return (
        layer, tokens_grad, grad_start, grad_gain, grad_shift, grad_qkv, grad_bqkv, grad_wout, grad_bout, grad_up,
        grad_bup, grad_down, grad_bdown,
    )


def solution(mesh):
    rows = P("dp", "seq", None)
    return jax.shard_map(
        per_device,
        mesh=mesh,
        in_specs=(rows, P("dp", "seq"), P("dp")) + (P(),) * 11 + (rows,),
        out_specs=(rows, rows) + (P(),) * 11,
        check_vma=False,
    )
```

time: 407 us -> 313 us (0.77)
  waiting for transfers between devices: 118 us -> 86.2 us
  local copies, waits for them, and re-layouts: 49.4 us -> 24.7 us
  other arithmetic: 50.7 us -> 29.8 us
  starting transfers between devices: 88.1 us -> 70.8 us
    pallas_call x2 -> x5, Pallas kernels: 19.6 us -> 44.9 us  [the longest x1 12 us: feed_forward(): pl.pallas_call(feed_second_kernel, grid_spec=pltpu.PrefetchScalarGridSpec...]
    ppermute x30 -> x25, waiting for transfers between devices: 70 us -> 51.8 us  [swap(): return lax.ppermute(value, ('dp', 'seq'), pairs)]
    pallas_call x3, Pallas kernels: 37.6 us -> 21.8 us  [spread(): pl.pallas_call(lambda *refs: spread_kernel(kind, *refs), grid_spec=pltpu....]
    ppermute x14 -> x24, waiting for transfers between devices: 48.2 us -> 34.4 us  [the longest x12 31.6 us: swap_seq(): return lax.ppermute(value, 'seq', xor_pairs(lax.axis_size('seq'), mask))]
    ppermute x30 -> x25, starting transfers between devices: 51.2 us -> 37.8 us  [swap(): return lax.ppermute(value, ('dp', 'seq'), pairs)]
    concatenate x11 -> x4, other arithmetic: 11.8 us -> 2.67 us  [the longest x1 1.77 us: gather(): value = jnp.concatenate([tokens, jnp.broadcast_to(extra, (8, width))])]
    unnamed x39 -> x69, local copies, waits for them, and re-layouts: 17 us -> 8.52 us
    squeeze x3 -> x0, local copies, waits for them, and re-layouts: 8.26 us -> none  [pick(): return lax.dynamic_index_in_dim(array, index, 1, keepdims=False)]
  transfers between devices with their start and end apart: 44 -> 49, of which waited for: 20 -> 15; matrix products, arithmetic and copies ran while one was open for 23% -> 14% of each run, Pallas kernels for 12% -> 26%
where the time goes in v2:
time: 313 us; the launch traced here: 312 us
  Pallas kernels  98.3 us (31%)
  waiting for transfers between devices  86.2 us (28%)
  starting transfers between devices  70.8 us (23%)
  other arithmetic  29.8 us (10%)
  local copies, waits for them, and re-layouts  24.7 us (8%)
    ppermute x25, waiting for transfers between devices, swap(): return lax.ppermute(value, ('dp', 'seq'), pairs)  51.8 us
    ppermute x25, starting transfers between devices, swap(): return lax.ppermute(value, ('dp', 'seq'), pairs)  37.8 us
    ppermute x12, waiting for transfers between devices, swap_seq(): return lax.ppermute(value, 'seq', xor_pairs(lax.axis_size('seq'), mask))  31.6 us
    pallas_call x3, Pallas kernels, spread(): pl.pallas_call(lambda *refs: spread_kernel(kind, *refs), grid_spec=pltpu....  21.8 us
    ppermute x12, starting transfers between devices, swap_seq(): return lax.ppermute(value, 'seq', xor_pairs(lax.axis_size('seq'), mask))  20.8 us
    convert_element_type x13, other arithmetic, add_up(): return sum((p.astype(F32) for p in parts)).astype(BF)  20.1 us
    pallas_call x1, Pallas kernels, attention_forward(): pl.pallas_call(forward_kernel, grid=(HEADS // HEADS_PER_STEP,), in_specs=...  17.7 us
    pallas_call x1, Pallas kernels, attention_backward(): pl.pallas_call(backward_kernel, grid=(HEADS // HEADS_PER_STEP,), in_specs...  13.8 us
  transfers between devices with their start and end apart: 49, of which 15 were waited for; matrix products, arithmetic and copies ran while one was open for 14% of the time, Pallas kernels for 26%

profile of v2, /device:TPU:0, one launch (start us, length us, event | category | flops | bytes accessed | tf_op | source)
XLA Modules:
  0.0 311.8 jit_solution(8619166604336576708)
XLA Ops:
  2.0 1.8 pad_maximum_fusion.2
  3.8 3.0 collective-permute-start
  6.8 1.4 collective-permute-start.1
  8.2 4.5 %copy.29 = bf16[768,2304]{0,1:T(8,128)(2,1)S(1)} copy(bf16[768,2304]{1,0:T(8,128)(2,1)} %param.21) | data formatting | bytes 7077888 | tf_op args[6]
  12.8 2.0 copy.30
  15.7 1.6 collective-permute-done
  17.2 1.3 select_bitcast_fusion.1
  18.6 5.9 %collective-permute-start.2 = (bf16[2,264,768]{2,1,0:T(8,128)(2,1)S(1)}, bf16[2,264,768]{2,1,0:T(8,128)(2,1)S(1)}, u32[]{:S(2)}, u32[]{:S(2)}) collective-permute-start(bf16[2,264,768]{2,1,0:T(8,128)(2,1)S(1)} %pad_maximum_fusion.1), channel_id=1, source_target_pairs={{0,4},{1,5},{2,6},{3,7},{4,0},{5,1},{6,2},{7,3},{8,12},{9,13},{10,... | collective-permute-start | bytes 2433032 | tf_op jit(solution)/shard_map/ppermute | solution.py:510
  27.1 1.4 copy.32.b_ref
  28.8 1.2 multiply_sine_fusion
  30.0 17.7 %attention_forward.1 = (bf16[768,256]{1,0:T(8,128)(2,1)}, bf16[768,1024]{1,0:T(8,128)(2,1)}, bf16[768,1024]{1,0:T(8,128)(2,1)}, bf16[12,1024,256]{2,1,0:T(8,128)...) custom-call(bf16[4,264,768]{2,1,0:T(8,128)(2,1)} %copy-done, f32[1,768]{1,0:T(1,128)} %broadcast_in_dim.30.shift_in_ref.start_ref, ...), custom_call_target="tpu_custom_call" | custom-call | flops 1 | bytes 1 | tf_op jit(solution)/shard_map/attention_forward/pallas_call | solution.py:103
  48.5 11.0 %feed_first.1 = (f32[256,768]{1,0:T(8,128)}, bf16[256,768]{1,0:T(8,128)(2,1)}, bf16[768,256]{1,0:T(8,128)(2,1)}, f32[256,768]{1,0:T(8,128)}, f32[256,768]{1,0:T(...) custom-call(s32[9]{0:T(128)} %stack.35.at_ref.refs_0_, ...), custom_call_target="tpu_custom_call" | custom-call | flops 1 | bytes 1 | tf_op jit(solution)/shard_map/feed_first/pallas_call | solution.py:254
  59.5 8.7 %collective-permute-start.5 = (bf16[2,8,96,768]{3,2,1,0:T(8,128)(2,1)}, bf16[2,8,96,768]{3,2,1,0:T(8,128)(2,1)S(1)}, u32[]{:S(2)}, u32[]{:S(2)}) collective-permute-start(bf16[2,8,96,768]{3,2,1,0:T(8,128)(2,1)} %get-tuple-element.203), channel_id=1, source_target_pairs={{0,4},{1,5},{2,6},{3,7},{4,0},{5,1},{6,2},{7,3},{8,12},{9,13},{10,... | collective-permute-start | bytes 7077896 | tf_op jit(solution)/shard_map/ppermute | solution.py:510
  68.9 12.0 %feed_second.1 = (bf16[256,768]{1,0:T(8,128)(2,1)}, f32[256,768]{1,0:T(8,128)}, bf16[256,768]{1,0:T(8,128)(2,1)}, bf16[768,256]{1,0:T(8,128)(2,1)}, bf16[2,8,96,...) custom-call(s32[9]{0:T(128)} %stack.35.at_ref.refs_0_, ...), custom_call_target="tpu_custom_call" | custom-call | flops 1 | bytes 1 | tf_op jit(solution)/shard_map/feed_second/pallas_call | solution.py:273
  80.9 2.7 add_convert_fusion.1
  83.6 1.4 collective-permute-start.6
  85.3 13.8 %attention_backward.1 = (bf16[256,768]{1,0:T(8,128)(2,1)}, bf16[1024,768]{1,0:T(8,128)(2,1)}, bf16[1024,768]{1,0:T(8,128)(2,1)}, f32[3,8,768]{2,1,0:T(8,128)}) custom-call(bf16[768,256]{1,0:T(8,128)(2,1)} %get-tuple-element.208.q_ref, bf16[768,1024]{1,0:T(8,128)(2,1)} %get-tuple-element.209.k_ref, bf16[768,1024]{1,0:T(8,128)(2,1)} %get-tuple-element.210.v_ref, ...), custom_call_target="tpu_custom_call" | custom-call | flops 1 | bytes 1 | tf_op jit(solution)/shard_map/attention_backward/pallas_call | solution.py:335
  100.1 2.3 fusion.4
  102.4 1.5 collective-permute-start.7
  103.9 6.6 %heads_first.1 = (bf16[4,96,768]{2,1,0:T(8,128)(2,1)}, bf16[4,96,768]{2,1,0:T(8,128)(2,1)}, bf16[4,96,768]{2,1,0:T(8,128)(2,1)}, bf16[4,96,768]{2,1,0:T(8,128)(2,1)}) custom-call(s32[9]{0:T(128)} %stack.35.at_ref.refs_0_, bf16[256,768]{1,0:T(8,128)(2,1)} %get-tuple-element.239.gq_ref, bf16[1024,768]{1,0:T(8,128)(2,1)} %get-tuple-element.240.gk_ref, ...), custom_call_target="tpu_custom_call" | custom-call | flops 1 | bytes 1 | tf_op jit(solution)/shard_map/heads_first/pallas_call | solution.py:426
  112.6 2.3 fusion.20
  114.9 11.9 %heads_second.1 = (bf16[4,4,96,768]{3,2,1,0:T(8,128)(2,1)}, f32[256,768]{1,0:T(8,128)}, f32[256,768]{1,0:T(8,128)}, bf16[512,768]{1,0:T(8,128)(2,1)}) custom-call(s32[9]{0:T(128)} %stack.35.at_ref.refs_0_, bf16[256,768]{1,0:T(8,128)(2,1)} %get-tuple-element.239.gq_ref, bf16[1024,768]{1,0:T(8,128)(2,1)} %get-tuple-element.240.gk_ref, ...), custom_call_target="tpu_custom_call" | custom-call | flops 1 | bytes 1 | tf_op jit(solution)/shard_map/heads_second/pallas_call | solution.py:443
  126.9 1.4 slice.233
  128.3 1.6 fusion
  130.0 1.5 collective-permute-start.16
  131.5 2.0 collective-permute-start.17
  133.9 2.2 collective-permute-start.19
  136.1 8.8 %collective-permute-done.14 = bf16[2,2,2,96,768]{4,3,2,1,0:T(8,128)(2,1)} collective-permute-done((bf16[2,2,2,96,768]{4,3,2,1,0:T(8,128)(2,1)S(1)}, bf16[2,2,2,96,768]{4,3,2,1,0:T(8,128)(2,1)}, u32[]{:S(2)}, u32[]{:S(2)}) %collective-permute-start.14) | collective-permute-done | bytes 1179680 | tf_op jit(solution)/shard_map/ppermute | solution.py:510
  144.9 1.3 fusion.3
  146.2 1.5 collective-permute-start.15
  147.7 1.3 collective-permute-done.17
  150.3 1.9 fusion.2
  154.9 4.8 %collective-permute-done.15 = bf16[2,2,96,768]{3,2,1,0:T(8,128)(2,1)S(1)} collective-permute-done((bf16[2,2,96,768]{3,2,1,0:T(8,128)(2,1)S(1)}, bf16[2,2,96,768]{3,2,1,0:T(8,128)(2,1)S(1)}, u32[]{:S(2)}, u32[]{:S(2)}) %collective-permute-start.15) | collective-permute-done | bytes 589856 | tf_op jit(solution)/shard_map/ppermute | solution.py:510
  159.7 1.8 fusion.5
  161.6 4.5 %collective-permute-start.24 = (bf16[2,96,768]{2,1,0:T(8,128)(2,1)}, bf16[2,96,768]{2,1,0:T(8,128)(2,1)}, u32[]{:S(2)}, u32[]{:S(2)}) collective-permute-start(bf16[2,96,768]{2,1,0:T(8,128)(2,1)} %fusion.5), channel_id=1, source_target_pairs={{0,16},{1,17},{2,18},{3,19},{4,12},{5,13},{6,14},{7,15},{8,24},{9,... | collective-permute-start | bytes 884744 | tf_op jit(solution)/shard_map/ppermute | solution.py:510
  166.8 3.5 %entry_backward.1 = (bf16[256,768]{1,0:T(8,128)(2,1)}, f32[3,768]{1,0:T(4,128)}) custom-call(f32[256,768]{1,0:T(8,128)} %get-tuple-element.273.own_ref, bf16[512,768]{1,0:T(8,128)(2,1)} %copy-done.5, bf16[256,768]{1,0:T(8,128)(2,1)} %copy-done.16, bf16[4,264,768]{2,1,0:T(8,128)(2,1)} %copy-done, f32[1,768]{1,0:T(1,128)} %broadcast_in_dim.30.shift_in_ref.start_ref, ...), custom_call_target="tpu_custom_call" | custom-call | flops 1 | bytes 1 | tf_op jit(solution)/shard_map/entry_backward/pallas_call | solution.py:476
  172.3 1.5 collective-permute-start.21
  173.7 2.1 collective-permute-start.23
  175.8 1.5 fusion.13
  178.5 4.4 %collective-permute-start.31 = (bf16[96,768]{1,0:T(8,128)(2,1)S(1)}, bf16[96,768]{1,0:T(8,128)(2,1)S(1)}, u32[]{:S(2)}, u32[]{:S(2)}) collective-permute-start(bf16[96,768]{1,0:T(8,128)(2,1)S(1)} %get-tuple-element.353), channel_id=1, source_target_pairs={{0,3},{1,2},{2,1},{3,0},{4,7},{5,6},{6,5},{7,4},{8,11},{9,10},{10,... | collective-permute-start | bytes 442376 | tf_op jit(solution)/shard_map/ppermute | solution.py:514
  183.6 15.6 %collective-permute-done.32 = bf16[96,768]{1,0:T(8,128)(2,1)S(1)} collective-permute-done((bf16[96,768]{1,0:T(8,128)(2,1)S(1)}, bf16[96,768]{1,0:T(8,128)(2,1)S(1)}, u32[]{:S(2)}, u32[]{:S(2)}) %collective-permute-start.32) | collective-permute-done | bytes 147488 | tf_op jit(solution)/shard_map/ppermute | solution.py:510
  200.4 1.4 collective-permute-start.28
  201.8 2.2 collective-permute-start.38
  204.8 1.5 collective-permute-start.40
  207.5 8.2 %collective-permute-done.38 = bf16[2,1,96,768]{3,2,1,0:T(8,128)(2,1)S(1)} collective-permute-done((bf16[2,1,96,768]{3,2,1,0:T(8,128)(2,1)S(1)}, bf16[2,1,96,768]{3,2,1,0:T(8,128)(2,1)S(1)}, u32[]{:S(2)}, u32[]{:S(2)}) %collective-permute-start.38) | collective-permute-done | bytes 294944 | tf_op jit(solution)/shard_map/ppermute | solution.py:514
  215.7 11.7 %collective-permute-done.39 = bf16[2,1,96,768]{3,2,1,0:T(8,128)(2,1)S(1)} collective-permute-done((bf16[2,1,96,768]{3,2,1,0:T(8,128)(2,1)S(1)}, bf16[2,1,96,768]{3,2,1,0:T(8,128)(2,1)S(1)}, u32[]{:S(2)}, u32[]{:S(2)}) %collective-permute-start.39) | collective-permute-done | bytes 294944 | tf_op jit(solution)/shard_map/ppermute | solution.py:514
  227.9 4.8 %collective-permute-start.35 = (bf16[1,1,96,768]{3,2,1,0:T(8,128)(2,1)S(1)}, bf16[1,1,96,768]{3,2,1,0:T(8,128)(2,1)S(1)}, u32[]{:S(2)}, u32[]{:S(2)}) collective-permute-start(bf16[1,1,96,768]{3,2,1,0:T(8,128)(2,1)S(1)} %bitcast.292), channel_id=1, source_target_pairs={{0,1},{1,0},{2,3},{3,2},{4,5},{5,4},{6,7},{7,6},{8,9},{9,8},{10,11... | collective-permute-start | bytes 442376 | tf_op jit(solution)/shard_map/ppermute | solution.py:514
  232.8 2.3 collective-permute-start.37
  235.1 1.9 collective-permute-done.35
  237.0 8.4 %collective-permute-done.36 = bf16[1,1,96,768]{3,2,1,0:T(8,128)(2,1)S(1)} collective-permute-done((bf16[1,1,96,768]{3,2,1,0:T(8,128)(2,1)S(1)}, bf16[1,1,96,768]{3,2,1,0:T(8,128)(2,1)S(1)}, u32[]{:S(2)}, u32[]{:S(2)}) %collective-permute-start.36) | collective-permute-done | bytes 147488 | tf_op jit(solution)/shard_map/ppermute | solution.py:514
  245.7 1.2 collective-permute-start.45
  248.6 14.6 %collective-permute-done.41 = bf16[1,4,96,768]{3,2,1,0:T(8,128)(2,1)S(1)} collective-permute-done((bf16[1,4,96,768]{3,2,1,0:T(8,128)(2,1)S(1)}, bf16[1,4,96,768]{3,2,1,0:T(8,128)(2,1)S(1)}, u32[]{:S(2)}, u32[]{:S(2)}) %collective-permute-start.41) | collective-permute-done | bytes 589856 | tf_op jit(solution)/shard_map/ppermute | solution.py:510
  264.6 6.3 %collective-permute-start.46 = (bf16[2,8,96,768]{3,2,1,0:T(8,128)(2,1)S(1)}, bf16[2,8,96,768]{3,2,1,0:T(8,128)(2,1)}, u32[]{:S(2)}, u32[]{:S(2)}) collective-permute-start(bf16[2,8,96,768]{3,2,1,0:T(8,128)(2,1)S(1)} %constant_dynamic-update-slice_fusion.8), channel_id=1, source_target_pairs={{0,4},{1,5},{2,6},{3,7},{4,0},{5,1},{6,2},{7,3},{8,12},{9,13},{10,... | collective-permute-start | bytes 7077896 | tf_op jit(solution)/shard_map/ppermute | solution.py:510
  270.9 1.4 reshape.340
  272.3 1.4 copy.51
  273.6 1.4 reshape.341
  275.6 1.6 slice_reduce_fusion
  277.8 2.1 select_bitcast_fusion.2
  281.4 3.3 %collective-permute-done.47 = bf16[2,8,96,768]{3,2,1,0:T(8,128)(2,1)S(1)} collective-permute-done((bf16[2,8,96,768]{3,2,1,0:T(8,128)(2,1)}, bf16[2,8,96,768]{3,2,1,0:T(8,128)(2,1)S(1)}, u32[]{:S(2)}, u32[]{:S(2)}) %collective-permute-start.47) | collective-permute-done | bytes 2359328 | tf_op jit(solution)/shard_map/ppermute | solution.py:510
  284.6 1.4 copy-done.2
  286.0 7.1 %spread_down.1 = f32[2,2,4,2,96,768]{5,4,3,2,1,0:T(8,128)} custom-call(s32[9]{0:T(128)} %stack.35.at_ref.refs_0_, bf16[2,4,2,96,768]{4,3,2,1,0:T(8,128)(2,1)} %bitcast.256, bf16[2,4,2,96,768]{4,3,2,1,0:T(8,128)(2,1)} %bitcast.101.refs_2_, bf16[2,4,2,96,768]{4,3,2,1,0:T(8,128)(2,1)} %bitcast.102.refs_3_, bf16[2,4,2,96,768]{4,3,2,1,0:T(8,128)(2,1)} %bitcast.261), custom_call_target="tpu_custom_call" | custom-call | flops 1 | bytes 1 | tf_op jit(solution)/shard_map/spread_down/pallas_call | solution.py:683
  293.2 7.1 %spread_up.1 = f32[4,2,96,3072]{3,2,1,0:T(8,128)} custom-call(s32[9]{0:T(128)} %stack.35.at_ref.refs_0_, bf16[2,4,2,96,768]{4,3,2,1,0:T(8,128)(2,1)} %bitcast.257, bf16[2,4,2,96,768]{4,3,2,1,0:T(8,128)(2,1)} %bitcast.106.refs_2_, bf16[2,4,2,96,768]{4,3,2,1,0:T(8,128)(2,1)} %bitcast.107.refs_3_, bf16[2,4,2,96,768]{4,3,2,1,0:T(8,128)(2,1)} %bitcast.262), custom_call_target="tpu_custom_call" | custom-call | flops 1 | bytes 1 | tf_op jit(solution)/shard_map/spread_up/pallas_call | solution.py:683
  300.5 2.7 collective-permute-done.48
  304.3 7.5 %spread_heads.1 = (f32[2,2,2,96,2304]{4,3,2,1,0:T(8,128)}, f32[2,2,2,96,768]{4,3,2,1,0:T(8,128)}) custom-call(s32[9]{0:T(128)} %stack.35.at_ref.refs_0_, bf16[1,2,4,96,768]{4,3,2,1,0:T(8,128)(2,1)} %bitcast.264, bf16[1,2,4,96,768]{4,3,2,1,0:T(8,128)(2,1)} %bitcast.289, bf16[1,2,4,96,768]{4,3,2,1,0:T(8,128)(2,1)} %bitcast.290, ...), custom_call_target="tpu_custom_call" | custom-call | flops 1 | bytes 1 | tf_op jit(solution)/shard_map/spread_heads/pallas_call | solution.py:683
  (169 shorter events, 29.1 us)
Async XLA Ops:
  3.8 13.4 %collective-permute-start = (bf16[264,768]{1,0:T(8,128)(2,1)}, bf16[264,768]{1,0:T(8,128)(2,1)}, u32[]{:S(2)}, u32[]{:S(2)}) collective-permute-start(bf16[264,768]{1,0:T(8,128)(2,1)} %pad_maximum_fusion.2), channel_id=1, source_target_pairs={{0,1},{1,0},{2,4},{3,5},{4,2},{5,3},{6,7},{7,6},{8,9},{9,8},{10,12... | collective-permute-start | bytes 1216520 | tf_op jit(solution)/shard_map/ppermute | solution.py:716
  6.8 10.4 %collective-permute-start.1 = (bf16[264,768]{1,0:T(8,128)(2,1)}, bf16[264,768]{1,0:T(8,128)(2,1)}, u32[]{:S(2)}, u32[]{:S(2)}) collective-permute-start(bf16[264,768]{1,0:T(8,128)(2,1)} %pad_maximum_fusion.2), channel_id=1, source_target_pairs={{2,5},{3,4},{4,3},{5,2},{10,13},{11,12},{12,11},{13,10},{18,21},{1... | collective-permute-start | bytes 1216520 | tf_op jit(solution)/shard_map/ppermute | solution.py:716
  18.5 6.0 %copy-start.17 = (bf16[1,256,768]{2,1,0:T(8,128)(2,1)S(1)}, bf16[1,256,768]{2,1,0:T(8,128)(2,1)}, u32[]{:S(2)}) copy-start(bf16[1,256,768]{2,1,0:T(8,128)(2,1)} %param.29) | copy-start | bytes 1179652
  18.5 6.7 %copy-start.25 = (f32[768]{0:T(1024)S(1)}, f32[768]{0:T(1024)}, u32[]{:S(2)}) copy-start(f32[768]{0:T(1024)} %param.18) | copy-start | bytes 9220
  18.5 7.3 %copy-start.26 = (f32[768]{0:T(1024)S(1)}, f32[768]{0:T(1024)}, u32[]{:S(2)}) copy-start(f32[768]{0:T(1024)} %param.24) | copy-start | bytes 9220
  18.6 9.9 %collective-permute-start.2 = (bf16[2,264,768]{2,1,0:T(8,128)(2,1)S(1)}, bf16[2,264,768]{2,1,0:T(8,128)(2,1)S(1)}, u32[]{:S(2)}, u32[]{:S(2)}) collective-permute-start(bf16[2,264,768]{2,1,0:T(8,128)(2,1)S(1)} %pad_maximum_fusion.1), channel_id=1, source_target_pairs={{0,4},{1,5},{2,6},{3,7},{4,0},{5,1},{6,2},{7,3},{8,12},{9,13},{10,... | collective-permute-start | bytes 2433032 | tf_op jit(solution)/shard_map/ppermute | solution.py:510
  24.5 23.2 %collective-permute-start.3 = (bf16[256,768]{1,0:T(8,128)(2,1)S(1)}, bf16[256,768]{1,0:T(8,128)(2,1)S(1)}, u32[]{:S(2)}, u32[]{:S(2)}) collective-permute-start(bf16[256,768]{1,0:T(8,128)(2,1)S(1)} %bitcast.298), channel_id=1, source_target_pairs={{2,4},{3,5},{4,2},{5,3},{10,12},{11,13},{12,10},{13,11},{18,20},{1... | collective-permute-start | bytes 1179656 | tf_op jit(solution)/shard_map/ppermute | solution.py:716
  48.5 19.8 %copy-start.27 = (f32[768]{0:T(1024)S(1)}, f32[768]{0:T(1024)}, u32[]{:S(2)}) copy-start(f32[768]{0:T(1024)} %param.28) | copy-start | bytes 9220
  59.5 21.3 %collective-permute-start.5 = (bf16[2,8,96,768]{3,2,1,0:T(8,128)(2,1)}, bf16[2,8,96,768]{3,2,1,0:T(8,128)(2,1)S(1)}, u32[]{:S(2)}, u32[]{:S(2)}) collective-permute-start(bf16[2,8,96,768]{3,2,1,0:T(8,128)(2,1)} %get-tuple-element.203), channel_id=1, source_target_pairs={{0,4},{1,5},{2,6},{3,7},{4,0},{5,1},{6,2},{7,3},{8,12},{9,13},{10,... | collective-permute-start | bytes 7077896 | tf_op jit(solution)/shard_map/ppermute | solution.py:510
  68.3 16.8 %collective-permute-start.4 = (bf16[2,8,96,768]{3,2,1,0:T(8,128)(2,1)}, bf16[2,8,96,768]{3,2,1,0:T(8,128)(2,1)S(1)}, u32[]{:S(2)}, u32[]{:S(2)}) collective-permute-start(bf16[2,8,96,768]{3,2,1,0:T(8,128)(2,1)} %get-tuple-element.201), channel_id=1, source_target_pairs={{0,4},{1,5},{2,6},{3,7},{4,0},{5,1},{6,2},{7,3},{8,12},{9,13},{10,... | collective-permute-start | bytes 7077896 | tf_op jit(solution)/shard_map/ppermute | solution.py:510
  80.9 4.2 %copy-start.4 = (bf16[2,8,96,768]{3,2,1,0:T(8,128)(2,1)S(1)}, bf16[2,8,96,768]{3,2,1,0:T(8,128)(2,1)}, u32[]{:S(2)}) copy-start(bf16[2,8,96,768]{3,2,1,0:T(8,128)(2,1)} %get-tuple-element.200) | copy-start | bytes 7077892
  83.6 16.5 %collective-permute-start.6 = (bf16[2,2,2,96,768]{4,3,2,1,0:T(8,128)(2,1)}, bf16[2,2,2,96,768]{4,3,2,1,0:T(8,128)(2,1)}, u32[]{:S(2)}, u32[]{:S(2)}) collective-permute-start(bf16[2,2,2,96,768]{4,3,2,1,0:T(8,128)(2,1)} %bitcast.19), channel_id=1, source_target_pairs={{0,8},{1,9},{2,10},{3,11},{4,20},{5,21},{6,22},{7,23},{8,0},{9,1},... | collective-permute-start | bytes 3538952 | tf_op jit(solution)/shard_map/ppermute | solution.py:510
  102.4 10.2 %collective-permute-start.7 = (bf16[2,2,96,768]{3,2,1,0:T(8,128)(2,1)}, bf16[2,2,96,768]{3,2,1,0:T(8,128)(2,1)}, u32[]{:S(2)}, u32[]{:S(2)}) collective-permute-start(bf16[2,2,96,768]{3,2,1,0:T(8,128)(2,1)} %fusion.4), channel_id=1, source_target_pairs={{0,16},{1,17},{2,18},{3,19},{4,12},{5,13},{6,14},{7,15},{8,24},{9,... | collective-permute-start | bytes 1769480 | tf_op jit(solution)/shard_map/ppermute | solution.py:510
  110.5 16.3 %collective-permute-start.10 = (bf16[4,96,768]{2,1,0:T(8,128)(2,1)}, bf16[4,96,768]{2,1,0:T(8,128)(2,1)}, u32[]{:S(2)}, u32[]{:S(2)}) collective-permute-start(bf16[4,96,768]{2,1,0:T(8,128)(2,1)} %get-tuple-element.232), channel_id=1, source_target_pairs={{0,4},{1,5},{2,6},{3,7},{4,0},{5,1},{6,2},{7,3},{8,12},{9,13},{10,... | collective-permute-start | bytes 1769480 | tf_op jit(solution)/shard_map/ppermute | solution.py:510
  110.6 16.4 %collective-permute-start.11 = (bf16[4,96,768]{2,1,0:T(8,128)(2,1)}, bf16[4,96,768]{2,1,0:T(8,128)(2,1)}, u32[]{:S(2)}, u32[]{:S(2)}) collective-permute-start(bf16[4,96,768]{2,1,0:T(8,128)(2,1)} %get-tuple-element.233), channel_id=1, source_target_pairs={{0,4},{1,5},{2,6},{3,7},{4,0},{5,1},{6,2},{7,3},{8,12},{9,13},{10,... | collective-permute-start | bytes 1769480 | tf_op jit(solution)/shard_map/ppermute | solution.py:510
  111.1 15.9 %collective-permute-start.12 = (bf16[4,96,768]{2,1,0:T(8,128)(2,1)}, bf16[4,96,768]{2,1,0:T(8,128)(2,1)}, u32[]{:S(2)}, u32[]{:S(2)}) collective-permute-start(bf16[4,96,768]{2,1,0:T(8,128)(2,1)} %get-tuple-element.234), channel_id=1, source_target_pairs={{0,4},{1,5},{2,6},{3,7},{4,0},{5,1},{6,2},{7,3},{8,12},{9,13},{10,... | collective-permute-start | bytes 1769480 | tf_op jit(solution)/shard_map/ppermute | solution.py:510
  111.1 15.8 %collective-permute-start.9 = (bf16[4,96,768]{2,1,0:T(8,128)(2,1)}, bf16[4,96,768]{2,1,0:T(8,128)(2,1)}, u32[]{:S(2)}, u32[]{:S(2)}) collective-permute-start(bf16[4,96,768]{2,1,0:T(8,128)(2,1)} %get-tuple-element.231), channel_id=1, source_target_pairs={{0,4},{1,5},{2,6},{3,7},{4,0},{5,1},{6,2},{7,3},{8,12},{9,13},{10,... | collective-permute-start | bytes 1769480 | tf_op jit(solution)/shard_map/ppermute | solution.py:510
  112.6 32.3 %collective-permute-start.14 = (bf16[2,2,2,96,768]{4,3,2,1,0:T(8,128)(2,1)S(1)}, bf16[2,2,2,96,768]{4,3,2,1,0:T(8,128)(2,1)}, u32[]{:S(2)}, u32[]{:S(2)}) collective-permute-start(bf16[2,2,2,96,768]{4,3,2,1,0:T(8,128)(2,1)S(1)} %fusion.1), channel_id=1, source_target_pairs={{0,1},{1,0},{2,3},{3,2},{4,5},{5,4},{6,7},{7,6},{8,9},{9,8},{10,11... | collective-permute-start | bytes 3538952 | tf_op jit(solution)/shard_map/ppermute | solution.py:510
  126.8 7.0 %collective-permute-start.8 = (bf16[512,768]{1,0:T(8,128)(2,1)}, bf16[512,768]{1,0:T(8,128)(2,1)S(1)}, u32[]{:S(2)}, u32[]{:S(2)}) collective-permute-start(bf16[512,768]{1,0:T(8,128)(2,1)} %get-tuple-element.247), channel_id=1, source_target_pairs={{0,4},{1,5},{2,6},{3,7},{4,0},{5,1},{6,2},{7,3},{8,12},{9,13},{10,... | collective-permute-start | bytes 2359304 | tf_op jit(solution)/shard_map/ppermute | solution.py:510
  128.3 5.2 %copy-start.20 = (bf16[96,768]{1,0:T(8,128)(2,1)S(1)}, bf16[96,768]{1,0:T(8,128)(2,1)}, u32[]{:S(2)}) copy-start(bf16[96,768]{1,0:T(8,128)(2,1)} %get-tuple-element.351) | copy-start | bytes 442372
  128.3 5.5 %copy-start.19 = (bf16[96,768]{1,0:T(8,128)(2,1)S(1)}, bf16[96,768]{1,0:T(8,128)(2,1)}, u32[]{:S(2)}) copy-start(bf16[96,768]{1,0:T(8,128)(2,1)} %get-tuple-element.350) | copy-start | bytes 442372
  128.3 7.7 %copy-start.11 = (f32[256,768]{1,0:T(8,128)S(1)}, f32[256,768]{1,0:T(8,128)}, u32[]{:S(2)}) copy-start(f32[256,768]{1,0:T(8,128)} %get-tuple-element.253) | copy-start | bytes 2359300
  130.0 20.2 %collective-permute-start.16 = (bf16[2,2,2,96,768]{4,3,2,1,0:T(8,128)(2,1)S(1)}, bf16[2,2,2,96,768]{4,3,2,1,0:T(8,128)(2,1)S(1)}, u32[]{:S(2)}, u32[]{:S(2)}) collective-permute-start(bf16[2,2,2,96,768]{4,3,2,1,0:T(8,128)(2,1)S(1)} %fusion), channel_id=1, source_target_pairs={{0,8},{1,9},{2,10},{3,11},{4,20},{5,21},{6,22},{7,23},{8,0},{9,1},... | collective-permute-start | bytes 3538952 | tf_op jit(solution)/shard_map/ppermute | solution.py:510
  131.5 17.5 %collective-permute-start.17 = (bf16[96,768]{1,0:T(8,128)(2,1)S(1)}, bf16[96,768]{1,0:T(8,128)(2,1)S(1)}, u32[]{:S(2)}, u32[]{:S(2)}) collective-permute-start(bf16[96,768]{1,0:T(8,128)(2,1)S(1)} %copy-done.21), channel_id=1, source_target_pairs={{0,1},{1,0},{2,3},{3,2},{4,5},{5,4},{6,7},{7,6},{8,9},{9,8},{10,11... | collective-permute-start | bytes 442376 | tf_op jit(solution)/shard_map/ppermute | solution.py:514
  133.5 15.5 %collective-permute-start.18 = (bf16[96,768]{1,0:T(8,128)(2,1)S(1)}, bf16[96,768]{1,0:T(8,128)(2,1)S(1)}, u32[]{:S(2)}, u32[]{:S(2)}) collective-permute-start(bf16[96,768]{1,0:T(8,128)(2,1)S(1)} %copy-done.20), channel_id=1, source_target_pairs={{0,2},{1,3},{2,0},{3,1},{4,6},{5,7},{6,4},{7,5},{8,10},{9,11},{10,... | collective-permute-start | bytes 442376 | tf_op jit(solution)/shard_map/ppermute | solution.py:514
  133.9 12.3 %copy-start.5 = (bf16[512,768]{1,0:T(8,128)(2,1)}, bf16[512,768]{1,0:T(8,128)(2,1)S(1)}, u32[]{:S(2)}) copy-start(bf16[512,768]{1,0:T(8,128)(2,1)S(1)} %collective-permute-done.8.core_ref) | copy-start | bytes 2359300
  133.9 15.2 %collective-permute-start.19 = (bf16[96,768]{1,0:T(8,128)(2,1)S(1)}, bf16[96,768]{1,0:T(8,128)(2,1)S(1)}, u32[]{:S(2)}, u32[]{:S(2)}) collective-permute-start(bf16[96,768]{1,0:T(8,128)(2,1)S(1)} %copy-done.19), channel_id=1, source_target_pairs={{0,3},{1,2},{2,1},{3,0},{4,7},{5,6},{6,5},{7,4},{8,11},{9,10},{10,... | collective-permute-start | bytes 442376 | tf_op jit(solution)/shard_map/ppermute | solution.py:514
  146.2 13.5 %collective-permute-start.15 = (bf16[2,2,96,768]{3,2,1,0:T(8,128)(2,1)S(1)}, bf16[2,2,96,768]{3,2,1,0:T(8,128)(2,1)S(1)}, u32[]{:S(2)}, u32[]{:S(2)}) collective-permute-start(bf16[2,2,96,768]{3,2,1,0:T(8,128)(2,1)S(1)} %fusion.3), channel_id=1, source_target_pairs={{0,8},{1,9},{2,10},{3,11},{4,20},{5,21},{6,22},{7,23},{8,0},{9,1},... | collective-permute-start | bytes 1769480 | tf_op jit(solution)/shard_map/ppermute | solution.py:510
  150.2 3.8 %copy-start.24 = (f32[2,1,768]{2,1,0:T(1,128)S(1)}, f32[2,1,768]{2,1,0:T(1,128)}, u32[]{:S(2)}) copy-start(f32[2,1,768]{2,1,0:T(1,128)} %get-tuple-element.193) | copy-start | bytes 18436
  150.2 3.7 %copy-start.23 = (f32[2,1,768]{2,1,0:T(1,128)S(1)}, f32[2,1,768]{2,1,0:T(1,128)}, u32[]{:S(2)}) copy-start(f32[2,1,768]{2,1,0:T(1,128)} %get-tuple-element.194) | copy-start | bytes 18436
  152.2 23.7 %collective-permute-start.25 = (bf16[2,2,96,768]{3,2,1,0:T(8,128)(2,1)S(1)}, bf16[2,2,96,768]{3,2,1,0:T(8,128)(2,1)S(1)}, u32[]{:S(2)}, u32[]{:S(2)}) collective-permute-start(bf16[2,2,96,768]{3,2,1,0:T(8,128)(2,1)S(1)} %fusion.2), channel_id=1, source_target_pairs={{0,16},{1,17},{2,18},{3,19},{4,12},{5,13},{6,14},{7,15},{8,24},{9,... | collective-permute-start | bytes 1769480 | tf_op jit(solution)/shard_map/ppermute | solution.py:510
  153.4 12.7 %collective-permute-start.13 = (bf16[256,768]{1,0:T(8,128)(2,1)S(1)}, bf16[256,768]{1,0:T(8,128)(2,1)S(1)}, u32[]{:S(2)}, u32[]{:S(2)}) collective-permute-start(bf16[256,768]{1,0:T(8,128)(2,1)S(1)} %add_convert_fusion.2), channel_id=1, source_target_pairs={{0,1},{1,0},{2,3},{3,2},{4,5},{5,4},{6,7},{7,6},{8,9},{9,8},{10,11... | collective-permute-start | bytes 1179656 | tf_op jit(solution)/shard_map/ppermute | solution.py:510
  161.6 15.8 %collective-permute-start.24 = (bf16[2,96,768]{2,1,0:T(8,128)(2,1)}, bf16[2,96,768]{2,1,0:T(8,128)(2,1)}, u32[]{:S(2)}, u32[]{:S(2)}) collective-permute-start(bf16[2,96,768]{2,1,0:T(8,128)(2,1)} %fusion.5), channel_id=1, source_target_pairs={{0,16},{1,17},{2,18},{3,19},{4,12},{5,13},{6,14},{7,15},{8,24},{9,... | collective-permute-start | bytes 884744 | tf_op jit(solution)/shard_map/ppermute | solution.py:510
  166.8 9.0 %copy-start.10 = (bf16[2,2,2,96,768]{4,3,2,1,0:T(8,128)(2,1)S(1)}, bf16[2,2,2,96,768]{4,3,2,1,0:T(8,128)(2,1)}, u32[]{:S(2)}) copy-start(bf16[2,2,2,96,768]{4,3,2,1,0:T(8,128)(2,1)} %copy-done.9) | copy-start | bytes 3538948
  171.0 1.3 collective-permute-start.20
  172.3 6.3 %collective-permute-start.21 = (f32[14,768]{1,0:T(8,128)S(1)}, f32[14,768]{1,0:T(8,128)S(1)}, u32[]{:S(2)}, u32[]{:S(2)}) collective-permute-start(f32[14,768]{1,0:T(8,128)S(1)} %add.315), channel_id=1, source_target_pairs={{0,8},{4,12},{8,0},{12,4},{16,24},{20,28},{24,16},{28,20},{1,9},{5... | collective-permute-start | bytes 129032 | tf_op jit(solution)/shard_map/ppermute | solution.py:626
  173.7 9.2 %collective-permute-start.22 = (f32[14,768]{1,0:T(8,128)S(1)}, f32[14,768]{1,0:T(8,128)S(1)}, u32[]{:S(2)}, u32[]{:S(2)}) collective-permute-start(f32[14,768]{1,0:T(8,128)S(1)} %add.315), channel_id=1, source_target_pairs={{0,16},{4,20},{8,24},{12,28},{16,0},{20,4},{24,8},{28,12},{1,17},{... | collective-permute-start | bytes 129032 | tf_op jit(solution)/shard_map/ppermute | solution.py:626
  173.7 9.2 %collective-permute-start.23 = (f32[14,768]{1,0:T(8,128)S(1)}, f32[14,768]{1,0:T(8,128)S(1)}, u32[]{:S(2)}, u32[]{:S(2)}) collective-permute-start(f32[14,768]{1,0:T(8,128)S(1)} %add.315), channel_id=1, source_target_pairs={{0,24},{4,28},{8,16},{12,20},{16,8},{20,12},{24,0},{28,4},{1,25},{... | collective-permute-start | bytes 129032 | tf_op jit(solution)/shard_map/ppermute | solution.py:626
  177.3 23.1 %collective-permute-start.29 = (bf16[96,768]{1,0:T(8,128)(2,1)S(1)}, bf16[96,768]{1,0:T(8,128)(2,1)S(1)}, u32[]{:S(2)}, u32[]{:S(2)}) collective-permute-start(bf16[96,768]{1,0:T(8,128)(2,1)S(1)} %get-tuple-element.355), channel_id=1, source_target_pairs={{0,1},{1,0},{2,3},{3,2},{4,5},{5,4},{6,7},{7,6},{8,9},{9,8},{10,11... | collective-permute-start | bytes 442376 | tf_op jit(solution)/shard_map/ppermute | solution.py:514
  177.4 24.4 %collective-permute-start.30 = (bf16[96,768]{1,0:T(8,128)(2,1)S(1)}, bf16[96,768]{1,0:T(8,128)(2,1)S(1)}, u32[]{:S(2)}, u32[]{:S(2)}) collective-permute-start(bf16[96,768]{1,0:T(8,128)(2,1)S(1)} %get-tuple-element.354), channel_id=1, source_target_pairs={{0,2},{1,3},{2,0},{3,1},{4,6},{5,7},{6,4},{7,5},{8,10},{9,11},{10,... | collective-permute-start | bytes 442376 | tf_op jit(solution)/shard_map/ppermute | solution.py:514
  178.5 25.4 %collective-permute-start.31 = (bf16[96,768]{1,0:T(8,128)(2,1)S(1)}, bf16[96,768]{1,0:T(8,128)(2,1)S(1)}, u32[]{:S(2)}, u32[]{:S(2)}) collective-permute-start(bf16[96,768]{1,0:T(8,128)(2,1)S(1)} %get-tuple-element.353), channel_id=1, source_target_pairs={{0,3},{1,2},{2,1},{3,0},{4,7},{5,6},{6,5},{7,4},{8,11},{9,10},{10,... | collective-permute-start | bytes 442376 | tf_op jit(solution)/shard_map/ppermute | solution.py:514
  182.9 16.3 %collective-permute-start.32 = (bf16[96,768]{1,0:T(8,128)(2,1)S(1)}, bf16[96,768]{1,0:T(8,128)(2,1)S(1)}, u32[]{:S(2)}, u32[]{:S(2)}) collective-permute-start(bf16[96,768]{1,0:T(8,128)(2,1)S(1)} %fusion.12), channel_id=1, source_target_pairs={{0,2},{1,3},{2,0},{3,1},{4,6},{5,7},{6,4},{7,5},{8,10},{9,11},{10,... | collective-permute-start | bytes 442376 | tf_op jit(solution)/shard_map/ppermute | solution.py:510
  182.9 21.9 %collective-permute-start.26 = (f32[14,768]{1,0:T(8,128)S(1)}, f32[14,768]{1,0:T(8,128)S(1)}, u32[]{:S(2)}, u32[]{:S(2)}) collective-permute-start(f32[14,768]{1,0:T(8,128)S(1)} %add_add_fusion.1), channel_id=1, source_target_pairs={{0,1},{1,0},{2,3},{3,2},{4,5},{5,4},{6,7},{7,6},{8,9},{9,8},{10,11... | collective-permute-start | bytes 129032 | tf_op jit(solution)/shard_map/ppermute | solution.py:626
  199.2 8.3 %collective-permute-start.27 = (f32[14,768]{1,0:T(8,128)S(1)}, f32[14,768]{1,0:T(8,128)S(1)}, u32[]{:S(2)}, u32[]{:S(2)}) collective-permute-start(f32[14,768]{1,0:T(8,128)S(1)} %add_add_fusion.1), channel_id=1, source_target_pairs={{0,2},{1,3},{2,0},{3,1},{4,6},{5,7},{6,4},{7,5},{8,10},{9,11},{10,... | collective-permute-start | bytes 129032 | tf_op jit(solution)/shard_map/ppermute | solution.py:626
  200.4 7.1 %collective-permute-start.28 = (f32[14,768]{1,0:T(8,128)S(1)}, f32[14,768]{1,0:T(8,128)S(1)}, u32[]{:S(2)}, u32[]{:S(2)}) collective-permute-start(f32[14,768]{1,0:T(8,128)S(1)} %add_add_fusion.1), channel_id=1, source_target_pairs={{0,3},{1,2},{2,1},{3,0},{4,7},{5,6},{6,5},{7,4},{8,11},{9,10},{10,... | collective-permute-start | bytes 129032 | tf_op jit(solution)/shard_map/ppermute | solution.py:626
  201.8 13.9 %collective-permute-start.38 = (bf16[2,1,96,768]{3,2,1,0:T(8,128)(2,1)S(1)}, bf16[2,1,96,768]{3,2,1,0:T(8,128)(2,1)S(1)}, u32[]{:S(2)}, u32[]{:S(2)}) collective-permute-start(bf16[2,1,96,768]{3,2,1,0:T(8,128)(2,1)S(1)} %pad_maximum_fusion.3), channel_id=1, source_target_pairs={{0,1},{1,0},{2,3},{3,2},{4,5},{5,4},{6,7},{7,6},{8,9},{9,8},{10,11... | collective-permute-start | bytes 884744 | tf_op jit(solution)/shard_map/ppermute | solution.py:514
  203.9 23.5 %collective-permute-start.39 = (bf16[2,1,96,768]{3,2,1,0:T(8,128)(2,1)S(1)}, bf16[2,1,96,768]{3,2,1,0:T(8,128)(2,1)S(1)}, u32[]{:S(2)}, u32[]{:S(2)}) collective-permute-start(bf16[2,1,96,768]{3,2,1,0:T(8,128)(2,1)S(1)} %pad_maximum_fusion.3), channel_id=1, source_target_pairs={{0,2},{1,3},{2,0},{3,1},{4,6},{5,7},{6,4},{7,5},{8,10},{9,11},{10,... | collective-permute-start | bytes 884744 | tf_op jit(solution)/shard_map/ppermute | solution.py:514
  204.8 22.6 %collective-permute-start.40 = (bf16[2,1,96,768]{3,2,1,0:T(8,128)(2,1)S(1)}, bf16[2,1,96,768]{3,2,1,0:T(8,128)(2,1)S(1)}, u32[]{:S(2)}, u32[]{:S(2)}) collective-permute-start(bf16[2,1,96,768]{3,2,1,0:T(8,128)(2,1)S(1)} %pad_maximum_fusion.3), channel_id=1, source_target_pairs={{0,3},{1,2},{2,1},{3,0},{4,7},{5,6},{6,5},{7,4},{8,11},{9,10},{10,... | collective-permute-start | bytes 884744 | tf_op jit(solution)/shard_map/ppermute | solution.py:514
  207.5 56.6 %copy-start.18 = (f32[14,768]{1,0:T(8,128)}, f32[14,768]{1,0:T(8,128)S(1)}, u32[]{:S(2)}) copy-start(f32[14,768]{1,0:T(8,128)S(1)} %add_add_fusion) | copy-start | bytes 129028
  227.5 18.0 %collective-permute-start.42 = (bf16[2,4,96,768]{3,2,1,0:T(8,128)(2,1)S(1)}, bf16[2,4,96,768]{3,2,1,0:T(8,128)(2,1)S(1)}, u32[]{:S(2)}, u32[]{:S(2)}) collective-permute-start(bf16[2,4,96,768]{3,2,1,0:T(8,128)(2,1)S(1)} %constant_dynamic-update-slice_fusion), channel_id=1, source_target_pairs={{0,16},{1,17},{2,18},{3,19},{4,12},{5,13},{6,14},{7,15},{8,24},{9,... | collective-permute-start | bytes 3538952 | tf_op jit(solution)/shard_map/ppermute | solution.py:510
  227.9 9.1 %collective-permute-start.35 = (bf16[1,1,96,768]{3,2,1,0:T(8,128)(2,1)S(1)}, bf16[1,1,96,768]{3,2,1,0:T(8,128)(2,1)S(1)}, u32[]{:S(2)}, u32[]{:S(2)}) collective-permute-start(bf16[1,1,96,768]{3,2,1,0:T(8,128)(2,1)S(1)} %bitcast.292), channel_id=1, source_target_pairs={{0,1},{1,0},{2,3},{3,2},{4,5},{5,4},{6,7},{7,6},{8,9},{9,8},{10,11... | collective-permute-start | bytes 442376 | tf_op jit(solution)/shard_map/ppermute | solution.py:514
  232.7 12.7 %collective-permute-start.36 = (bf16[1,1,96,768]{3,2,1,0:T(8,128)(2,1)S(1)}, bf16[1,1,96,768]{3,2,1,0:T(8,128)(2,1)S(1)}, u32[]{:S(2)}, u32[]{:S(2)}) collective-permute-start(bf16[1,1,96,768]{3,2,1,0:T(8,128)(2,1)S(1)} %bitcast.293), channel_id=1, source_target_pairs={{0,2},{1,3},{2,0},{3,1},{4,6},{5,7},{6,4},{7,5},{8,10},{9,11},{10,... | collective-permute-start | bytes 442376 | tf_op jit(solution)/shard_map/ppermute | solution.py:514
  232.8 12.6 %collective-permute-start.37 = (bf16[1,1,96,768]{3,2,1,0:T(8,128)(2,1)S(1)}, bf16[1,1,96,768]{3,2,1,0:T(8,128)(2,1)S(1)}, u32[]{:S(2)}, u32[]{:S(2)}) collective-permute-start(bf16[1,1,96,768]{3,2,1,0:T(8,128)(2,1)S(1)} %bitcast.294), channel_id=1, source_target_pairs={{0,3},{1,2},{2,1},{3,0},{4,7},{5,6},{6,5},{7,4},{8,11},{9,10},{10,... | collective-permute-start | bytes 442376 | tf_op jit(solution)/shard_map/ppermute | solution.py:514
  245.7 18.4 %copy-start.1 = (bf16[2,8,96,768]{3,2,1,0:T(8,128)(2,1)}, bf16[2,8,96,768]{3,2,1,0:T(8,128)(2,1)S(1)}, u32[]{:S(2)}) copy-start(bf16[2,8,96,768]{3,2,1,0:T(8,128)(2,1)S(1)} %constant_dynamic-update-slice_fusion.8) | copy-start | bytes 7077892
  245.7 34.2 %collective-permute-start.45 = (bf16[2,8,96,768]{3,2,1,0:T(8,128)(2,1)S(1)}, bf16[2,8,96,768]{3,2,1,0:T(8,128)(2,1)}, u32[]{:S(2)}, u32[]{:S(2)}) collective-permute-start(bf16[2,8,96,768]{3,2,1,0:T(8,128)(2,1)S(1)} %constant_dynamic-update-slice_fusion.8), channel_id=1, source_target_pairs={{0,8},{1,9},{2,10},{3,11},{4,20},{5,21},{6,22},{7,23},{8,0},{9,1},... | collective-permute-start | bytes 7077896 | tf_op jit(solution)/shard_map/ppermute | solution.py:510
  247.0 16.3 %collective-permute-start.41 = (bf16[1,4,96,768]{3,2,1,0:T(8,128)(2,1)S(1)}, bf16[1,4,96,768]{3,2,1,0:T(8,128)(2,1)S(1)}, u32[]{:S(2)}, u32[]{:S(2)}) collective-permute-start(bf16[1,4,96,768]{3,2,1,0:T(8,128)(2,1)S(1)} %constant_dynamic-update-slice_fusion.4), channel_id=1, source_target_pairs={{0,16},{1,17},{2,18},{3,19},{4,12},{5,13},{6,14},{7,15},{8,24},{9,... | collective-permute-start | bytes 1769480 | tf_op jit(solution)/shard_map/ppermute | solution.py:510
  247.3 16.1 %collective-permute-start.33 = (bf16[256,768]{1,0:T(8,128)(2,1)S(1)}, bf16[256,768]{1,0:T(8,128)(2,1)S(1)}, u32[]{:S(2)}, u32[]{:S(2)}) collective-permute-start(bf16[256,768]{1,0:T(8,128)(2,1)S(1)} %copy-done.12), channel_id=1, source_target_pairs={{2,4},{3,5},{4,2},{5,3},{10,12},{11,13},{12,10},{13,11},{18,20},{1... | collective-permute-start | bytes 1179656 | tf_op jit(solution)/shard_map/ppermute | solution.py:716
  247.9 15.4 %collective-permute-start.34 = (bf16[256,768]{1,0:T(8,128)(2,1)S(1)}, bf16[256,768]{1,0:T(8,128)(2,1)S(1)}, u32[]{:S(2)}, u32[]{:S(2)}) collective-permute-start(bf16[256,768]{1,0:T(8,128)(2,1)S(1)} %copy-done.13), channel_id=1, source_target_pairs={{2,4},{3,5},{4,2},{5,3},{10,12},{11,13},{12,10},{13,11},{18,20},{1... | collective-permute-start | bytes 1179656 | tf_op jit(solution)/shard_map/ppermute | solution.py:716
  263.3 17.7 %copy-start.3 = (bf16[1,8,96,768]{3,2,1,0:T(8,128)(2,1)}, bf16[1,8,96,768]{3,2,1,0:T(8,128)(2,1)S(1)}, u32[]{:S(2)}) copy-start(bf16[1,8,96,768]{3,2,1,0:T(8,128)(2,1)S(1)} %constant_dynamic-update-slice_fusion.10) | copy-start | bytes 3538948
  264.6 16.8 %collective-permute-start.46 = (bf16[2,8,96,768]{3,2,1,0:T(8,128)(2,1)S(1)}, bf16[2,8,96,768]{3,2,1,0:T(8,128)(2,1)}, u32[]{:S(2)}, u32[]{:S(2)}) collective-permute-start(bf16[2,8,96,768]{3,2,1,0:T(8,128)(2,1)S(1)} %constant_dynamic-update-slice_fusion.8), channel_id=1, source_target_pairs={{0,4},{1,5},{2,6},{3,7},{4,0},{5,1},{6,2},{7,3},{8,12},{9,13},{10,... | collective-permute-start | bytes 7077896 | tf_op jit(solution)/shard_map/ppermute | solution.py:510
  279.9 4.7 %collective-permute-start.47 = (bf16[2,8,96,768]{3,2,1,0:T(8,128)(2,1)}, bf16[2,8,96,768]{3,2,1,0:T(8,128)(2,1)S(1)}, u32[]{:S(2)}, u32[]{:S(2)}) collective-permute-start(bf16[2,8,96,768]{3,2,1,0:T(8,128)(2,1)} %collective-permute-done.45), channel_id=1, source_target_pairs={{0,4},{1,5},{2,6},{3,7},{4,0},{5,1},{6,2},{7,3},{8,12},{9,13},{10,... | collective-permute-start | bytes 7077896 | tf_op jit(solution)/shard_map/ppermute | solution.py:510
  279.9 20.4 %collective-permute-start.43 = (bf16[1,8,96,768]{3,2,1,0:T(8,128)(2,1)S(1)}, bf16[1,8,96,768]{3,2,1,0:T(8,128)(2,1)S(1)}, u32[]{:S(2)}, u32[]{:S(2)}) collective-permute-start(bf16[1,8,96,768]{3,2,1,0:T(8,128)(2,1)S(1)} %constant_dynamic-update-slice_fusion.10), channel_id=1, source_target_pairs={{0,8},{1,9},{2,10},{3,11},{4,20},{5,21},{6,22},{7,23},{8,0},{9,1},... | collective-permute-start | bytes 3538952 | tf_op jit(solution)/shard_map/ppermute | solution.py:510
  281.0 19.6 %collective-permute-start.44 = (bf16[1,8,96,768]{3,2,1,0:T(8,128)(2,1)S(1)}, bf16[1,8,96,768]{3,2,1,0:T(8,128)(2,1)S(1)}, u32[]{:S(2)}, u32[]{:S(2)}) collective-permute-start(bf16[1,8,96,768]{3,2,1,0:T(8,128)(2,1)S(1)} %constant_dynamic-update-slice_fusion.10), channel_id=1, source_target_pairs={{0,4},{1,5},{2,6},{3,7},{4,0},{5,1},{6,2},{7,3},{8,12},{9,13},{10,... | collective-permute-start | bytes 3538952 | tf_op jit(solution)/shard_map/ppermute | solution.py:510
  300.3 2.9 collective-permute-start.48
  (13 other events, 24.7 us)

commit v3 on v2

--- a/solution.py
+++ b/solution.py
@@ -375,7 +375,7 @@
 
 def heads_first_kernel(at_ref, gq_ref, gk_ref, gv_ref, first_t_ref, o_ref, branch_ref, *outs):
     def store(place, mat, value):
-        outs[place][mat] = value
+        outs[place // 2][place % 2, mat] = value
 
     head_grads(store, 1 - at_ref[0], 5, at_ref, gq_ref, gk_ref, gv_ref, first_t_ref, o_ref, branch_ref)
 
@@ -422,13 +422,13 @@
 def heads_first(at, gq, gk, gv, first_t, o_t, branch):
     rows, width = gq.shape
     ins, _, _ = heads_specs(rows, width, gk.shape[0])
-    piece = pl.BlockSpec((4, width // 8, HEADS_PER_STEP * HEAD_DIM), lambda g, at: (0, 0, g))
+    piece = pl.BlockSpec((2, 4, width // 8, HEADS_PER_STEP * HEAD_DIM), lambda g, at: (0, 0, 0, g))
     return pl.pallas_call(
         heads_first_kernel,
         grid_spec=pltpu.PrefetchScalarGridSpec(
-            num_scalar_prefetch=1, grid=(HEADS // HEADS_PER_STEP,), in_specs=ins, out_specs=[piece] * 4
+            num_scalar_prefetch=1, grid=(HEADS // HEADS_PER_STEP,), in_specs=ins, out_specs=[piece] * 2
         ),
-        out_shape=[jax.ShapeDtypeStruct((4, width // 8, width), BF)] * 4,
+        out_shape=[jax.ShapeDtypeStruct((2, 4, width // 8, width), BF)] * 2,
         compiler_params=params(),
         name="heads_first",
         cost_estimate=LIGHT,
@@ -452,7 +452,7 @@
         out_shape=[shape, piece(F32, 1), piece(F32, 1), piece(BF, 2)],
         compiler_params=params(),
         name="heads_second",
-        cost_estimate=LIGHT,
+        cost_estimate=pl.CostEstimate(flops=10**10, bytes_accessed=3 * 10**7, transcendentals=0),
     )(at, gq, gk, gv, first_t, o_t, branch, w_t)
 
 
@@ -542,12 +542,8 @@
 
     def take(self, value, sides):
         if isinstance(value, tuple):
-            size = 2 if self.bits[1] in sides else 1
-            first = 2 * sides[self.bits[0]] + sides.get(self.bits[1], 0)
-            picked = value[first : first + 1] if size == 2 else value[first : first + 2]
-            rest = {bit: side for bit, side in sides.items() if bit not in self.bits[:2]}
-            inner = [Part(v, self.bits[2:]).take(v, rest) for v in picked]
-            return inner[0] if size == 2 else jnp.stack(inner)
+            rest = {bit: side for bit, side in sides.items() if bit != self.bits[0]}
+            return Part(None, self.bits[1:]).take(value[sides[self.bits[0]]], rest)
         index = tuple(sides[bit] if bit in sides else slice(None) for bit in self.bits)
         return value.reshape((2,) * len(self.bits) + value.shape[-2:])[index]
 
@@ -768,48 +764,50 @@
     head_inputs = (gq, gk, gv, first_t, o_t, branch)
     head_theirs = chain.then(lambda *args: heads_first(at, *args), *head_inputs)
     head_received = tuple(swap(piece, "cc") for piece in head_theirs)
-    down.quarter(chain)
+    up.halve(chain, "a")
+    down.halve(chain, "z")
+    layer_moved = homes.move(layer_out, None, (1, 2))
     head_mine, gx_own, gx_near, gx_core = chain.then(lambda *args: heads_second(at, *args), *head_inputs, w_t)
     heads = Chunk(None, head_received, head_mine)
     gx_core = swap(gx_core, "cc")
     heads.halve(chain, "a")
+    up.halve(chain, "b")
     gx_near = chain.then(lambda a, b: (a + b[rows:].astype(F32)).astype(BF), gx_near, gx_core)
     gx_near = swap(gx_near, "zz")
-    up.halve(chain, "a")
+    down.halve(chain, "w")
+    up.halve(chain, "w")
+    heads.halve(chain, "b")
     down_sum = down.finish(chain)
-    layer_moved = homes.move(layer_out, None, (1, 2))
-    heads.halve(chain, "b")
-    up.halve(chain, "b")
+    native = homes.native
+    layer_out = chain.then(lambda a, b: jnp.where(native, a, b), layer_out, layer_moved)
     grad_tokens, small_entry = chain.then(
         lambda *args: entry_backward(args[:3], *args[3:]), gx_own, gx_core, gx_near, x_all, start_row, norm_gain, gmid
     )
-    tokens_moved = homes.move(grad_tokens, None, (1, 2))
     hidden_bias = [jnp.concatenate([a[2][:, 0], b[2][:, 0]]) for a, b in ((mine, theirs), (theirs, mine))]
     smalls = jnp.concatenate(
         [small_feed, jnp.where(core == 0, hidden_bias[0], hidden_bias[1]), gbqkv[:, 0], small_entry]
     )
+    up_sum = up.finish(chain)
+    heads.halve(chain, "z")
+    feed = Gather(chain, [down_sum, up_sum])
     smalls = sum_small(chain, smalls, "dp", [1])
-    heads.quarter(chain)
-    up.halve(chain, "w")
-    smalls = sum_small(chain, smalls, "dp", [2, 4, 6])
-    for k in range(3, lax.axis_size("dp").bit_length() - 1):
+    heads.halve(chain, "w")
+    for k in range(1, lax.axis_size("dp").bit_length() - 1):
         smalls = sum_small(chain, smalls, "dp", [1 << k])
-    up_sum = up.finish(chain)
-    feed = Gather(chain, [down_sum, up_sum])
+    feed.double(chain)
     heads = Gather(chain, [heads.finish(chain)])
-    smalls = sum_small(chain, smalls, "seq", [1, 2, 3])
+    smalls = sum_small(chain, smalls, "seq", [1])
+    smalls = sum_small(chain, smalls, "seq", [2])
+    tokens_moved = homes.move(grad_tokens, None, (1, 2))
     feed.double(chain)
     heads.double(chain)
-    feed.double(chain)
-    heads.double(chain)
-
-    def settled(smalls, layer, tokens):
+    grad_tokens = chain.then(lambda a, b: jnp.where(native, a, b), grad_tokens, tokens_moved)
+
+    def settled(smalls):
         gain_1, shift_1, grad_bout, grad_bdown = smalls[:4]
         grad_bqkv = smalls[-6:-3].reshape(3, HEADS, HEAD_DIM).transpose(1, 0, 2).reshape(-1)
         gain_0, shift_0, grad_start = smalls[-3:]
         return (
-            jnp.where(homes.native, layer_out, layer)[None],
-            jnp.where(homes.native, grad_tokens, tokens)[None],
             grad_start,
             jnp.stack([gain_0, gain_1]),
             jnp.stack([shift_0, shift_1]),
@@ -819,15 +817,16 @@
             grad_bdown,
         )
 
-    small_outs = chain.then(settled, smalls, layer_moved, tokens_moved)
+    small_outs = chain.then(settled, smalls)
+    heads.double(chain)
     feed.cross(chain)
     (grad_down,) = feed.spread(chain, "down", 0)
     (grad_up,) = feed.spread(chain, "up", 1)
     heads.cross(chain)
     grad_qkv, grad_wout = heads.spread(chain, "heads", 0)
-    layer, tokens_grad, grad_start, grad_gain, grad_shift, grad_bqkv, grad_bout, grad_bup, grad_bdown = small_outs
+    grad_start, grad_gain, grad_shift, grad_bqkv, grad_bout, grad_bup, grad_bdown = small_outs
     return (
-        layer, tokens_grad, grad_start, grad_gain, grad_shift, grad_qkv, grad_bqkv, grad_wout, grad_bout, grad_up,
+        layer_out[None], grad_tokens[None], grad_start, grad_gain, grad_shift, grad_qkv, grad_bqkv, grad_wout, grad_bout, grad_up,
         grad_bup, grad_down, grad_bdown,
     )
 

time: 313 us -> 289 us (0.923)
  waiting for transfers between devices: 86.2 us -> 64 us
  starting transfers between devices: 70.8 us -> 67.4 us
    ppermute x25 -> x27, waiting for transfers between devices: 51.8 us -> 36.1 us  [swap(): return lax.ppermute(value, ('dp', 'seq'), pairs)]
    ppermute x12 -> x6, starting transfers between devices: 20.8 us -> 8.86 us  [swap_seq(): return lax.ppermute(value, 'seq', xor_pairs(lax.axis_size('seq'), mask))]
    ppermute x12 -> x6, waiting for transfers between devices: 31.6 us -> 21.3 us  [swap_seq(): return lax.ppermute(value, 'seq', xor_pairs(lax.axis_size('seq'), mask))]
    ppermute x25 -> x27, starting transfers between devices: 37.8 us -> 45.9 us  [swap(): return lax.ppermute(value, ('dp', 'seq'), pairs)]
    ppermute x7 -> x5, waiting for transfers between devices: 1.23 us -> 4.96 us  [sum_small(): parts = [lax.ppermute(value, axis, xor_pairs(size, mask)) for mask in masks]]
    convert_element_type x13 -> x15, other arithmetic: 20.1 us -> 22.6 us  [add_up(): return sum((p.astype(F32) for p in parts)).astype(BF)]
    unnamed x69 -> x63, local copies, waits for them, and re-layouts: 8.52 us -> 7.28 us
  transfers between devices with their start and end apart: 49 -> 43, of which waited for: 15 -> 14; matrix products, arithmetic and copies ran while one was open for 14% -> 16% of each run, Pallas kernels for 26% -> 28%
where the time goes in v3:
time: 289 us; the launch traced here: 287 us
  Pallas kernels  98.2 us (34%)
  starting transfers between devices  67.4 us (23%)
  waiting for transfers between devices  64 us (22%)
  other arithmetic  31 us (11%)
  local copies, waits for them, and re-layouts  24.5 us (8%)
    ppermute x27, starting transfers between devices, swap(): return lax.ppermute(value, ('dp', 'seq'), pairs)  45.9 us
    ppermute x27, waiting for transfers between devices, swap(): return lax.ppermute(value, ('dp', 'seq'), pairs)  36.1 us
    convert_element_type x15, other arithmetic, add_up(): return sum((p.astype(F32) for p in parts)).astype(BF)  22.6 us
    pallas_call x3, Pallas kernels, spread(): pl.pallas_call(lambda *refs: spread_kernel(kind, *refs), grid_spec=pltpu....  21.8 us
    ppermute x6, waiting for transfers between devices, swap_seq(): return lax.ppermute(value, 'seq', xor_pairs(lax.axis_size('seq'), mask))  21.3 us
    pallas_call x1, Pallas kernels, attention_forward(): pl.pallas_call(forward_kernel, grid=(HEADS // HEADS_PER_STEP,), in_specs=...  17.7 us
    pallas_call x1, Pallas kernels, attention_backward(): pl.pallas_call(backward_kernel, grid=(HEADS // HEADS_PER_STEP,), in_specs...  13.8 us
    pallas_call x1, Pallas kernels, heads_second(): pl.pallas_call(heads_second_kernel, grid_spec=pltpu.PrefetchScalarGridSpe...  11.9 us
  transfers between devices with their start and end apart: 43, of which 14 were waited for; matrix products, arithmetic and copies ran while one was open for 16% of the time, Pallas kernels for 28%

profile of v3, /device:TPU:0, one launch (start us, length us, event | category | flops | bytes accessed | tf_op | source)
XLA Modules:
  0.0 287.1 jit_solution(15724975912435241763)
XLA Ops:
  2.0 1.8 pad_maximum_fusion.2
  3.8 3.0 %collective-permute-start = (bf16[264,768]{1,0:T(8,128)(2,1)}, bf16[264,768]{1,0:T(8,128)(2,1)}, u32[]{:S(2)}, u32[]{:S(2)}) collective-permute-start(bf16[264,768]{1,0:T(8,128)(2,1)} %pad_maximum_fusion.2), channel_id=1, source_target_pairs={{0,1},{1,0},{2,4},{3,5},{4,2},{5,3},{6,7},{7,6},{8,9},{9,8},{10,12... | collective-permute-start | bytes 1216520 | tf_op jit(solution)/shard_map/ppermute | solution.py:712
  6.8 1.4 collective-permute-start.1
  8.2 4.5 %copy.32 = bf16[768,2304]{0,1:T(8,128)(2,1)S(1)} copy(bf16[768,2304]{1,0:T(8,128)(2,1)} %param.21) | data formatting | bytes 7077888 | tf_op args[6]
  12.8 2.0 copy.33
  15.7 1.6 collective-permute-done
  17.2 1.3 select_bitcast_fusion.1
  18.6 5.9 %collective-permute-start.2 = (bf16[2,264,768]{2,1,0:T(8,128)(2,1)S(1)}, bf16[2,264,768]{2,1,0:T(8,128)(2,1)S(1)}, u32[]{:S(2)}, u32[]{:S(2)}) collective-permute-start(bf16[2,264,768]{2,1,0:T(8,128)(2,1)S(1)} %pad_maximum_fusion.1), channel_id=1, source_target_pairs={{0,4},{1,5},{2,6},{3,7},{4,0},{5,1},{6,2},{7,3},{8,12},{9,13},{10,... | collective-permute-start | bytes 2433032 | tf_op jit(solution)/shard_map/ppermute | solution.py:510
  27.1 1.4 copy.35.b_ref
  28.8 1.2 multiply_sine_fusion
  30.0 17.7 %attention_forward.1 = (bf16[768,256]{1,0:T(8,128)(2,1)}, bf16[768,1024]{1,0:T(8,128)(2,1)}, bf16[768,1024]{1,0:T(8,128)(2,1)}, bf16[12,1024,256]{2,1,0:T(8,128)...) custom-call(bf16[4,264,768]{2,1,0:T(8,128)(2,1)} %copy-done, f32[1,768]{1,0:T(1,128)} %broadcast_in_dim.30.shift_in_ref.start_ref, ...), custom_call_target="tpu_custom_call" | custom-call | flops 1 | bytes 1 | tf_op jit(solution)/shard_map/attention_forward/pallas_call | solution.py:103
  48.5 11.0 %feed_first.1 = (f32[256,768]{1,0:T(8,128)}, bf16[256,768]{1,0:T(8,128)(2,1)}, bf16[768,256]{1,0:T(8,128)(2,1)}, f32[256,768]{1,0:T(8,128)}, f32[256,768]{1,0:T(...) custom-call(s32[9]{0:T(128)} %stack.33.at_ref.refs_0_, ...), custom_call_target="tpu_custom_call" | custom-call | flops 1 | bytes 1 | tf_op jit(solution)/shard_map/feed_first/pallas_call | solution.py:254
  59.6 8.7 %collective-permute-start.5 = (bf16[2,8,96,768]{3,2,1,0:T(8,128)(2,1)}, bf16[2,8,96,768]{3,2,1,0:T(8,128)(2,1)S(1)}, u32[]{:S(2)}, u32[]{:S(2)}) collective-permute-start(bf16[2,8,96,768]{3,2,1,0:T(8,128)(2,1)} %get-tuple-element.200), channel_id=1, source_target_pairs={{0,4},{1,5},{2,6},{3,7},{4,0},{5,1},{6,2},{7,3},{8,12},{9,13},{10,... | collective-permute-start | bytes 7077896 | tf_op jit(solution)/shard_map/ppermute | solution.py:510
  68.9 11.9 %feed_second.1 = (bf16[256,768]{1,0:T(8,128)(2,1)}, f32[256,768]{1,0:T(8,128)}, bf16[256,768]{1,0:T(8,128)(2,1)}, bf16[768,256]{1,0:T(8,128)(2,1)}, bf16[2,8,96,...) custom-call(s32[9]{0:T(128)} %stack.33.at_ref.refs_0_, ...), custom_call_target="tpu_custom_call" | custom-call | flops 1 | bytes 1 | tf_op jit(solution)/shard_map/feed_second/pallas_call | solution.py:273
  80.9 1.7 add_convert_fusion.1
  82.6 1.6 collective-permute-start.6
  84.2 1.3 fusion.1
  85.5 13.8 %attention_backward.1 = (bf16[256,768]{1,0:T(8,128)(2,1)}, bf16[1024,768]{1,0:T(8,128)(2,1)}, bf16[1024,768]{1,0:T(8,128)(2,1)}, f32[3,8,768]{2,1,0:T(8,128)}) custom-call(bf16[768,256]{1,0:T(8,128)(2,1)} %get-tuple-element.212.q_ref, bf16[768,1024]{1,0:T(8,128)(2,1)} %get-tuple-element.213.k_ref, bf16[768,1024]{1,0:T(8,128)(2,1)} %get-tuple-element.214.v_ref, ...), custom_call_target="tpu_custom_call" | custom-call | flops 1 | bytes 1 | tf_op jit(solution)/shard_map/attention_backward/pallas_call | solution.py:335
  99.3 2.3 fusion.4
  101.6 1.5 collective-permute-start.8
  103.1 6.6 %heads_first.1 = (bf16[2,4,96,768]{3,2,1,0:T(8,128)(2,1)}, bf16[2,4,96,768]{3,2,1,0:T(8,128)(2,1)}) custom-call(s32[9]{0:T(128)} %stack.33.at_ref.refs_0_, bf16[256,768]{1,0:T(8,128)(2,1)} %get-tuple-element.244.gq_ref, bf16[1024,768]{1,0:T(8,128)(2,1)} %get-tuple-element.245.gk_ref, bf16[1024,768]{1,0:T(8,128)(2,1)} %get-tuple-element.246.gv_ref, ...), custom_call_target="tpu_custom_call" | custom-call | flops 1 | bytes 1 | tf_op jit(solution)/shard_map/heads_first/pallas_call | solution.py:426
  110.3 3.6 %collective-permute-done.9 = bf16[2,2,2,96,768]{4,3,2,1,0:T(8,128)(2,1)} collective-permute-done((bf16[2,2,2,96,768]{4,3,2,1,0:T(8,128)(2,1)}, bf16[2,2,2,96,768]{4,3,2,1,0:T(8,128)(2,1)}, u32[]{:S(2)}, u32[]{:S(2)}) %collective-permute-start.9) | collective-permute-done | bytes 1179680 | tf_op jit(solution)/shard_map/ppermute | solution.py:510
  113.9 2.1 fusion.3
  117.0 2.0 fusion.7
  119.0 11.9 %heads_second.1 = (bf16[4,4,96,768]{3,2,1,0:T(8,128)(2,1)}, f32[256,768]{1,0:T(8,128)}, f32[256,768]{1,0:T(8,128)}, bf16[512,768]{1,0:T(8,128)(2,1)}) custom-call(s32[9]{0:T(128)} %stack.33.at_ref.refs_0_, bf16[256,768]{1,0:T(8,128)(2,1)} %get-tuple-element.244.gq_ref, bf16[1024,768]{1,0:T(8,128)(2,1)} %get-tuple-element.245.gk_ref, ...), custom_call_target="tpu_custom_call" | custom-call | flops 10000000000 | bytes 30000000 | tf_op jit(solution)/shard_map/heads_second/pallas_call | solution.py:443
  131.0 1.4 slice.219
  137.1 2.1 collective-permute-start.18
  139.2 9.4 %collective-permute-done.10 = bf16[2,96,768]{2,1,0:T(8,128)(2,1)S(1)} collective-permute-done((bf16[2,96,768]{2,1,0:T(8,128)(2,1)S(1)}, bf16[2,96,768]{2,1,0:T(8,128)(2,1)S(1)}, u32[]{:S(2)}, u32[]{:S(2)}) %collective-permute-start.10) | collective-permute-done | bytes 294944 | tf_op jit(solution)/shard_map/ppermute | solution.py:510
  149.8 4.2 %collective-permute-start.15 = (bf16[96,768]{1,0:T(8,128)(2,1)S(1)}, bf16[96,768]{1,0:T(8,128)(2,1)S(1)}, u32[]{:S(2)}, u32[]{:S(2)}) collective-permute-start(bf16[96,768]{1,0:T(8,128)(2,1)S(1)} %fusion.16), channel_id=1, source_target_pairs={{0,2},{1,3},{2,0},{3,1},{4,6},{5,7},{6,4},{7,5},{8,10},{9,11},{10,... | collective-permute-start | bytes 442376 | tf_op jit(solution)/shard_map/ppermute | solution.py:510
  153.9 1.8 fusion.15
  156.9 2.1 fusion.2
  159.0 1.2 collective-permute-start.20
  160.2 4.4 %collective-permute-done.15 = bf16[96,768]{1,0:T(8,128)(2,1)S(1)} collective-permute-done((bf16[96,768]{1,0:T(8,128)(2,1)S(1)}, bf16[96,768]{1,0:T(8,128)(2,1)S(1)}, u32[]{:S(2)}, u32[]{:S(2)}) %collective-permute-start.15) | collective-permute-done | bytes 147488 | tf_op jit(solution)/shard_map/ppermute | solution.py:510
  164.6 1.8 fusion.14
  167.3 3.4 %entry_backward.1 = (bf16[256,768]{1,0:T(8,128)(2,1)}, f32[3,768]{1,0:T(4,128)}) custom-call(f32[256,768]{1,0:T(8,128)} %get-tuple-element.285.own_ref, bf16[512,768]{1,0:T(8,128)(2,1)} %copy-done.5, bf16[256,768]{1,0:T(8,128)(2,1)} %collective-permute-done.18.near_ref, bf16[4,264,768]{2,1,0:T(8,128)(2,1)} %copy-done, ...), custom_call_target="tpu_custom_call" | custom-call | flops 1 | bytes 1 | tf_op jit(solution)/shard_map/entry_backward/pallas_call | solution.py:476
  170.7 1.2 fusion.12
  171.9 1.3 fusion.5
  175.2 1.8 collective-permute-start.25
  178.1 1.6 collective-permute-start.27
  180.5 9.0 %collective-permute-done.22 = bf16[2,96,768]{2,1,0:T(8,128)(2,1)S(1)} collective-permute-done((bf16[2,96,768]{2,1,0:T(8,128)(2,1)S(1)}, bf16[2,96,768]{2,1,0:T(8,128)(2,1)S(1)}, u32[]{:S(2)}, u32[]{:S(2)}) %collective-permute-start.22) | collective-permute-done | bytes 294944 | tf_op jit(solution)/shard_map/ppermute | solution.py:510
  190.7 1.6 collective-permute-start.29
  192.3 2.5 collective-permute-done.29
  194.8 7.2 %collective-permute-done.25 = bf16[2,1,96,768]{3,2,1,0:T(8,128)(2,1)S(1)} collective-permute-done((bf16[2,1,96,768]{3,2,1,0:T(8,128)(2,1)S(1)}, bf16[2,1,96,768]{3,2,1,0:T(8,128)(2,1)S(1)}, u32[]{:S(2)}, u32[]{:S(2)}) %collective-permute-start.25) | collective-permute-done | bytes 294944 | tf_op jit(solution)/shard_map/ppermute | solution.py:514
  202.7 5.5 %collective-permute-start.24 = (bf16[96,768]{1,0:T(8,128)(2,1)S(1)}, bf16[96,768]{1,0:T(8,128)(2,1)S(1)}, u32[]{:S(2)}, u32[]{:S(2)}) collective-permute-start(bf16[96,768]{1,0:T(8,128)(2,1)S(1)} %fusion.10), channel_id=1, source_target_pairs={{0,2},{1,3},{2,0},{3,1},{4,6},{5,7},{6,4},{7,5},{8,10},{9,11},{10,... | collective-permute-start | bytes 442376 | tf_op jit(solution)/shard_map/ppermute | solution.py:510
  208.2 3.6 %collective-permute-done.24 = bf16[96,768]{1,0:T(8,128)(2,1)S(1)} collective-permute-done((bf16[96,768]{1,0:T(8,128)(2,1)S(1)}, bf16[96,768]{1,0:T(8,128)(2,1)S(1)}, u32[]{:S(2)}, u32[]{:S(2)}) %collective-permute-start.24) | collective-permute-done | bytes 147488 | tf_op jit(solution)/shard_map/ppermute | solution.py:510
  213.0 2.6 collective-permute-start.35
  215.6 2.4 collective-permute-done.35
  218.6 2.9 %collective-permute-start.39 = (bf16[2,8,96,768]{3,2,1,0:T(8,128)(2,1)S(1)}, bf16[2,8,96,768]{3,2,1,0:T(8,128)(2,1)}, u32[]{:S(2)}, u32[]{:S(2)}) collective-permute-start(bf16[2,8,96,768]{3,2,1,0:T(8,128)(2,1)S(1)} %constant_dynamic-update-slice_fusion.4), channel_id=1, source_target_pairs={{0,8},{1,9},{2,10},{3,11},{4,20},{5,21},{6,22},{7,23},{8,0},{9,1},... | collective-permute-start | bytes 7077896 | tf_op jit(solution)/shard_map/ppermute | solution.py:510
  221.5 2.0 collective-permute-start.30
  224.4 1.5 collective-permute-start.32
  226.6 1.3 collective-permute-done.30
  227.8 12.9 %collective-permute-done.31 = bf16[1,1,96,768]{3,2,1,0:T(8,128)(2,1)S(1)} collective-permute-done((bf16[1,1,96,768]{3,2,1,0:T(8,128)(2,1)S(1)}, bf16[1,1,96,768]{3,2,1,0:T(8,128)(2,1)S(1)}, u32[]{:S(2)}, u32[]{:S(2)}) %collective-permute-start.31) | collective-permute-done | bytes 147488 | tf_op jit(solution)/shard_map/ppermute | solution.py:514
  242.7 5.4 %collective-permute-start.40 = (bf16[2,8,96,768]{3,2,1,0:T(8,128)(2,1)S(1)}, bf16[2,8,96,768]{3,2,1,0:T(8,128)(2,1)}, u32[]{:S(2)}, u32[]{:S(2)}) collective-permute-start(bf16[2,8,96,768]{3,2,1,0:T(8,128)(2,1)S(1)} %constant_dynamic-update-slice_fusion.4), channel_id=1, source_target_pairs={{0,4},{1,5},{2,6},{3,7},{4,0},{5,1},{6,2},{7,3},{8,12},{9,13},{10,... | collective-permute-start | bytes 7077896 | tf_op jit(solution)/shard_map/ppermute | solution.py:510
  248.1 1.4 reshape.346
  249.5 1.4 copy.63
  250.8 1.4 reshape.347
  252.8 1.6 slice_reduce_fusion
  255.2 1.5 collective-permute-start.37
  257.0 3.0 %collective-permute-done.41 = bf16[2,8,96,768]{3,2,1,0:T(8,128)(2,1)S(1)} collective-permute-done((bf16[2,8,96,768]{3,2,1,0:T(8,128)(2,1)}, bf16[2,8,96,768]{3,2,1,0:T(8,128)(2,1)S(1)}, u32[]{:S(2)}, u32[]{:S(2)}) %collective-permute-start.41) | collective-permute-done | bytes 2359328 | tf_op jit(solution)/shard_map/ppermute | solution.py:510
  259.9 1.4 copy-done.2
  261.3 7.1 %spread_down.1 = f32[2,2,4,2,96,768]{5,4,3,2,1,0:T(8,128)} custom-call(s32[9]{0:T(128)} %stack.33.at_ref.refs_0_, bf16[2,4,2,96,768]{4,3,2,1,0:T(8,128)(2,1)} %bitcast.256, bf16[2,4,2,96,768]{4,3,2,1,0:T(8,128)(2,1)} %bitcast.101.refs_2_, bf16[2,4,2,96,768]{4,3,2,1,0:T(8,128)(2,1)} %bitcast.102.refs_3_, bf16[2,4,2,96,768]{4,3,2,1,0:T(8,128)(2,1)} %bitcast.263), custom_call_target="tpu_custom_call" | custom-call | flops 1 | bytes 1 | tf_op jit(solution)/shard_map/spread_down/pallas_call | solution.py:679
  268.5 7.1 %spread_up.1 = f32[4,2,96,3072]{3,2,1,0:T(8,128)} custom-call(s32[9]{0:T(128)} %stack.33.at_ref.refs_0_, bf16[2,4,2,96,768]{4,3,2,1,0:T(8,128)(2,1)} %bitcast.257, bf16[2,4,2,96,768]{4,3,2,1,0:T(8,128)(2,1)} %bitcast.106.refs_2_, bf16[2,4,2,96,768]{4,3,2,1,0:T(8,128)(2,1)} %bitcast.107.refs_3_, bf16[2,4,2,96,768]{4,3,2,1,0:T(8,128)(2,1)} %bitcast.264), custom_call_target="tpu_custom_call" | custom-call | flops 1 | bytes 1 | tf_op jit(solution)/shard_map/spread_up/pallas_call | solution.py:679
  275.8 2.7 collective-permute-done.42
  279.6 7.5 %spread_heads.1 = (f32[2,2,2,96,2304]{4,3,2,1,0:T(8,128)}, f32[2,2,2,96,768]{4,3,2,1,0:T(8,128)}) custom-call(s32[9]{0:T(128)} %stack.33.at_ref.refs_0_, bf16[1,2,4,96,768]{4,3,2,1,0:T(8,128)(2,1)} %bitcast.266, bf16[1,2,4,96,768]{4,3,2,1,0:T(8,128)(2,1)} %bitcast.296, bf16[1,2,4,96,768]{4,3,2,1,0:T(8,128)(2,1)} %bitcast.297, ...), custom_call_target="tpu_custom_call" | custom-call | flops 1 | bytes 1 | tf_op jit(solution)/shard_map/spread_heads/pallas_call | solution.py:679
  (157 shorter events, 28.8 us)
Async XLA Ops:
  3.8 13.4 %collective-permute-start = (bf16[264,768]{1,0:T(8,128)(2,1)}, bf16[264,768]{1,0:T(8,128)(2,1)}, u32[]{:S(2)}, u32[]{:S(2)}) collective-permute-start(bf16[264,768]{1,0:T(8,128)(2,1)} %pad_maximum_fusion.2), channel_id=1, source_target_pairs={{0,1},{1,0},{2,4},{3,5},{4,2},{5,3},{6,7},{7,6},{8,9},{9,8},{10,12... | collective-permute-start | bytes 1216520 | tf_op jit(solution)/shard_map/ppermute | solution.py:712
  6.8 10.4 %collective-permute-start.1 = (bf16[264,768]{1,0:T(8,128)(2,1)}, bf16[264,768]{1,0:T(8,128)(2,1)}, u32[]{:S(2)}, u32[]{:S(2)}) collective-permute-start(bf16[264,768]{1,0:T(8,128)(2,1)} %pad_maximum_fusion.2), channel_id=1, source_target_pairs={{2,5},{3,4},{4,3},{5,2},{10,13},{11,12},{12,11},{13,10},{18,21},{1... | collective-permute-start | bytes 1216520 | tf_op jit(solution)/shard_map/ppermute | solution.py:712
  18.5 6.0 %copy-start.11 = (bf16[1,256,768]{2,1,0:T(8,128)(2,1)S(1)}, bf16[1,256,768]{2,1,0:T(8,128)(2,1)}, u32[]{:S(2)}) copy-start(bf16[1,256,768]{2,1,0:T(8,128)(2,1)} %param.29) | copy-start | bytes 1179652
  18.5 6.7 %copy-start.22 = (f32[768]{0:T(1024)S(1)}, f32[768]{0:T(1024)}, u32[]{:S(2)}) copy-start(f32[768]{0:T(1024)} %param.18) | copy-start | bytes 9220
  18.5 7.3 %copy-start.23 = (f32[768]{0:T(1024)S(1)}, f32[768]{0:T(1024)}, u32[]{:S(2)}) copy-start(f32[768]{0:T(1024)} %param.24) | copy-start | bytes 9220
  18.6 9.9 %collective-permute-start.2 = (bf16[2,264,768]{2,1,0:T(8,128)(2,1)S(1)}, bf16[2,264,768]{2,1,0:T(8,128)(2,1)S(1)}, u32[]{:S(2)}, u32[]{:S(2)}) collective-permute-start(bf16[2,264,768]{2,1,0:T(8,128)(2,1)S(1)} %pad_maximum_fusion.1), channel_id=1, source_target_pairs={{0,4},{1,5},{2,6},{3,7},{4,0},{5,1},{6,2},{7,3},{8,12},{9,13},{10,... | collective-permute-start | bytes 2433032 | tf_op jit(solution)/shard_map/ppermute | solution.py:510
  24.5 23.2 %collective-permute-start.3 = (bf16[256,768]{1,0:T(8,128)(2,1)S(1)}, bf16[256,768]{1,0:T(8,128)(2,1)S(1)}, u32[]{:S(2)}, u32[]{:S(2)}) collective-permute-start(bf16[256,768]{1,0:T(8,128)(2,1)S(1)} %bitcast.306), channel_id=1, source_target_pairs={{2,4},{3,5},{4,2},{5,3},{10,12},{11,13},{12,10},{13,11},{18,20},{1... | collective-permute-start | bytes 1179656 | tf_op jit(solution)/shard_map/ppermute | solution.py:712
  48.5 19.8 %copy-start.24 = (f32[768]{0:T(1024)S(1)}, f32[768]{0:T(1024)}, u32[]{:S(2)}) copy-start(f32[768]{0:T(1024)} %param.28) | copy-start | bytes 9220
  59.6 21.3 %collective-permute-start.5 = (bf16[2,8,96,768]{3,2,1,0:T(8,128)(2,1)}, bf16[2,8,96,768]{3,2,1,0:T(8,128)(2,1)S(1)}, u32[]{:S(2)}, u32[]{:S(2)}) collective-permute-start(bf16[2,8,96,768]{3,2,1,0:T(8,128)(2,1)} %get-tuple-element.200), channel_id=1, source_target_pairs={{0,4},{1,5},{2,6},{3,7},{4,0},{5,1},{6,2},{7,3},{8,12},{9,13},{10,... | collective-permute-start | bytes 7077896 | tf_op jit(solution)/shard_map/ppermute | solution.py:510
  68.3 15.9 %collective-permute-start.7 = (bf16[2,8,96,768]{3,2,1,0:T(8,128)(2,1)}, bf16[2,8,96,768]{3,2,1,0:T(8,128)(2,1)S(1)}, u32[]{:S(2)}, u32[]{:S(2)}) collective-permute-start(bf16[2,8,96,768]{3,2,1,0:T(8,128)(2,1)} %get-tuple-element.209), channel_id=1, source_target_pairs={{0,4},{1,5},{2,6},{3,7},{4,0},{5,1},{6,2},{7,3},{8,12},{9,13},{10,... | collective-permute-start | bytes 7077896 | tf_op jit(solution)/shard_map/ppermute | solution.py:510
  80.9 3.3 %copy-start.4 = (bf16[2,8,96,768]{3,2,1,0:T(8,128)(2,1)S(1)}, bf16[2,8,96,768]{3,2,1,0:T(8,128)(2,1)}, u32[]{:S(2)}) copy-start(bf16[2,8,96,768]{3,2,1,0:T(8,128)(2,1)} %get-tuple-element.208) | copy-start | bytes 7077892
  82.6 16.7 %collective-permute-start.6 = (bf16[2,2,2,96,768]{4,3,2,1,0:T(8,128)(2,1)S(1)}, bf16[2,2,2,96,768]{4,3,2,1,0:T(8,128)(2,1)}, u32[]{:S(2)}, u32[]{:S(2)}) collective-permute-start(bf16[2,2,2,96,768]{4,3,2,1,0:T(8,128)(2,1)S(1)} %bitcast.298), channel_id=1, source_target_pairs={{0,8},{1,9},{2,10},{3,11},{4,20},{5,21},{6,22},{7,23},{8,0},{9,1},... | collective-permute-start | bytes 3538952 | tf_op jit(solution)/shard_map/ppermute | solution.py:510
  85.5 28.4 %collective-permute-start.9 = (bf16[2,2,2,96,768]{4,3,2,1,0:T(8,128)(2,1)}, bf16[2,2,2,96,768]{4,3,2,1,0:T(8,128)(2,1)}, u32[]{:S(2)}, u32[]{:S(2)}) collective-permute-start(bf16[2,2,2,96,768]{4,3,2,1,0:T(8,128)(2,1)} %fusion.1), channel_id=1, source_target_pairs={{0,1},{1,0},{2,3},{3,2},{4,5},{5,4},{6,7},{7,6},{8,9},{9,8},{10,11... | collective-permute-start | bytes 3538952 | tf_op jit(solution)/shard_map/ppermute | solution.py:510
  101.6 15.4 %collective-permute-start.8 = (bf16[2,2,96,768]{3,2,1,0:T(8,128)(2,1)}, bf16[2,2,96,768]{3,2,1,0:T(8,128)(2,1)}, u32[]{:S(2)}, u32[]{:S(2)}) collective-permute-start(bf16[2,2,96,768]{3,2,1,0:T(8,128)(2,1)} %fusion.4), channel_id=1, source_target_pairs={{0,16},{1,17},{2,18},{3,19},{4,12},{5,13},{6,14},{7,15},{8,24},{9,... | collective-permute-start | bytes 1769480 | tf_op jit(solution)/shard_map/ppermute | solution.py:510
  109.8 21.2 %collective-permute-start.13 = (bf16[2,4,96,768]{3,2,1,0:T(8,128)(2,1)}, bf16[2,4,96,768]{3,2,1,0:T(8,128)(2,1)}, u32[]{:S(2)}, u32[]{:S(2)}) collective-permute-start(bf16[2,4,96,768]{3,2,1,0:T(8,128)(2,1)} %get-tuple-element.235), channel_id=1, source_target_pairs={{0,4},{1,5},{2,6},{3,7},{4,0},{5,1},{6,2},{7,3},{8,12},{9,13},{10,... | collective-permute-start | bytes 3538952 | tf_op jit(solution)/shard_map/ppermute | solution.py:510
  109.8 21.2 %collective-permute-start.14 = (bf16[2,4,96,768]{3,2,1,0:T(8,128)(2,1)}, bf16[2,4,96,768]{3,2,1,0:T(8,128)(2,1)S(1)}, u32[]{:S(2)}, u32[]{:S(2)}) collective-permute-start(bf16[2,4,96,768]{3,2,1,0:T(8,128)(2,1)} %get-tuple-element.236), channel_id=1, source_target_pairs={{0,4},{1,5},{2,6},{3,7},{4,0},{5,1},{6,2},{7,3},{8,12},{9,13},{10,... | collective-permute-start | bytes 3538952 | tf_op jit(solution)/shard_map/ppermute | solution.py:510
  116.0 19.2 %collective-permute-start.12 = (bf16[2,2,96,768]{3,2,1,0:T(8,128)(2,1)}, bf16[2,2,96,768]{3,2,1,0:T(8,128)(2,1)}, u32[]{:S(2)}, u32[]{:S(2)}) collective-permute-start(bf16[2,2,96,768]{3,2,1,0:T(8,128)(2,1)} %fusion.3), channel_id=1, source_target_pairs={{0,8},{1,9},{2,10},{3,11},{4,20},{5,21},{6,22},{7,23},{8,0},{9,1},... | collective-permute-start | bytes 1769480 | tf_op jit(solution)/shard_map/ppermute | solution.py:510
  130.9 6.1 %collective-permute-start.11 = (bf16[512,768]{1,0:T(8,128)(2,1)}, bf16[512,768]{1,0:T(8,128)(2,1)S(1)}, u32[]{:S(2)}, u32[]{:S(2)}) collective-permute-start(bf16[512,768]{1,0:T(8,128)(2,1)} %get-tuple-element.252), channel_id=1, source_target_pairs={{0,4},{1,5},{2,6},{3,7},{4,0},{5,1},{6,2},{7,3},{8,12},{9,13},{10,... | collective-permute-start | bytes 2359304 | tf_op jit(solution)/shard_map/ppermute | solution.py:510
  132.4 2.4 copy-start.21
  132.4 2.4 copy-start.20
  132.4 2.4 copy-start.16
  132.7 4.3 %copy-start.9 = (f32[256,768]{1,0:T(8,128)S(1)}, f32[256,768]{1,0:T(8,128)}, u32[]{:S(2)}) copy-start(f32[256,768]{1,0:T(8,128)} %get-tuple-element.261) | copy-start | bytes 2359300
  132.8 23.1 %collective-permute-start.16 = (bf16[2,2,2,96,768]{4,3,2,1,0:T(8,128)(2,1)S(1)}, bf16[2,2,2,96,768]{4,3,2,1,0:T(8,128)(2,1)S(1)}, u32[]{:S(2)}, u32[]{:S(2)}) collective-permute-start(bf16[2,2,2,96,768]{4,3,2,1,0:T(8,128)(2,1)S(1)} %fusion), channel_id=1, source_target_pairs={{0,8},{1,9},{2,10},{3,11},{4,20},{5,21},{6,22},{7,23},{8,0},{9,1},... | collective-permute-start | bytes 3538952 | tf_op jit(solution)/shard_map/ppermute | solution.py:510
  133.8 32.7 %collective-permute-start.4 = (bf16[256,768]{1,0:T(8,128)(2,1)S(1)}, bf16[256,768]{1,0:T(8,128)(2,1)S(1)}, u32[]{:S(2)}, u32[]{:S(2)}) collective-permute-start(bf16[256,768]{1,0:T(8,128)(2,1)S(1)} %copy-done.13), channel_id=1, source_target_pairs={{2,4},{3,5},{4,2},{5,3},{10,12},{11,13},{12,10},{13,11},{18,20},{1... | collective-permute-start | bytes 1179656 | tf_op jit(solution)/shard_map/ppermute | solution.py:712
  134.8 13.8 %collective-permute-start.10 = (bf16[2,96,768]{2,1,0:T(8,128)(2,1)S(1)}, bf16[2,96,768]{2,1,0:T(8,128)(2,1)S(1)}, u32[]{:S(2)}, u32[]{:S(2)}) collective-permute-start(bf16[2,96,768]{2,1,0:T(8,128)(2,1)S(1)} %copy-done.16), channel_id=1, source_target_pairs={{0,1},{1,0},{2,3},{3,2},{4,5},{5,4},{6,7},{7,6},{8,9},{9,8},{10,11... | collective-permute-start | bytes 884744 | tf_op jit(solution)/shard_map/ppermute | solution.py:510
  136.4 17.6 %collective-permute-start.17 = (bf16[2,96,768]{2,1,0:T(8,128)(2,1)S(1)}, bf16[2,96,768]{2,1,0:T(8,128)(2,1)S(1)}, u32[]{:S(2)}, u32[]{:S(2)}) collective-permute-start(bf16[2,96,768]{2,1,0:T(8,128)(2,1)S(1)} %fusion.6), channel_id=1, source_target_pairs={{0,16},{1,17},{2,18},{3,19},{4,12},{5,13},{6,14},{7,15},{8,24},{9,... | collective-permute-start | bytes 884744 | tf_op jit(solution)/shard_map/ppermute | solution.py:510
  137.0 12.7 %copy-start.5 = (bf16[512,768]{1,0:T(8,128)(2,1)}, bf16[512,768]{1,0:T(8,128)(2,1)S(1)}, u32[]{:S(2)}) copy-start(bf16[512,768]{1,0:T(8,128)(2,1)S(1)} %collective-permute-done.11.core_ref) | copy-start | bytes 2359300
  137.1 30.2 %collective-permute-start.18 = (bf16[256,768]{1,0:T(8,128)(2,1)S(1)}, bf16[256,768]{1,0:T(8,128)(2,1)}, u32[]{:S(2)}, u32[]{:S(2)}) collective-permute-start(bf16[256,768]{1,0:T(8,128)(2,1)S(1)} %add_convert_fusion.2), channel_id=1, source_target_pairs={{0,1},{1,0},{2,3},{3,2},{4,5},{5,4},{6,7},{7,6},{8,9},{9,8},{10,11... | collective-permute-start | bytes 1179656 | tf_op jit(solution)/shard_map/ppermute | solution.py:510
  149.8 14.9 %collective-permute-start.15 = (bf16[96,768]{1,0:T(8,128)(2,1)S(1)}, bf16[96,768]{1,0:T(8,128)(2,1)S(1)}, u32[]{:S(2)}, u32[]{:S(2)}) collective-permute-start(bf16[96,768]{1,0:T(8,128)(2,1)S(1)} %fusion.16), channel_id=1, source_target_pairs={{0,2},{1,3},{2,0},{3,1},{4,6},{5,7},{6,4},{7,5},{8,10},{9,11},{10,... | collective-permute-start | bytes 442376 | tf_op jit(solution)/shard_map/ppermute | solution.py:510
  153.9 1.9 copy-start.14
  155.8 14.9 %collective-permute-start.21 = (bf16[96,768]{1,0:T(8,128)(2,1)}, bf16[96,768]{1,0:T(8,128)(2,1)}, u32[]{:S(2)}, u32[]{:S(2)}) collective-permute-start(bf16[96,768]{1,0:T(8,128)(2,1)} %fusion.15), channel_id=1, source_target_pairs={{0,2},{1,3},{2,0},{3,1},{4,6},{5,7},{6,4},{7,5},{8,10},{9,11},{10,... | collective-permute-start | bytes 442376 | tf_op jit(solution)/shard_map/ppermute | solution.py:510
  159.0 12.9 %collective-permute-start.20 = (bf16[2,2,96,768]{3,2,1,0:T(8,128)(2,1)}, bf16[2,2,96,768]{3,2,1,0:T(8,128)(2,1)}, u32[]{:S(2)}, u32[]{:S(2)}) collective-permute-start(bf16[2,2,96,768]{3,2,1,0:T(8,128)(2,1)} %fusion.2), channel_id=1, source_target_pairs={{0,16},{1,17},{2,18},{3,19},{4,12},{5,13},{6,14},{7,15},{8,24},{9,... | collective-permute-start | bytes 1769480 | tf_op jit(solution)/shard_map/ppermute | solution.py:510
  167.3 3.4 %copy-start.15 = (bf16[2,96,768]{2,1,0:T(8,128)(2,1)S(1)}, bf16[2,96,768]{2,1,0:T(8,128)(2,1)}, u32[]{:S(2)}) copy-start(bf16[2,96,768]{2,1,0:T(8,128)(2,1)} %copy-done.14) | copy-start | bytes 884740
  170.7 3.6 %copy-start.18 = (f32[4,768]{1,0:T(4,128)S(1)}, f32[4,768]{1,0:T(4,128)}, u32[]{:S(2)}) copy-start(f32[4,768]{1,0:T(4,128)} %get-tuple-element.304) | copy-start | bytes 36868
  170.7 3.5 %copy-start.19 = (f32[3,768]{1,0:T(4,128)S(1)}, f32[3,768]{1,0:T(4,128)}, u32[]{:S(2)}) copy-start(f32[3,768]{1,0:T(4,128)} %get-tuple-element.293) | copy-start | bytes 27652
  170.7 4.5 %copy-start.10 = (bf16[96,768]{1,0:T(8,128)(2,1)S(1)}, bf16[96,768]{1,0:T(8,128)(2,1)}, u32[]{:S(2)}) copy-start(bf16[96,768]{1,0:T(8,128)(2,1)} %fusion.14) | copy-start | bytes 442372
  173.2 16.3 %collective-permute-start.22 = (bf16[2,96,768]{2,1,0:T(8,128)(2,1)S(1)}, bf16[2,96,768]{2,1,0:T(8,128)(2,1)S(1)}, u32[]{:S(2)}, u32[]{:S(2)}) collective-permute-start(bf16[2,96,768]{2,1,0:T(8,128)(2,1)S(1)} %fusion.5), channel_id=1, source_target_pairs={{0,1},{1,0},{2,3},{3,2},{4,5},{5,4},{6,7},{7,6},{8,9},{9,8},{10,11... | collective-permute-start | bytes 884744 | tf_op jit(solution)/shard_map/ppermute | solution.py:510
  174.3 5.4 %collective-permute-start.23 = (f32[14,768]{1,0:T(8,128)S(1)}, f32[14,768]{1,0:T(8,128)S(1)}, u32[]{:S(2)}, u32[]{:S(2)}) collective-permute-start(f32[14,768]{1,0:T(8,128)S(1)} %pad_maximum_fusion.4), channel_id=1, source_target_pairs={{0,4},{4,0},{8,12},{12,8},{16,20},{20,16},{24,28},{28,24},{1,5},{5... | collective-permute-start | bytes 129032 | tf_op jit(solution)/shard_map/ppermute | solution.py:622
  175.2 26.8 %collective-permute-start.25 = (bf16[2,1,96,768]{3,2,1,0:T(8,128)(2,1)S(1)}, bf16[2,1,96,768]{3,2,1,0:T(8,128)(2,1)S(1)}, u32[]{:S(2)}, u32[]{:S(2)}) collective-permute-start(bf16[2,1,96,768]{3,2,1,0:T(8,128)(2,1)S(1)} %pad_maximum_fusion.3), channel_id=1, source_target_pairs={{0,1},{1,0},{2,3},{3,2},{4,5},{5,4},{6,7},{7,6},{8,9},{9,8},{10,11... | collective-permute-start | bytes 884744 | tf_op jit(solution)/shard_map/ppermute | solution.py:514
  177.0 25.0 %collective-permute-start.26 = (bf16[2,1,96,768]{3,2,1,0:T(8,128)(2,1)S(1)}, bf16[2,1,96,768]{3,2,1,0:T(8,128)(2,1)S(1)}, u32[]{:S(2)}, u32[]{:S(2)}) collective-permute-start(bf16[2,1,96,768]{3,2,1,0:T(8,128)(2,1)S(1)} %pad_maximum_fusion.3), channel_id=1, source_target_pairs={{0,2},{1,3},{2,0},{3,1},{4,6},{5,7},{6,4},{7,5},{8,10},{9,11},{10,... | collective-permute-start | bytes 884744 | tf_op jit(solution)/shard_map/ppermute | solution.py:514
  178.1 23.9 %collective-permute-start.27 = (bf16[2,1,96,768]{3,2,1,0:T(8,128)(2,1)S(1)}, bf16[2,1,96,768]{3,2,1,0:T(8,128)(2,1)S(1)}, u32[]{:S(2)}, u32[]{:S(2)}) collective-permute-start(bf16[2,1,96,768]{3,2,1,0:T(8,128)(2,1)S(1)} %pad_maximum_fusion.3), channel_id=1, source_target_pairs={{0,3},{1,2},{2,1},{3,0},{4,7},{5,6},{6,5},{7,4},{8,11},{9,10},{10,... | collective-permute-start | bytes 884744 | tf_op jit(solution)/shard_map/ppermute | solution.py:514
  179.7 11.0 %collective-permute-start.28 = (f32[14,768]{1,0:T(8,128)S(1)}, f32[14,768]{1,0:T(8,128)S(1)}, u32[]{:S(2)}, u32[]{:S(2)}) collective-permute-start(f32[14,768]{1,0:T(8,128)S(1)} %add.298), channel_id=1, source_target_pairs={{0,8},{4,12},{8,0},{12,4},{16,24},{20,28},{24,16},{28,20},{1,9},{5... | collective-permute-start | bytes 129032 | tf_op jit(solution)/shard_map/ppermute | solution.py:622
  190.7 4.2 %collective-permute-start.29 = (f32[14,768]{1,0:T(8,128)S(1)}, f32[14,768]{1,0:T(8,128)S(1)}, u32[]{:S(2)}, u32[]{:S(2)}) collective-permute-start(f32[14,768]{1,0:T(8,128)S(1)} %add.303), channel_id=1, source_target_pairs={{0,16},{4,20},{8,24},{12,28},{16,0},{20,4},{24,8},{28,12},{1,17},{... | collective-permute-start | bytes 129032 | tf_op jit(solution)/shard_map/ppermute | solution.py:622
  202.1 16.3 %collective-permute-start.33 = (bf16[2,4,96,768]{3,2,1,0:T(8,128)(2,1)S(1)}, bf16[2,4,96,768]{3,2,1,0:T(8,128)(2,1)S(1)}, u32[]{:S(2)}, u32[]{:S(2)}) collective-permute-start(bf16[2,4,96,768]{3,2,1,0:T(8,128)(2,1)S(1)} %constant_dynamic-update-slice_fusion), channel_id=1, source_target_pairs={{0,16},{1,17},{2,18},{3,19},{4,12},{5,13},{6,14},{7,15},{8,24},{9,... | collective-permute-start | bytes 3538952 | tf_op jit(solution)/shard_map/ppermute | solution.py:510
  202.7 9.1 %collective-permute-start.24 = (bf16[96,768]{1,0:T(8,128)(2,1)S(1)}, bf16[96,768]{1,0:T(8,128)(2,1)S(1)}, u32[]{:S(2)}, u32[]{:S(2)}) collective-permute-start(bf16[96,768]{1,0:T(8,128)(2,1)S(1)} %fusion.10), channel_id=1, source_target_pairs={{0,2},{1,3},{2,0},{3,1},{4,6},{5,7},{6,4},{7,5},{8,10},{9,11},{10,... | collective-permute-start | bytes 442376 | tf_op jit(solution)/shard_map/ppermute | solution.py:510
  208.2 4.8 %collective-permute-start.34 = (f32[14,768]{1,0:T(8,128)S(1)}, f32[14,768]{1,0:T(8,128)S(1)}, u32[]{:S(2)}, u32[]{:S(2)}) collective-permute-start(f32[14,768]{1,0:T(8,128)S(1)} %add.304), channel_id=1, source_target_pairs={{0,1},{1,0},{2,3},{3,2},{4,5},{5,4},{6,7},{7,6},{8,9},{9,8},{10,11... | collective-permute-start | bytes 129032 | tf_op jit(solution)/shard_map/ppermute | solution.py:622
  213.0 5.1 %collective-permute-start.35 = (f32[14,768]{1,0:T(8,128)S(1)}, f32[14,768]{1,0:T(8,128)S(1)}, u32[]{:S(2)}, u32[]{:S(2)}) collective-permute-start(f32[14,768]{1,0:T(8,128)S(1)} %add.310), channel_id=1, source_target_pairs={{0,2},{1,3},{2,0},{3,1},{4,6},{5,7},{6,4},{7,5},{8,10},{9,11},{10,... | collective-permute-start | bytes 129032 | tf_op jit(solution)/shard_map/ppermute | solution.py:622
  218.0 24.6 %copy-start.17 = (f32[14,768]{1,0:T(8,128)}, f32[14,768]{1,0:T(8,128)S(1)}, u32[]{:S(2)}) copy-start(f32[14,768]{1,0:T(8,128)S(1)} %add.311) | copy-start | bytes 129028
  218.5 7.4 %copy-start.12 = (bf16[256,768]{1,0:T(8,128)(2,1)S(1)}, bf16[256,768]{1,0:T(8,128)(2,1)}, u32[]{:S(2)}) copy-start(bf16[256,768]{1,0:T(8,128)(2,1)} %get-tuple-element.340) | copy-start | bytes 1179652
  218.6 24.1 %copy-start.1 = (bf16[2,8,96,768]{3,2,1,0:T(8,128)(2,1)}, bf16[2,8,96,768]{3,2,1,0:T(8,128)(2,1)S(1)}, u32[]{:S(2)}) copy-start(bf16[2,8,96,768]{3,2,1,0:T(8,128)(2,1)S(1)} %constant_dynamic-update-slice_fusion.4) | copy-start | bytes 7077892
  218.6 36.5 %collective-permute-start.39 = (bf16[2,8,96,768]{3,2,1,0:T(8,128)(2,1)S(1)}, bf16[2,8,96,768]{3,2,1,0:T(8,128)(2,1)}, u32[]{:S(2)}, u32[]{:S(2)}) collective-permute-start(bf16[2,8,96,768]{3,2,1,0:T(8,128)(2,1)S(1)} %constant_dynamic-update-slice_fusion.4), channel_id=1, source_target_pairs={{0,8},{1,9},{2,10},{3,11},{4,20},{5,21},{6,22},{7,23},{8,0},{9,1},... | collective-permute-start | bytes 7077896 | tf_op jit(solution)/shard_map/ppermute | solution.py:510
  221.5 6.4 %collective-permute-start.30 = (bf16[1,1,96,768]{3,2,1,0:T(8,128)(2,1)S(1)}, bf16[1,1,96,768]{3,2,1,0:T(8,128)(2,1)S(1)}, u32[]{:S(2)}, u32[]{:S(2)}) collective-permute-start(bf16[1,1,96,768]{3,2,1,0:T(8,128)(2,1)S(1)} %bitcast.300), channel_id=1, source_target_pairs={{0,1},{1,0},{2,3},{3,2},{4,5},{5,4},{6,7},{7,6},{8,9},{9,8},{10,11... | collective-permute-start | bytes 442376 | tf_op jit(solution)/shard_map/ppermute | solution.py:514
  223.5 17.2 %collective-permute-start.31 = (bf16[1,1,96,768]{3,2,1,0:T(8,128)(2,1)S(1)}, bf16[1,1,96,768]{3,2,1,0:T(8,128)(2,1)S(1)}, u32[]{:S(2)}, u32[]{:S(2)}) collective-permute-start(bf16[1,1,96,768]{3,2,1,0:T(8,128)(2,1)S(1)} %bitcast.301), channel_id=1, source_target_pairs={{0,2},{1,3},{2,0},{3,1},{4,6},{5,7},{6,4},{7,5},{8,10},{9,11},{10,... | collective-permute-start | bytes 442376 | tf_op jit(solution)/shard_map/ppermute | solution.py:514
  224.4 16.3 %collective-permute-start.32 = (bf16[1,1,96,768]{3,2,1,0:T(8,128)(2,1)S(1)}, bf16[1,1,96,768]{3,2,1,0:T(8,128)(2,1)S(1)}, u32[]{:S(2)}, u32[]{:S(2)}) collective-permute-start(bf16[1,1,96,768]{3,2,1,0:T(8,128)(2,1)S(1)} %bitcast.302), channel_id=1, source_target_pairs={{0,3},{1,2},{2,1},{3,0},{4,7},{5,6},{6,5},{7,4},{8,11},{9,10},{10,... | collective-permute-start | bytes 442376 | tf_op jit(solution)/shard_map/ppermute | solution.py:514
  225.9 15.4 %collective-permute-start.19 = (bf16[256,768]{1,0:T(8,128)(2,1)S(1)}, bf16[256,768]{1,0:T(8,128)(2,1)S(1)}, u32[]{:S(2)}, u32[]{:S(2)}) collective-permute-start(bf16[256,768]{1,0:T(8,128)(2,1)S(1)} %copy-done.12), channel_id=1, source_target_pairs={{2,4},{3,5},{4,2},{5,3},{10,12},{11,13},{12,10},{13,11},{18,20},{1... | collective-permute-start | bytes 1179656 | tf_op jit(solution)/shard_map/ppermute | solution.py:712
  240.8 14.2 %collective-permute-start.36 = (bf16[1,4,96,768]{3,2,1,0:T(8,128)(2,1)S(1)}, bf16[1,4,96,768]{3,2,1,0:T(8,128)(2,1)S(1)}, u32[]{:S(2)}, u32[]{:S(2)}) collective-permute-start(bf16[1,4,96,768]{3,2,1,0:T(8,128)(2,1)S(1)} %constant_dynamic-update-slice_fusion.6), channel_id=1, source_target_pairs={{0,16},{1,17},{2,18},{3,19},{4,12},{5,13},{6,14},{7,15},{8,24},{9,... | collective-permute-start | bytes 1769480 | tf_op jit(solution)/shard_map/ppermute | solution.py:510
  242.7 14.3 %collective-permute-start.40 = (bf16[2,8,96,768]{3,2,1,0:T(8,128)(2,1)S(1)}, bf16[2,8,96,768]{3,2,1,0:T(8,128)(2,1)}, u32[]{:S(2)}, u32[]{:S(2)}) collective-permute-start(bf16[2,8,96,768]{3,2,1,0:T(8,128)(2,1)S(1)} %constant_dynamic-update-slice_fusion.4), channel_id=1, source_target_pairs={{0,4},{1,5},{2,6},{3,7},{4,0},{5,1},{6,2},{7,3},{8,12},{9,13},{10,... | collective-permute-start | bytes 7077896 | tf_op jit(solution)/shard_map/ppermute | solution.py:510
  255.1 13.4 %copy-start.3 = (bf16[1,8,96,768]{3,2,1,0:T(8,128)(2,1)}, bf16[1,8,96,768]{3,2,1,0:T(8,128)(2,1)S(1)}, u32[]{:S(2)}) copy-start(bf16[1,8,96,768]{3,2,1,0:T(8,128)(2,1)S(1)} %constant_dynamic-update-slice_fusion.10) | copy-start | bytes 3538948
  255.1 4.8 %collective-permute-start.41 = (bf16[2,8,96,768]{3,2,1,0:T(8,128)(2,1)}, bf16[2,8,96,768]{3,2,1,0:T(8,128)(2,1)S(1)}, u32[]{:S(2)}, u32[]{:S(2)}) collective-permute-start(bf16[2,8,96,768]{3,2,1,0:T(8,128)(2,1)} %collective-permute-done.39), channel_id=1, source_target_pairs={{0,4},{1,5},{2,6},{3,7},{4,0},{5,1},{6,2},{7,3},{8,12},{9,13},{10,... | collective-permute-start | bytes 7077896 | tf_op jit(solution)/shard_map/ppermute | solution.py:510
  255.2 20.4 %collective-permute-start.37 = (bf16[1,8,96,768]{3,2,1,0:T(8,128)(2,1)S(1)}, bf16[1,8,96,768]{3,2,1,0:T(8,128)(2,1)S(1)}, u32[]{:S(2)}, u32[]{:S(2)}) collective-permute-start(bf16[1,8,96,768]{3,2,1,0:T(8,128)(2,1)S(1)} %constant_dynamic-update-slice_fusion.10), channel_id=1, source_target_pairs={{0,8},{1,9},{2,10},{3,11},{4,20},{5,21},{6,22},{7,23},{8,0},{9,1},... | collective-permute-start | bytes 3538952 | tf_op jit(solution)/shard_map/ppermute | solution.py:510
  256.7 19.1 %collective-permute-start.38 = (bf16[1,8,96,768]{3,2,1,0:T(8,128)(2,1)S(1)}, bf16[1,8,96,768]{3,2,1,0:T(8,128)(2,1)S(1)}, u32[]{:S(2)}, u32[]{:S(2)}) collective-permute-start(bf16[1,8,96,768]{3,2,1,0:T(8,128)(2,1)S(1)} %constant_dynamic-update-slice_fusion.10), channel_id=1, source_target_pairs={{0,4},{1,5},{2,6},{3,7},{4,0},{5,1},{6,2},{7,3},{8,12},{9,13},{10,... | collective-permute-start | bytes 3538952 | tf_op jit(solution)/shard_map/ppermute | solution.py:510
  275.6 2.9 %copy-start.6 = (bf16[1,8,96,768]{3,2,1,0:T(8,128)(2,1)}, bf16[1,8,96,768]{3,2,1,0:T(8,128)(2,1)S(1)}, u32[]{:S(2)}) copy-start(bf16[1,8,96,768]{3,2,1,0:T(8,128)(2,1)S(1)} %collective-permute-done.37) | copy-start | bytes 3538948
  275.6 2.9 %collective-permute-start.42 = (bf16[1,8,96,768]{3,2,1,0:T(8,128)(2,1)S(1)}, bf16[1,8,96,768]{3,2,1,0:T(8,128)(2,1)S(1)}, u32[]{:S(2)}, u32[]{:S(2)}) collective-permute-start(bf16[1,8,96,768]{3,2,1,0:T(8,128)(2,1)S(1)} %collective-permute-done.37), channel_id=1, source_target_pairs={{0,4},{1,5},{2,6},{3,7},{4,0},{5,1},{6,2},{7,3},{8,12},{9,13},{10,... | collective-permute-start | bytes 3538952 | tf_op jit(solution)/shard_map/ppermute | solution.py:510
  275.8 2.7 copy-start.7
  (4 other events, 5.1 us)

commit v4 on v3

--- a/solution.py
+++ b/solution.py
@@ -85,8 +85,9 @@
         q_t = (rotated(query, head, rows) * HEAD_DIM**-0.5).astype(BF)
         k_t = rotated(keys, head, first.shape[0])
         q_out[at, :] = q_t
-        k_out[at, :] = k_t.astype(BF)
-        scores = dot(k_t.T.astype(BF), q_t, NN)
+        k_t = k_t.astype(BF)
+        k_out[at, :] = k_t
+        scores = dot(k_t.T, q_t, NN)
         top = jnp.max(scores, axis=0, keepdims=True)
         weights = jnp.exp(scores - top)
         total = jnp.sum(weights, axis=0, keepdims=True)
@@ -166,7 +167,7 @@
 ):
     @pl.when(pl.program_id(0) == 0)
     def _():
-        attended = o_ref[...].T.astype(BF)
+        attended = o_ref[...].astype(BF).T
         rows = o_ref.shape[1]
         residual = x_ref[0, :rows].astype(F32) + start_flag(x_ref, rows) * start_ref[...]
         middle = residual + dot(attended, w_out_ref[...], NN) + b_out_ref[...]
@@ -174,7 +175,7 @@
         unit, _ = unit_norm(middle)
         second = unit * gain_ref[1:2, :] + shift_ref[1:2, :]
         second_ref[...] = second.astype(BF)
-        second_t_ref[...] = second.T.astype(BF)
+        second_t_ref[...] = second.astype(BF).T
         acc_ref[...] = jnp.zeros_like(acc_ref)
         gsec_ref[...] = jnp.zeros_like(gsec_ref)
 
@@ -801,7 +802,6 @@
     tokens_moved = homes.move(grad_tokens, None, (1, 2))
     feed.double(chain)
     heads.double(chain)
-    grad_tokens = chain.then(lambda a, b: jnp.where(native, a, b), grad_tokens, tokens_moved)
 
     def settled(smalls):
         gain_1, shift_1, grad_bout, grad_bdown = smalls[:4]
@@ -818,6 +818,7 @@
         )
 
     small_outs = chain.then(settled, smalls)
+    grad_tokens = chain.then(lambda a, b: jnp.where(native, a, b), grad_tokens, tokens_moved)
     heads.double(chain)
     feed.cross(chain)
     (grad_down,) = feed.spread(chain, "down", 0)

time: 289 us -> 289 us (level)
  starting transfers between devices: 67.4 us -> 58.9 us
  waiting for transfers between devices: 64 us -> 71.9 us
    ppermute x27, starting transfers between devices: 45.9 us -> 38.2 us  [swap(): return lax.ppermute(value, ('dp', 'seq'), pairs)]
    ppermute x27, waiting for transfers between devices: 36.1 us -> 42.7 us  [swap(): return lax.ppermute(value, ('dp', 'seq'), pairs)]
    unnamed x63 -> x61, local copies, waits for them, and re-layouts: 7.28 us -> 7.26 us
  transfers between devices with their start and end apart: 43 -> 43, of which waited for: 14 -> 15; matrix products, arithmetic and copies ran while one was open for 16% -> 17% of each run, Pallas kernels for 28% -> 28%
where the time goes in v4:
time: 289 us; the launch traced here: 287 us
  Pallas kernels  98.1 us (34%)
  waiting for transfers between devices  71.9 us (25%)
  starting transfers between devices  58.9 us (20%)
  other arithmetic  32 us (11%)
  local copies, waits for them, and re-layouts  24.4 us (8%)
    ppermute x27, waiting for transfers between devices, swap(): return lax.ppermute(value, ('dp', 'seq'), pairs)  42.7 us
    ppermute x27, starting transfers between devices, swap(): return lax.ppermute(value, ('dp', 'seq'), pairs)  38.2 us
    convert_element_type x15, other arithmetic, add_up(): return sum((p.astype(F32) for p in parts)).astype(BF)  22.6 us
    pallas_call x3, Pallas kernels, spread(): pl.pallas_call(lambda *refs: spread_kernel(kind, *refs), grid_spec=pltpu....  21.8 us
    ppermute x6, waiting for transfers between devices, swap_seq(): return lax.ppermute(value, 'seq', xor_pairs(lax.axis_size('seq'), mask))  20.5 us
    pallas_call x1, Pallas kernels, attention_forward(): pl.pallas_call(forward_kernel, grid=(HEADS // HEADS_PER_STEP,), in_specs=...  17.7 us
    pallas_call x1, Pallas kernels, attention_backward(): pl.pallas_call(backward_kernel, grid=(HEADS // HEADS_PER_STEP,), in_specs...  13.8 us
    pallas_call x1, Pallas kernels, feed_forward(): pl.pallas_call(feed_second_kernel, grid_spec=pltpu.PrefetchScalarGridSpec...  11.9 us
  transfers between devices with their start and end apart: 43, of which 15 were waited for; matrix products, arithmetic and copies ran while one was open for 17% of the time, Pallas kernels for 28%

profile of v4, /device:TPU:0, one launch (start us, length us, event | category | flops | bytes accessed | tf_op | source)
XLA Modules:
  0.0 287.5 jit_solution(8632619141100112286)
XLA Ops:
  2.0 1.8 pad_maximum_fusion.2
  3.8 3.0 %collective-permute-start = (bf16[264,768]{1,0:T(8,128)(2,1)}, bf16[264,768]{1,0:T(8,128)(2,1)}, u32[]{:S(2)}, u32[]{:S(2)}) collective-permute-start(bf16[264,768]{1,0:T(8,128)(2,1)} %pad_maximum_fusion.2), channel_id=1, source_target_pairs={{0,1},{1,0},{2,4},{3,5},{4,2},{5,3},{6,7},{7,6},{8,9},{9,8},{10,12... | collective-permute-start | bytes 1216520 | tf_op jit(solution)/shard_map/ppermute | solution.py:713
  6.8 1.4 collective-permute-start.1
  8.2 4.5 %copy.32 = bf16[768,2304]{0,1:T(8,128)(2,1)S(1)} copy(bf16[768,2304]{1,0:T(8,128)(2,1)} %param.21) | data formatting | bytes 7077888 | tf_op args[6]
  12.7 2.0 copy.33
  15.7 1.6 collective-permute-done
  17.2 1.3 select_bitcast_fusion.1
  18.6 5.9 %collective-permute-start.2 = (bf16[2,264,768]{2,1,0:T(8,128)(2,1)S(1)}, bf16[2,264,768]{2,1,0:T(8,128)(2,1)S(1)}, u32[]{:S(2)}, u32[]{:S(2)}) collective-permute-start(bf16[2,264,768]{2,1,0:T(8,128)(2,1)S(1)} %pad_maximum_fusion.1), channel_id=1, source_target_pairs={{0,4},{1,5},{2,6},{3,7},{4,0},{5,1},{6,2},{7,3},{8,12},{9,13},{10,... | collective-permute-start | bytes 2433032 | tf_op jit(solution)/shard_map/ppermute | solution.py:511
  27.1 1.4 copy.35.b_ref
  28.8 1.2 multiply_sine_fusion
  30.0 17.7 %attention_forward.1 = (bf16[768,256]{1,0:T(8,128)(2,1)}, bf16[768,1024]{1,0:T(8,128)(2,1)}, bf16[768,1024]{1,0:T(8,128)(2,1)}, bf16[12,1024,256]{2,1,0:T(8,128)...) custom-call(bf16[4,264,768]{2,1,0:T(8,128)(2,1)} %copy-done, f32[1,768]{1,0:T(1,128)} %broadcast_in_dim.30.shift_in_ref.start_ref, ...), custom_call_target="tpu_custom_call" | custom-call | flops 1 | bytes 1 | tf_op jit(solution)/shard_map/attention_forward/pallas_call | solution.py:104
  48.5 11.0 %feed_first.1 = (f32[256,768]{1,0:T(8,128)}, bf16[256,768]{1,0:T(8,128)(2,1)}, bf16[768,256]{1,0:T(8,128)(2,1)}, f32[256,768]{1,0:T(8,128)}, f32[256,768]{1,0:T(...) custom-call(s32[9]{0:T(128)} %stack.33.at_ref.refs_0_, ...), custom_call_target="tpu_custom_call" | custom-call | flops 1 | bytes 1 | tf_op jit(solution)/shard_map/feed_first/pallas_call | solution.py:255
  59.5 8.7 %collective-permute-start.5 = (bf16[2,8,96,768]{3,2,1,0:T(8,128)(2,1)}, bf16[2,8,96,768]{3,2,1,0:T(8,128)(2,1)S(1)}, u32[]{:S(2)}, u32[]{:S(2)}) collective-permute-start(bf16[2,8,96,768]{3,2,1,0:T(8,128)(2,1)} %get-tuple-element.200), channel_id=1, source_target_pairs={{0,4},{1,5},{2,6},{3,7},{4,0},{5,1},{6,2},{7,3},{8,12},{9,13},{10,... | collective-permute-start | bytes 7077896 | tf_op jit(solution)/shard_map/ppermute | solution.py:511
  68.9 11.9 %feed_second.1 = (bf16[256,768]{1,0:T(8,128)(2,1)}, f32[256,768]{1,0:T(8,128)}, bf16[256,768]{1,0:T(8,128)(2,1)}, bf16[768,256]{1,0:T(8,128)(2,1)}, bf16[2,8,96,...) custom-call(s32[9]{0:T(128)} %stack.33.at_ref.refs_0_, ...), custom_call_target="tpu_custom_call" | custom-call | flops 1 | bytes 1 | tf_op jit(solution)/shard_map/feed_second/pallas_call | solution.py:274
  80.8 1.7 add_convert_fusion.1
  82.5 1.6 collective-permute-start.6
  84.1 1.3 fusion.1
  85.4 13.8 %attention_backward.1 = (bf16[256,768]{1,0:T(8,128)(2,1)}, bf16[1024,768]{1,0:T(8,128)(2,1)}, bf16[1024,768]{1,0:T(8,128)(2,1)}, f32[3,8,768]{2,1,0:T(8,128)}) custom-call(bf16[768,256]{1,0:T(8,128)(2,1)} %get-tuple-element.212.q_ref, bf16[768,1024]{1,0:T(8,128)(2,1)} %get-tuple-element.213.k_ref, bf16[768,1024]{1,0:T(8,128)(2,1)} %get-tuple-element.214.v_ref, ...), custom_call_target="tpu_custom_call" | custom-call | flops 1 | bytes 1 | tf_op jit(solution)/shard_map/attention_backward/pallas_call | solution.py:336
  99.2 2.3 fusion.4
  101.5 1.5 collective-permute-start.8
  103.0 6.7 %heads_first.1 = (bf16[2,4,96,768]{3,2,1,0:T(8,128)(2,1)}, bf16[2,4,96,768]{3,2,1,0:T(8,128)(2,1)}) custom-call(s32[9]{0:T(128)} %stack.33.at_ref.refs_0_, bf16[256,768]{1,0:T(8,128)(2,1)} %get-tuple-element.244.gq_ref, bf16[1024,768]{1,0:T(8,128)(2,1)} %get-tuple-element.245.gk_ref, bf16[1024,768]{1,0:T(8,128)(2,1)} %get-tuple-element.246.gv_ref, ...), custom_call_target="tpu_custom_call" | custom-call | flops 1 | bytes 1 | tf_op jit(solution)/shard_map/heads_first/pallas_call | solution.py:427
  110.2 3.6 %collective-permute-done.9 = bf16[2,2,2,96,768]{4,3,2,1,0:T(8,128)(2,1)} collective-permute-done((bf16[2,2,2,96,768]{4,3,2,1,0:T(8,128)(2,1)}, bf16[2,2,2,96,768]{4,3,2,1,0:T(8,128)(2,1)}, u32[]{:S(2)}, u32[]{:S(2)}) %collective-permute-start.9) | collective-permute-done | bytes 1179680 | tf_op jit(solution)/shard_map/ppermute | solution.py:511
  113.8 2.1 fusion.3
  117.0 2.0 fusion.7
  119.0 11.9 %heads_second.1 = (bf16[4,4,96,768]{3,2,1,0:T(8,128)(2,1)}, f32[256,768]{1,0:T(8,128)}, f32[256,768]{1,0:T(8,128)}, bf16[512,768]{1,0:T(8,128)(2,1)}) custom-call(s32[9]{0:T(128)} %stack.33.at_ref.refs_0_, bf16[256,768]{1,0:T(8,128)(2,1)} %get-tuple-element.244.gq_ref, bf16[1024,768]{1,0:T(8,128)(2,1)} %get-tuple-element.245.gk_ref, ...), custom_call_target="tpu_custom_call" | custom-call | flops 10000000000 | bytes 30000000 | tf_op jit(solution)/shard_map/heads_second/pallas_call | solution.py:444
  131.0 1.4 slice.219
  135.1 1.2 fusion.6
  137.1 2.1 collective-permute-start.18
  139.1 9.4 %collective-permute-done.10 = bf16[2,96,768]{2,1,0:T(8,128)(2,1)S(1)} collective-permute-done((bf16[2,96,768]{2,1,0:T(8,128)(2,1)S(1)}, bf16[2,96,768]{2,1,0:T(8,128)(2,1)S(1)}, u32[]{:S(2)}, u32[]{:S(2)}) %collective-permute-start.10) | collective-permute-done | bytes 294944 | tf_op jit(solution)/shard_map/ppermute | solution.py:511
  149.7 4.1 %collective-permute-start.15 = (bf16[96,768]{1,0:T(8,128)(2,1)S(1)}, bf16[96,768]{1,0:T(8,128)(2,1)S(1)}, u32[]{:S(2)}, u32[]{:S(2)}) collective-permute-start(bf16[96,768]{1,0:T(8,128)(2,1)S(1)} %fusion.16), channel_id=1, source_target_pairs={{0,2},{1,3},{2,0},{3,1},{4,6},{5,7},{6,4},{7,5},{8,10},{9,11},{10,... | collective-permute-start | bytes 442376 | tf_op jit(solution)/shard_map/ppermute | solution.py:511
  153.8 1.8 fusion.15
  156.8 2.1 fusion.2
  158.9 1.2 collective-permute-start.22
  160.1 4.4 %collective-permute-done.15 = bf16[96,768]{1,0:T(8,128)(2,1)S(1)} collective-permute-done((bf16[96,768]{1,0:T(8,128)(2,1)S(1)}, bf16[96,768]{1,0:T(8,128)(2,1)S(1)}, u32[]{:S(2)}, u32[]{:S(2)}) %collective-permute-start.15) | collective-permute-done | bytes 147488 | tf_op jit(solution)/shard_map/ppermute | solution.py:511
  164.5 1.8 fusion.14
  167.2 3.4 %entry_backward.1 = (bf16[256,768]{1,0:T(8,128)(2,1)}, f32[3,768]{1,0:T(4,128)}) custom-call(f32[256,768]{1,0:T(8,128)} %get-tuple-element.285.own_ref, bf16[512,768]{1,0:T(8,128)(2,1)} %copy-done.5, bf16[256,768]{1,0:T(8,128)(2,1)} %collective-permute-done.18.near_ref, bf16[4,264,768]{2,1,0:T(8,128)(2,1)} %copy-done, ...), custom_call_target="tpu_custom_call" | custom-call | flops 1 | bytes 1 | tf_op jit(solution)/shard_map/entry_backward/pallas_call | solution.py:477
  170.6 1.2 fusion.12
  171.8 1.3 fusion.5
  175.1 1.8 collective-permute-start.28
  178.1 1.5 collective-permute-start.30
  180.5 8.9 %collective-permute-done.24 = bf16[2,96,768]{2,1,0:T(8,128)(2,1)S(1)} collective-permute-done((bf16[2,96,768]{2,1,0:T(8,128)(2,1)S(1)}, bf16[2,96,768]{2,1,0:T(8,128)(2,1)S(1)}, u32[]{:S(2)}, u32[]{:S(2)}) %collective-permute-start.24) | collective-permute-done | bytes 294944 | tf_op jit(solution)/shard_map/ppermute | solution.py:511
  190.6 1.6 collective-permute-start.25
  192.2 2.5 collective-permute-done.25
  194.7 7.2 %collective-permute-done.28 = bf16[2,1,96,768]{3,2,1,0:T(8,128)(2,1)S(1)} collective-permute-done((bf16[2,1,96,768]{3,2,1,0:T(8,128)(2,1)S(1)}, bf16[2,1,96,768]{3,2,1,0:T(8,128)(2,1)S(1)}, u32[]{:S(2)}, u32[]{:S(2)}) %collective-permute-start.28) | collective-permute-done | bytes 294944 | tf_op jit(solution)/shard_map/ppermute | solution.py:515
  202.8 5.3 %collective-permute-start.27 = (bf16[96,768]{1,0:T(8,128)(2,1)S(1)}, bf16[96,768]{1,0:T(8,128)(2,1)S(1)}, u32[]{:S(2)}, u32[]{:S(2)}) collective-permute-start(bf16[96,768]{1,0:T(8,128)(2,1)S(1)} %fusion.10), channel_id=1, source_target_pairs={{0,2},{1,3},{2,0},{3,1},{4,6},{5,7},{6,4},{7,5},{8,10},{9,11},{10,... | collective-permute-start | bytes 442376 | tf_op jit(solution)/shard_map/ppermute | solution.py:511
  208.1 5.3 %collective-permute-done.27 = bf16[96,768]{1,0:T(8,128)(2,1)S(1)} collective-permute-done((bf16[96,768]{1,0:T(8,128)(2,1)S(1)}, bf16[96,768]{1,0:T(8,128)(2,1)S(1)}, u32[]{:S(2)}, u32[]{:S(2)}) %collective-permute-start.27) | collective-permute-done | bytes 147488 | tf_op jit(solution)/shard_map/ppermute | solution.py:511
  213.4 1.2 fusion.9
  215.5 4.6 %collective-permute-done.31 = f32[14,768]{1,0:T(8,128)S(1)} collective-permute-done((f32[14,768]{1,0:T(8,128)S(1)}, f32[14,768]{1,0:T(8,128)S(1)}, u32[]{:S(2)}, u32[]{:S(2)}) %collective-permute-start.31) | collective-permute-done | bytes 43040 | tf_op jit(solution)/shard_map/ppermute | solution.py:623
  221.4 2.1 collective-permute-start.32
  224.3 1.5 collective-permute-start.34
  225.9 1.4 collective-permute-start.19
  227.8 12.8 %collective-permute-done.33 = bf16[1,1,96,768]{3,2,1,0:T(8,128)(2,1)S(1)} collective-permute-done((bf16[1,1,96,768]{3,2,1,0:T(8,128)(2,1)S(1)}, bf16[1,1,96,768]{3,2,1,0:T(8,128)(2,1)S(1)}, u32[]{:S(2)}, u32[]{:S(2)}) %collective-permute-start.33) | collective-permute-done | bytes 147488 | tf_op jit(solution)/shard_map/ppermute | solution.py:515
  241.9 1.4 reshape.346
  243.3 1.4 copy.63
  244.6 1.4 reshape.347
  246.7 1.6 slice_reduce_fusion
  248.8 1.8 broadcast_select_fusion
  251.7 3.9 %collective-permute-done.39 = bf16[2,8,96,768]{3,2,1,0:T(8,128)(2,1)} collective-permute-done((bf16[2,8,96,768]{3,2,1,0:T(8,128)(2,1)S(1)}, bf16[2,8,96,768]{3,2,1,0:T(8,128)(2,1)}, u32[]{:S(2)}, u32[]{:S(2)}) %collective-permute-start.39) | collective-permute-done | bytes 2359328 | tf_op jit(solution)/shard_map/ppermute | solution.py:511
  256.9 3.5 %collective-permute-done.41 = bf16[2,8,96,768]{3,2,1,0:T(8,128)(2,1)S(1)} collective-permute-done((bf16[2,8,96,768]{3,2,1,0:T(8,128)(2,1)}, bf16[2,8,96,768]{3,2,1,0:T(8,128)(2,1)S(1)}, u32[]{:S(2)}, u32[]{:S(2)}) %collective-permute-start.41) | collective-permute-done | bytes 2359328 | tf_op jit(solution)/shard_map/ppermute | solution.py:511
  260.3 1.4 copy-done.2
  261.7 7.1 %spread_down.1 = f32[2,2,4,2,96,768]{5,4,3,2,1,0:T(8,128)} custom-call(s32[9]{0:T(128)} %stack.33.at_ref.refs_0_, bf16[2,4,2,96,768]{4,3,2,1,0:T(8,128)(2,1)} %bitcast.256, bf16[2,4,2,96,768]{4,3,2,1,0:T(8,128)(2,1)} %bitcast.101.refs_2_, bf16[2,4,2,96,768]{4,3,2,1,0:T(8,128)(2,1)} %bitcast.102.refs_3_, bf16[2,4,2,96,768]{4,3,2,1,0:T(8,128)(2,1)} %bitcast.263), custom_call_target="tpu_custom_call" | custom-call | flops 1 | bytes 1 | tf_op jit(solution)/shard_map/spread_down/pallas_call | solution.py:680
  268.9 7.1 %spread_up.1 = f32[4,2,96,3072]{3,2,1,0:T(8,128)} custom-call(s32[9]{0:T(128)} %stack.33.at_ref.refs_0_, bf16[2,4,2,96,768]{4,3,2,1,0:T(8,128)(2,1)} %bitcast.257, bf16[2,4,2,96,768]{4,3,2,1,0:T(8,128)(2,1)} %bitcast.106.refs_2_, bf16[2,4,2,96,768]{4,3,2,1,0:T(8,128)(2,1)} %bitcast.107.refs_3_, bf16[2,4,2,96,768]{4,3,2,1,0:T(8,128)(2,1)} %bitcast.264), custom_call_target="tpu_custom_call" | custom-call | flops 1 | bytes 1 | tf_op jit(solution)/shard_map/spread_up/pallas_call | solution.py:680
  276.3 2.7 collective-permute-done.42
  280.0 7.5 %spread_heads.1 = (f32[2,2,2,96,2304]{4,3,2,1,0:T(8,128)}, f32[2,2,2,96,768]{4,3,2,1,0:T(8,128)}) custom-call(s32[9]{0:T(128)} %stack.33.at_ref.refs_0_, bf16[1,2,4,96,768]{4,3,2,1,0:T(8,128)(2,1)} %bitcast.266, bf16[1,2,4,96,768]{4,3,2,1,0:T(8,128)(2,1)} %bitcast.296, bf16[1,2,4,96,768]{4,3,2,1,0:T(8,128)(2,1)} %bitcast.297, ...), custom_call_target="tpu_custom_call" | custom-call | flops 1 | bytes 1 | tf_op jit(solution)/shard_map/spread_heads/pallas_call | solution.py:680
  (155 shorter events, 29.6 us)
Async XLA Ops:
  3.8 13.4 %collective-permute-start = (bf16[264,768]{1,0:T(8,128)(2,1)}, bf16[264,768]{1,0:T(8,128)(2,1)}, u32[]{:S(2)}, u32[]{:S(2)}) collective-permute-start(bf16[264,768]{1,0:T(8,128)(2,1)} %pad_maximum_fusion.2), channel_id=1, source_target_pairs={{0,1},{1,0},{2,4},{3,5},{4,2},{5,3},{6,7},{7,6},{8,9},{9,8},{10,12... | collective-permute-start | bytes 1216520 | tf_op jit(solution)/shard_map/ppermute | solution.py:713
  6.8 10.4 %collective-permute-start.1 = (bf16[264,768]{1,0:T(8,128)(2,1)}, bf16[264,768]{1,0:T(8,128)(2,1)}, u32[]{:S(2)}, u32[]{:S(2)}) collective-permute-start(bf16[264,768]{1,0:T(8,128)(2,1)} %pad_maximum_fusion.2), channel_id=1, source_target_pairs={{2,5},{3,4},{4,3},{5,2},{10,13},{11,12},{12,11},{13,10},{18,21},{1... | collective-permute-start | bytes 1216520 | tf_op jit(solution)/shard_map/ppermute | solution.py:713
  18.5 6.0 %copy-start.11 = (bf16[1,256,768]{2,1,0:T(8,128)(2,1)S(1)}, bf16[1,256,768]{2,1,0:T(8,128)(2,1)}, u32[]{:S(2)}) copy-start(bf16[1,256,768]{2,1,0:T(8,128)(2,1)} %param.29) | copy-start | bytes 1179652
  18.5 6.7 %copy-start.21 = (f32[768]{0:T(1024)S(1)}, f32[768]{0:T(1024)}, u32[]{:S(2)}) copy-start(f32[768]{0:T(1024)} %param.18) | copy-start | bytes 9220
  18.5 7.3 %copy-start.22 = (f32[768]{0:T(1024)S(1)}, f32[768]{0:T(1024)}, u32[]{:S(2)}) copy-start(f32[768]{0:T(1024)} %param.24) | copy-start | bytes 9220
  18.6 9.9 %collective-permute-start.2 = (bf16[2,264,768]{2,1,0:T(8,128)(2,1)S(1)}, bf16[2,264,768]{2,1,0:T(8,128)(2,1)S(1)}, u32[]{:S(2)}, u32[]{:S(2)}) collective-permute-start(bf16[2,264,768]{2,1,0:T(8,128)(2,1)S(1)} %pad_maximum_fusion.1), channel_id=1, source_target_pairs={{0,4},{1,5},{2,6},{3,7},{4,0},{5,1},{6,2},{7,3},{8,12},{9,13},{10,... | collective-permute-start | bytes 2433032 | tf_op jit(solution)/shard_map/ppermute | solution.py:511
  24.5 23.2 %collective-permute-start.3 = (bf16[256,768]{1,0:T(8,128)(2,1)S(1)}, bf16[256,768]{1,0:T(8,128)(2,1)S(1)}, u32[]{:S(2)}, u32[]{:S(2)}) collective-permute-start(bf16[256,768]{1,0:T(8,128)(2,1)S(1)} %bitcast.306), channel_id=1, source_target_pairs={{2,4},{3,5},{4,2},{5,3},{10,12},{11,13},{12,10},{13,11},{18,20},{1... | collective-permute-start | bytes 1179656 | tf_op jit(solution)/shard_map/ppermute | solution.py:713
  48.5 19.8 %copy-start.23 = (f32[768]{0:T(1024)S(1)}, f32[768]{0:T(1024)}, u32[]{:S(2)}) copy-start(f32[768]{0:T(1024)} %param.28) | copy-start | bytes 9220
  59.5 21.3 %collective-permute-start.5 = (bf16[2,8,96,768]{3,2,1,0:T(8,128)(2,1)}, bf16[2,8,96,768]{3,2,1,0:T(8,128)(2,1)S(1)}, u32[]{:S(2)}, u32[]{:S(2)}) collective-permute-start(bf16[2,8,96,768]{3,2,1,0:T(8,128)(2,1)} %get-tuple-element.200), channel_id=1, source_target_pairs={{0,4},{1,5},{2,6},{3,7},{4,0},{5,1},{6,2},{7,3},{8,12},{9,13},{10,... | collective-permute-start | bytes 7077896 | tf_op jit(solution)/shard_map/ppermute | solution.py:511
  68.2 15.9 %collective-permute-start.7 = (bf16[2,8,96,768]{3,2,1,0:T(8,128)(2,1)}, bf16[2,8,96,768]{3,2,1,0:T(8,128)(2,1)S(1)}, u32[]{:S(2)}, u32[]{:S(2)}) collective-permute-start(bf16[2,8,96,768]{3,2,1,0:T(8,128)(2,1)} %get-tuple-element.209), channel_id=1, source_target_pairs={{0,4},{1,5},{2,6},{3,7},{4,0},{5,1},{6,2},{7,3},{8,12},{9,13},{10,... | collective-permute-start | bytes 7077896 | tf_op jit(solution)/shard_map/ppermute | solution.py:511
  80.8 3.3 %copy-start.4 = (bf16[2,8,96,768]{3,2,1,0:T(8,128)(2,1)S(1)}, bf16[2,8,96,768]{3,2,1,0:T(8,128)(2,1)}, u32[]{:S(2)}) copy-start(bf16[2,8,96,768]{3,2,1,0:T(8,128)(2,1)} %get-tuple-element.208) | copy-start | bytes 7077892
  82.5 16.7 %collective-permute-start.6 = (bf16[2,2,2,96,768]{4,3,2,1,0:T(8,128)(2,1)S(1)}, bf16[2,2,2,96,768]{4,3,2,1,0:T(8,128)(2,1)}, u32[]{:S(2)}, u32[]{:S(2)}) collective-permute-start(bf16[2,2,2,96,768]{4,3,2,1,0:T(8,128)(2,1)S(1)} %bitcast.298), channel_id=1, source_target_pairs={{0,8},{1,9},{2,10},{3,11},{4,20},{5,21},{6,22},{7,23},{8,0},{9,1},... | collective-permute-start | bytes 3538952 | tf_op jit(solution)/shard_map/ppermute | solution.py:511
  85.4 28.4 %collective-permute-start.9 = (bf16[2,2,2,96,768]{4,3,2,1,0:T(8,128)(2,1)}, bf16[2,2,2,96,768]{4,3,2,1,0:T(8,128)(2,1)}, u32[]{:S(2)}, u32[]{:S(2)}) collective-permute-start(bf16[2,2,2,96,768]{4,3,2,1,0:T(8,128)(2,1)} %fusion.1), channel_id=1, source_target_pairs={{0,1},{1,0},{2,3},{3,2},{4,5},{5,4},{6,7},{7,6},{8,9},{9,8},{10,11... | collective-permute-start | bytes 3538952 | tf_op jit(solution)/shard_map/ppermute | solution.py:511
  101.5 15.5 %collective-permute-start.8 = (bf16[2,2,96,768]{3,2,1,0:T(8,128)(2,1)}, bf16[2,2,96,768]{3,2,1,0:T(8,128)(2,1)}, u32[]{:S(2)}, u32[]{:S(2)}) collective-permute-start(bf16[2,2,96,768]{3,2,1,0:T(8,128)(2,1)} %fusion.4), channel_id=1, source_target_pairs={{0,16},{1,17},{2,18},{3,19},{4,12},{5,13},{6,14},{7,15},{8,24},{9,... | collective-permute-start | bytes 1769480 | tf_op jit(solution)/shard_map/ppermute | solution.py:511
  109.7 21.3 %collective-permute-start.13 = (bf16[2,4,96,768]{3,2,1,0:T(8,128)(2,1)}, bf16[2,4,96,768]{3,2,1,0:T(8,128)(2,1)}, u32[]{:S(2)}, u32[]{:S(2)}) collective-permute-start(bf16[2,4,96,768]{3,2,1,0:T(8,128)(2,1)} %get-tuple-element.235), channel_id=1, source_target_pairs={{0,4},{1,5},{2,6},{3,7},{4,0},{5,1},{6,2},{7,3},{8,12},{9,13},{10,... | collective-permute-start | bytes 3538952 | tf_op jit(solution)/shard_map/ppermute | solution.py:511
  109.7 21.3 %collective-permute-start.14 = (bf16[2,4,96,768]{3,2,1,0:T(8,128)(2,1)}, bf16[2,4,96,768]{3,2,1,0:T(8,128)(2,1)S(1)}, u32[]{:S(2)}, u32[]{:S(2)}) collective-permute-start(bf16[2,4,96,768]{3,2,1,0:T(8,128)(2,1)} %get-tuple-element.236), channel_id=1, source_target_pairs={{0,4},{1,5},{2,6},{3,7},{4,0},{5,1},{6,2},{7,3},{8,12},{9,13},{10,... | collective-permute-start | bytes 3538952 | tf_op jit(solution)/shard_map/ppermute | solution.py:511
  115.9 19.2 %collective-permute-start.12 = (bf16[2,2,96,768]{3,2,1,0:T(8,128)(2,1)}, bf16[2,2,96,768]{3,2,1,0:T(8,128)(2,1)}, u32[]{:S(2)}, u32[]{:S(2)}) collective-permute-start(bf16[2,2,96,768]{3,2,1,0:T(8,128)(2,1)} %fusion.3), channel_id=1, source_target_pairs={{0,8},{1,9},{2,10},{3,11},{4,20},{5,21},{6,22},{7,23},{8,0},{9,1},... | collective-permute-start | bytes 1769480 | tf_op jit(solution)/shard_map/ppermute | solution.py:511
  130.9 6.1 %collective-permute-start.11 = (bf16[512,768]{1,0:T(8,128)(2,1)}, bf16[512,768]{1,0:T(8,128)(2,1)S(1)}, u32[]{:S(2)}, u32[]{:S(2)}) collective-permute-start(bf16[512,768]{1,0:T(8,128)(2,1)} %get-tuple-element.252), channel_id=1, source_target_pairs={{0,4},{1,5},{2,6},{3,7},{4,0},{5,1},{6,2},{7,3},{8,12},{9,13},{10,... | collective-permute-start | bytes 2359304 | tf_op jit(solution)/shard_map/ppermute | solution.py:511
  132.4 2.3 copy-start.20
  132.4 2.3 copy-start.19
  132.4 2.3 copy-start.15
  132.7 4.3 %copy-start.9 = (f32[256,768]{1,0:T(8,128)S(1)}, f32[256,768]{1,0:T(8,128)}, u32[]{:S(2)}) copy-start(f32[256,768]{1,0:T(8,128)} %get-tuple-element.261) | copy-start | bytes 2359300
  132.7 23.0 %collective-permute-start.16 = (bf16[2,2,2,96,768]{4,3,2,1,0:T(8,128)(2,1)S(1)}, bf16[2,2,2,96,768]{4,3,2,1,0:T(8,128)(2,1)S(1)}, u32[]{:S(2)}, u32[]{:S(2)}) collective-permute-start(bf16[2,2,2,96,768]{4,3,2,1,0:T(8,128)(2,1)S(1)} %fusion), channel_id=1, source_target_pairs={{0,8},{1,9},{2,10},{3,11},{4,20},{5,21},{6,22},{7,23},{8,0},{9,1},... | collective-permute-start | bytes 3538952 | tf_op jit(solution)/shard_map/ppermute | solution.py:511
  133.7 32.6 %collective-permute-start.4 = (bf16[256,768]{1,0:T(8,128)(2,1)S(1)}, bf16[256,768]{1,0:T(8,128)(2,1)S(1)}, u32[]{:S(2)}, u32[]{:S(2)}) collective-permute-start(bf16[256,768]{1,0:T(8,128)(2,1)S(1)} %copy-done.12), channel_id=1, source_target_pairs={{2,4},{3,5},{4,2},{5,3},{10,12},{11,13},{12,10},{13,11},{18,20},{1... | collective-permute-start | bytes 1179656 | tf_op jit(solution)/shard_map/ppermute | solution.py:713
  134.7 13.8 %collective-permute-start.10 = (bf16[2,96,768]{2,1,0:T(8,128)(2,1)S(1)}, bf16[2,96,768]{2,1,0:T(8,128)(2,1)S(1)}, u32[]{:S(2)}, u32[]{:S(2)}) collective-permute-start(bf16[2,96,768]{2,1,0:T(8,128)(2,1)S(1)} %copy-done.15), channel_id=1, source_target_pairs={{0,1},{1,0},{2,3},{3,2},{4,5},{5,4},{6,7},{7,6},{8,9},{9,8},{10,11... | collective-permute-start | bytes 884744 | tf_op jit(solution)/shard_map/ppermute | solution.py:511
  136.3 17.5 %collective-permute-start.17 = (bf16[2,96,768]{2,1,0:T(8,128)(2,1)S(1)}, bf16[2,96,768]{2,1,0:T(8,128)(2,1)S(1)}, u32[]{:S(2)}, u32[]{:S(2)}) collective-permute-start(bf16[2,96,768]{2,1,0:T(8,128)(2,1)S(1)} %fusion.6), channel_id=1, source_target_pairs={{0,16},{1,17},{2,18},{3,19},{4,12},{5,13},{6,14},{7,15},{8,24},{9,... | collective-permute-start | bytes 884744 | tf_op jit(solution)/shard_map/ppermute | solution.py:511
  137.0 12.7 %copy-start.5 = (bf16[512,768]{1,0:T(8,128)(2,1)}, bf16[512,768]{1,0:T(8,128)(2,1)S(1)}, u32[]{:S(2)}) copy-start(bf16[512,768]{1,0:T(8,128)(2,1)S(1)} %collective-permute-done.11.core_ref) | copy-start | bytes 2359300
  137.1 30.1 %collective-permute-start.18 = (bf16[256,768]{1,0:T(8,128)(2,1)S(1)}, bf16[256,768]{1,0:T(8,128)(2,1)}, u32[]{:S(2)}, u32[]{:S(2)}) collective-permute-start(bf16[256,768]{1,0:T(8,128)(2,1)S(1)} %add_convert_fusion.2), channel_id=1, source_target_pairs={{0,1},{1,0},{2,3},{3,2},{4,5},{5,4},{6,7},{7,6},{8,9},{9,8},{10,11... | collective-permute-start | bytes 1179656 | tf_op jit(solution)/shard_map/ppermute | solution.py:511
  149.7 14.8 %collective-permute-start.15 = (bf16[96,768]{1,0:T(8,128)(2,1)S(1)}, bf16[96,768]{1,0:T(8,128)(2,1)S(1)}, u32[]{:S(2)}, u32[]{:S(2)}) collective-permute-start(bf16[96,768]{1,0:T(8,128)(2,1)S(1)} %fusion.16), channel_id=1, source_target_pairs={{0,2},{1,3},{2,0},{3,1},{4,6},{5,7},{6,4},{7,5},{8,10},{9,11},{10,... | collective-permute-start | bytes 442376 | tf_op jit(solution)/shard_map/ppermute | solution.py:511
  153.8 1.9 copy-start.13
  155.7 14.9 %collective-permute-start.21 = (bf16[96,768]{1,0:T(8,128)(2,1)}, bf16[96,768]{1,0:T(8,128)(2,1)}, u32[]{:S(2)}, u32[]{:S(2)}) collective-permute-start(bf16[96,768]{1,0:T(8,128)(2,1)} %fusion.15), channel_id=1, source_target_pairs={{0,2},{1,3},{2,0},{3,1},{4,6},{5,7},{6,4},{7,5},{8,10},{9,11},{10,... | collective-permute-start | bytes 442376 | tf_op jit(solution)/shard_map/ppermute | solution.py:511
  158.9 12.9 %collective-permute-start.22 = (bf16[2,2,96,768]{3,2,1,0:T(8,128)(2,1)}, bf16[2,2,96,768]{3,2,1,0:T(8,128)(2,1)}, u32[]{:S(2)}, u32[]{:S(2)}) collective-permute-start(bf16[2,2,96,768]{3,2,1,0:T(8,128)(2,1)} %fusion.2), channel_id=1, source_target_pairs={{0,16},{1,17},{2,18},{3,19},{4,12},{5,13},{6,14},{7,15},{8,24},{9,... | collective-permute-start | bytes 1769480 | tf_op jit(solution)/shard_map/ppermute | solution.py:511
  167.2 3.4 %copy-start.14 = (bf16[2,96,768]{2,1,0:T(8,128)(2,1)S(1)}, bf16[2,96,768]{2,1,0:T(8,128)(2,1)}, u32[]{:S(2)}) copy-start(bf16[2,96,768]{2,1,0:T(8,128)(2,1)} %copy-done.13) | copy-start | bytes 884740
  170.6 3.6 %copy-start.17 = (f32[4,768]{1,0:T(4,128)S(1)}, f32[4,768]{1,0:T(4,128)}, u32[]{:S(2)}) copy-start(f32[4,768]{1,0:T(4,128)} %get-tuple-element.293) | copy-start | bytes 36868
  170.6 3.5 %copy-start.18 = (f32[3,768]{1,0:T(4,128)S(1)}, f32[3,768]{1,0:T(4,128)}, u32[]{:S(2)}) copy-start(f32[3,768]{1,0:T(4,128)} %get-tuple-element.296) | copy-start | bytes 27652
  170.6 4.5 %copy-start.10 = (bf16[96,768]{1,0:T(8,128)(2,1)S(1)}, bf16[96,768]{1,0:T(8,128)(2,1)}, u32[]{:S(2)}) copy-start(bf16[96,768]{1,0:T(8,128)(2,1)} %fusion.14) | copy-start | bytes 442372
  173.1 16.3 %collective-permute-start.24 = (bf16[2,96,768]{2,1,0:T(8,128)(2,1)S(1)}, bf16[2,96,768]{2,1,0:T(8,128)(2,1)S(1)}, u32[]{:S(2)}, u32[]{:S(2)}) collective-permute-start(bf16[2,96,768]{2,1,0:T(8,128)(2,1)S(1)} %fusion.5), channel_id=1, source_target_pairs={{0,1},{1,0},{2,3},{3,2},{4,5},{5,4},{6,7},{7,6},{8,9},{9,8},{10,11... | collective-permute-start | bytes 884744 | tf_op jit(solution)/shard_map/ppermute | solution.py:511
  174.2 5.4 %collective-permute-start.20 = (f32[14,768]{1,0:T(8,128)S(1)}, f32[14,768]{1,0:T(8,128)S(1)}, u32[]{:S(2)}, u32[]{:S(2)}) collective-permute-start(f32[14,768]{1,0:T(8,128)S(1)} %pad_maximum_fusion.4), channel_id=1, source_target_pairs={{0,4},{4,0},{8,12},{12,8},{16,20},{20,16},{24,28},{28,24},{1,5},{5... | collective-permute-start | bytes 129032 | tf_op jit(solution)/shard_map/ppermute | solution.py:623
  175.1 26.8 %collective-permute-start.28 = (bf16[2,1,96,768]{3,2,1,0:T(8,128)(2,1)S(1)}, bf16[2,1,96,768]{3,2,1,0:T(8,128)(2,1)S(1)}, u32[]{:S(2)}, u32[]{:S(2)}) collective-permute-start(bf16[2,1,96,768]{3,2,1,0:T(8,128)(2,1)S(1)} %pad_maximum_fusion.3), channel_id=1, source_target_pairs={{0,1},{1,0},{2,3},{3,2},{4,5},{5,4},{6,7},{7,6},{8,9},{9,8},{10,11... | collective-permute-start | bytes 884744 | tf_op jit(solution)/shard_map/ppermute | solution.py:515
  176.9 25.0 %collective-permute-start.29 = (bf16[2,1,96,768]{3,2,1,0:T(8,128)(2,1)S(1)}, bf16[2,1,96,768]{3,2,1,0:T(8,128)(2,1)S(1)}, u32[]{:S(2)}, u32[]{:S(2)}) collective-permute-start(bf16[2,1,96,768]{3,2,1,0:T(8,128)(2,1)S(1)} %pad_maximum_fusion.3), channel_id=1, source_target_pairs={{0,2},{1,3},{2,0},{3,1},{4,6},{5,7},{6,4},{7,5},{8,10},{9,11},{10,... | collective-permute-start | bytes 884744 | tf_op jit(solution)/shard_map/ppermute | solution.py:515
  178.1 23.9 %collective-permute-start.30 = (bf16[2,1,96,768]{3,2,1,0:T(8,128)(2,1)S(1)}, bf16[2,1,96,768]{3,2,1,0:T(8,128)(2,1)S(1)}, u32[]{:S(2)}, u32[]{:S(2)}) collective-permute-start(bf16[2,1,96,768]{3,2,1,0:T(8,128)(2,1)S(1)} %pad_maximum_fusion.3), channel_id=1, source_target_pairs={{0,3},{1,2},{2,1},{3,0},{4,7},{5,6},{6,5},{7,4},{8,11},{9,10},{10,... | collective-permute-start | bytes 884744 | tf_op jit(solution)/shard_map/ppermute | solution.py:515
  179.6 11.0 %collective-permute-start.23 = (f32[14,768]{1,0:T(8,128)S(1)}, f32[14,768]{1,0:T(8,128)S(1)}, u32[]{:S(2)}, u32[]{:S(2)}) collective-permute-start(f32[14,768]{1,0:T(8,128)S(1)} %add.298), channel_id=1, source_target_pairs={{0,8},{4,12},{8,0},{12,4},{16,24},{20,28},{24,16},{28,20},{1,9},{5... | collective-permute-start | bytes 129032 | tf_op jit(solution)/shard_map/ppermute | solution.py:623
  190.6 4.2 %collective-permute-start.25 = (f32[14,768]{1,0:T(8,128)S(1)}, f32[14,768]{1,0:T(8,128)S(1)}, u32[]{:S(2)}, u32[]{:S(2)}) collective-permute-start(f32[14,768]{1,0:T(8,128)S(1)} %add.303), channel_id=1, source_target_pairs={{0,16},{4,20},{8,24},{12,28},{16,0},{20,4},{24,8},{28,12},{1,17},{... | collective-permute-start | bytes 129032 | tf_op jit(solution)/shard_map/ppermute | solution.py:623
  202.1 18.0 %collective-permute-start.35 = (bf16[2,4,96,768]{3,2,1,0:T(8,128)(2,1)S(1)}, bf16[2,4,96,768]{3,2,1,0:T(8,128)(2,1)S(1)}, u32[]{:S(2)}, u32[]{:S(2)}) collective-permute-start(bf16[2,4,96,768]{3,2,1,0:T(8,128)(2,1)S(1)} %constant_dynamic-update-slice_fusion), channel_id=1, source_target_pairs={{0,16},{1,17},{2,18},{3,19},{4,12},{5,13},{6,14},{7,15},{8,24},{9,... | collective-permute-start | bytes 3538952 | tf_op jit(solution)/shard_map/ppermute | solution.py:511
  202.8 10.6 %collective-permute-start.27 = (bf16[96,768]{1,0:T(8,128)(2,1)S(1)}, bf16[96,768]{1,0:T(8,128)(2,1)S(1)}, u32[]{:S(2)}, u32[]{:S(2)}) collective-permute-start(bf16[96,768]{1,0:T(8,128)(2,1)S(1)} %fusion.10), channel_id=1, source_target_pairs={{0,2},{1,3},{2,0},{3,1},{4,6},{5,7},{6,4},{7,5},{8,10},{9,11},{10,... | collective-permute-start | bytes 442376 | tf_op jit(solution)/shard_map/ppermute | solution.py:511
  208.1 6.4 %collective-permute-start.26 = (f32[14,768]{1,0:T(8,128)S(1)}, f32[14,768]{1,0:T(8,128)S(1)}, u32[]{:S(2)}, u32[]{:S(2)}) collective-permute-start(f32[14,768]{1,0:T(8,128)S(1)} %add.304), channel_id=1, source_target_pairs={{0,1},{1,0},{2,3},{3,2},{4,5},{5,4},{6,7},{7,6},{8,9},{9,8},{10,11... | collective-permute-start | bytes 129032 | tf_op jit(solution)/shard_map/ppermute | solution.py:623
  214.6 5.5 %collective-permute-start.31 = (f32[14,768]{1,0:T(8,128)S(1)}, f32[14,768]{1,0:T(8,128)S(1)}, u32[]{:S(2)}, u32[]{:S(2)}) collective-permute-start(f32[14,768]{1,0:T(8,128)S(1)} %add.310), channel_id=1, source_target_pairs={{0,2},{1,3},{2,0},{3,1},{4,6},{5,7},{6,4},{7,5},{8,10},{9,11},{10,... | collective-permute-start | bytes 129032 | tf_op jit(solution)/shard_map/ppermute | solution.py:623
  220.1 21.7 %copy-start.16 = (f32[14,768]{1,0:T(8,128)}, f32[14,768]{1,0:T(8,128)S(1)}, u32[]{:S(2)}) copy-start(f32[14,768]{1,0:T(8,128)S(1)} %add.311) | copy-start | bytes 129028
  220.2 30.4 %copy-start.1 = (bf16[2,8,96,768]{3,2,1,0:T(8,128)(2,1)}, bf16[2,8,96,768]{3,2,1,0:T(8,128)(2,1)S(1)}, u32[]{:S(2)}) copy-start(bf16[2,8,96,768]{3,2,1,0:T(8,128)(2,1)S(1)} %constant_dynamic-update-slice_fusion.4) | copy-start | bytes 7077892
  220.3 35.3 %collective-permute-start.39 = (bf16[2,8,96,768]{3,2,1,0:T(8,128)(2,1)S(1)}, bf16[2,8,96,768]{3,2,1,0:T(8,128)(2,1)}, u32[]{:S(2)}, u32[]{:S(2)}) collective-permute-start(bf16[2,8,96,768]{3,2,1,0:T(8,128)(2,1)S(1)} %constant_dynamic-update-slice_fusion.4), channel_id=1, source_target_pairs={{0,8},{1,9},{2,10},{3,11},{4,20},{5,21},{6,22},{7,23},{8,0},{9,1},... | collective-permute-start | bytes 7077896 | tf_op jit(solution)/shard_map/ppermute | solution.py:511
  221.4 6.4 %collective-permute-start.32 = (bf16[1,1,96,768]{3,2,1,0:T(8,128)(2,1)S(1)}, bf16[1,1,96,768]{3,2,1,0:T(8,128)(2,1)S(1)}, u32[]{:S(2)}, u32[]{:S(2)}) collective-permute-start(bf16[1,1,96,768]{3,2,1,0:T(8,128)(2,1)S(1)} %bitcast.300), channel_id=1, source_target_pairs={{0,1},{1,0},{2,3},{3,2},{4,5},{5,4},{6,7},{7,6},{8,9},{9,8},{10,11... | collective-permute-start | bytes 442376 | tf_op jit(solution)/shard_map/ppermute | solution.py:515
  223.5 17.1 %collective-permute-start.33 = (bf16[1,1,96,768]{3,2,1,0:T(8,128)(2,1)S(1)}, bf16[1,1,96,768]{3,2,1,0:T(8,128)(2,1)S(1)}, u32[]{:S(2)}, u32[]{:S(2)}) collective-permute-start(bf16[1,1,96,768]{3,2,1,0:T(8,128)(2,1)S(1)} %bitcast.301), channel_id=1, source_target_pairs={{0,2},{1,3},{2,0},{3,1},{4,6},{5,7},{6,4},{7,5},{8,10},{9,11},{10,... | collective-permute-start | bytes 442376 | tf_op jit(solution)/shard_map/ppermute | solution.py:515
  224.3 16.3 %collective-permute-start.34 = (bf16[1,1,96,768]{3,2,1,0:T(8,128)(2,1)S(1)}, bf16[1,1,96,768]{3,2,1,0:T(8,128)(2,1)S(1)}, u32[]{:S(2)}, u32[]{:S(2)}) collective-permute-start(bf16[1,1,96,768]{3,2,1,0:T(8,128)(2,1)S(1)} %bitcast.302), channel_id=1, source_target_pairs={{0,3},{1,2},{2,1},{3,0},{4,7},{5,6},{6,5},{7,4},{8,11},{9,10},{10,... | collective-permute-start | bytes 442376 | tf_op jit(solution)/shard_map/ppermute | solution.py:515
  225.9 23.0 %collective-permute-start.19 = (bf16[256,768]{1,0:T(8,128)(2,1)}, bf16[256,768]{1,0:T(8,128)(2,1)}, u32[]{:S(2)}, u32[]{:S(2)}) collective-permute-start(bf16[256,768]{1,0:T(8,128)(2,1)} %get-tuple-element.341), channel_id=1, source_target_pairs={{2,4},{3,5},{4,2},{5,3},{10,12},{11,13},{12,10},{13,11},{18,20},{1... | collective-permute-start | bytes 1179656 | tf_op jit(solution)/shard_map/ppermute | solution.py:713
  240.7 10.9 %collective-permute-start.36 = (bf16[1,4,96,768]{3,2,1,0:T(8,128)(2,1)S(1)}, bf16[1,4,96,768]{3,2,1,0:T(8,128)(2,1)S(1)}, u32[]{:S(2)}, u32[]{:S(2)}) collective-permute-start(bf16[1,4,96,768]{3,2,1,0:T(8,128)(2,1)S(1)} %constant_dynamic-update-slice_fusion.6), channel_id=1, source_target_pairs={{0,16},{1,17},{2,18},{3,19},{4,12},{5,13},{6,14},{7,15},{8,24},{9,... | collective-permute-start | bytes 1769480 | tf_op jit(solution)/shard_map/ppermute | solution.py:511
  241.8 15.1 %collective-permute-start.40 = (bf16[2,8,96,768]{3,2,1,0:T(8,128)(2,1)S(1)}, bf16[2,8,96,768]{3,2,1,0:T(8,128)(2,1)}, u32[]{:S(2)}, u32[]{:S(2)}) collective-permute-start(bf16[2,8,96,768]{3,2,1,0:T(8,128)(2,1)S(1)} %constant_dynamic-update-slice_fusion.4), channel_id=1, source_target_pairs={{0,4},{1,5},{2,6},{3,7},{4,0},{5,1},{6,2},{7,3},{8,12},{9,13},{10,... | collective-permute-start | bytes 7077896 | tf_op jit(solution)/shard_map/ppermute | solution.py:511
  251.7 17.2 %copy-start.3 = (bf16[1,8,96,768]{3,2,1,0:T(8,128)(2,1)}, bf16[1,8,96,768]{3,2,1,0:T(8,128)(2,1)S(1)}, u32[]{:S(2)}) copy-start(bf16[1,8,96,768]{3,2,1,0:T(8,128)(2,1)S(1)} %constant_dynamic-update-slice_fusion.10) | copy-start | bytes 3538948
  255.6 4.7 %collective-permute-start.41 = (bf16[2,8,96,768]{3,2,1,0:T(8,128)(2,1)}, bf16[2,8,96,768]{3,2,1,0:T(8,128)(2,1)S(1)}, u32[]{:S(2)}, u32[]{:S(2)}) collective-permute-start(bf16[2,8,96,768]{3,2,1,0:T(8,128)(2,1)} %collective-permute-done.39), channel_id=1, source_target_pairs={{0,4},{1,5},{2,6},{3,7},{4,0},{5,1},{6,2},{7,3},{8,12},{9,13},{10,... | collective-permute-start | bytes 7077896 | tf_op jit(solution)/shard_map/ppermute | solution.py:511
  255.6 20.4 %collective-permute-start.37 = (bf16[1,8,96,768]{3,2,1,0:T(8,128)(2,1)S(1)}, bf16[1,8,96,768]{3,2,1,0:T(8,128)(2,1)S(1)}, u32[]{:S(2)}, u32[]{:S(2)}) collective-permute-start(bf16[1,8,96,768]{3,2,1,0:T(8,128)(2,1)S(1)} %constant_dynamic-update-slice_fusion.10), channel_id=1, source_target_pairs={{0,8},{1,9},{2,10},{3,11},{4,20},{5,21},{6,22},{7,23},{8,0},{9,1},... | collective-permute-start | bytes 3538952 | tf_op jit(solution)/shard_map/ppermute | solution.py:511
  256.7 19.6 %collective-permute-start.38 = (bf16[1,8,96,768]{3,2,1,0:T(8,128)(2,1)S(1)}, bf16[1,8,96,768]{3,2,1,0:T(8,128)(2,1)S(1)}, u32[]{:S(2)}, u32[]{:S(2)}) collective-permute-start(bf16[1,8,96,768]{3,2,1,0:T(8,128)(2,1)S(1)} %constant_dynamic-update-slice_fusion.10), channel_id=1, source_target_pairs={{0,4},{1,5},{2,6},{3,7},{4,0},{5,1},{6,2},{7,3},{8,12},{9,13},{10,... | collective-permute-start | bytes 3538952 | tf_op jit(solution)/shard_map/ppermute | solution.py:511
  260.3 1.4 copy-start.2
  276.0 2.9 %copy-start.6 = (bf16[1,8,96,768]{3,2,1,0:T(8,128)(2,1)}, bf16[1,8,96,768]{3,2,1,0:T(8,128)(2,1)S(1)}, u32[]{:S(2)}) copy-start(bf16[1,8,96,768]{3,2,1,0:T(8,128)(2,1)S(1)} %collective-permute-done.37) | copy-start | bytes 3538948
  276.0 2.9 %collective-permute-start.42 = (bf16[1,8,96,768]{3,2,1,0:T(8,128)(2,1)S(1)}, bf16[1,8,96,768]{3,2,1,0:T(8,128)(2,1)S(1)}, u32[]{:S(2)}, u32[]{:S(2)}) collective-permute-start(bf16[1,8,96,768]{3,2,1,0:T(8,128)(2,1)S(1)} %collective-permute-done.37), channel_id=1, source_target_pairs={{0,4},{1,5},{2,6},{3,7},{4,0},{5,1},{6,2},{7,3},{8,12},{9,13},{10,... | collective-permute-start | bytes 3538952 | tf_op jit(solution)/shard_map/ppermute | solution.py:511
  276.2 2.7 copy-start.7
  (3 other events, 3.7 us)
